TPU v7x, 32 devices: a whole 2x2x4 slice. The times are simulated.
32 devices in a mesh: seq: 2 (over x), ffn: 16 (over z, y, core).
Axes of the slice: x: 2, y: 2, z: 4, core: 2. Of those that a mesh axis runs over, the one named last changes fastest.
Arguments:
- hidden_in: bfloat16 [20480, 768], P(('seq', 'ffn')), may hold values from -6 to 6
- doc_lengths: int32 [2, 32], P('seq'), may hold values from 79 to 561, as said below
- box_x: int32 [20480], P('seq'), may hold values from 0 to 1000
- box_y: int32 [20480], P('seq'), may hold values from 0 to 1000
- token_valid: int32 [20480], P('seq'), may hold values from 0 to 1, as said below
- w_query: bfloat16 [768, 768], replicated, may hold values from -0.21875 to 0.21875
- b_query: bfloat16 [768], replicated, may hold values from -1.75 to 1.75
- w_key: bfloat16 [768, 768], replicated, may hold values from -0.21875 to 0.21875
- w_value: bfloat16 [768, 768], replicated, may hold values from -0.21875 to 0.21875
- b_value: bfloat16 [768], replicated, may hold values from -1.75 to 1.75
- w_out: bfloat16 [768, 768], replicated, may hold values from -3 to 3
- b_out: bfloat16 [768], replicated, may hold values from -1.75 to 1.75
- gain_attn: bfloat16 [768], replicated, may hold values from 0.5 to 1.5
- shift_attn: bfloat16 [768], replicated, may hold values from -1.75 to 1.75
- w_up: bfloat16 [768, 3072], P(None, 'ffn'), may hold values from -0.21875 to 0.21875
- b_up: bfloat16 [3072], P('ffn'), may hold values from -1.75 to 1.75
- w_down: bfloat16 [3072, 768], P('ffn'), may hold values from -0.109375 to 0.109375
- b_down: bfloat16 [768], replicated, may hold values from -1.75 to 1.75
- gain_out: bfloat16 [768], replicated, may hold values from 0.5 to 1.5
- shift_out: bfloat16 [768], replicated, may hold values from -1.75 to 1.75
- table_seq: bfloat16 [32, 12], replicated, may hold values from -6 to 6
- table_x: bfloat16 [64, 12], replicated, may hold values from -6 to 6
- table_y: bfloat16 [64, 12], replicated, may hold values from -6 to 6
- out_grad: bfloat16 [20480, 768], P(('seq', 'ffn')), may hold values from -6 to 6
Outputs:
- hidden_out: float32 [20480, 768], P(('seq', 'ffn'))
- hidden_grad: float32 [20480, 768], P(('seq', 'ffn'))
- grad_w_query: float32 [768, 768], replicated
- grad_b_query: float32 [768], replicated
- grad_w_key: float32 [768, 768], replicated
- grad_w_value: float32 [768, 768], replicated
- grad_b_value: float32 [768], replicated
- grad_w_out: float32 [768, 768], replicated
- grad_b_out: float32 [768], replicated
- grad_gain_attn: float32 [768], replicated
- grad_shift_attn: float32 [768], replicated
- grad_w_up: float32 [768, 3072], P(None, 'ffn')
- grad_b_up: float32 [3072], P('ffn')
- grad_w_down: float32 [3072, 768], P('ffn')
- grad_b_down: float32 [768], replicated
- grad_gain_out: float32 [768], replicated
- grad_shift_out: float32 [768], replicated
- grad_table_seq: float32 [32, 12], replicated
- grad_table_x: float32 [64, 12], replicated
- grad_table_y: float32 [64, 12], replicated
Inputs may be any that keep to these rules, and one draw needn't show every extreme that they name: `doc_lengths`: each row holds the lengths of the 32 documents of one pack, in order; they sum to 10240. Every pack has a document of the most and one of the least length. `token_valid`: padding rows are the last rows of their document, at most half of those after its first 49 rows, which are never padding.
All inputs are finite; a program needn't handle non-finite values.
Results may differ from a plain program's by a relative error of at most 0.014.
Values may be sent and summed in bfloat16 or wider, within the bound.
A program may use at most 448 MiB of HBM per device.

v0:
```python
import jax
import jax.numpy as jnp
from jax import lax
from jax.sharding import PartitionSpec as P

VISUAL = 49
KEY_BLOCK = 640


sequence_edges = (12, 16, 23, 32, 46, 64, 91)
edges_box = (20, 23, 27, 32, 39, 46, 54, 64, 77, 91, 108, 128, 153, 182, 216)
norm_eps = 1e-12
bucket_settings = ((8, sequence_edges, 16), (16, edges_box, 32), (16, edges_box, 32))


def padded_2(block, sides, width):
    for axis, dim in sides:
        count = lax.axis_size(axis)
        forward = [(i, i + 1) for i in range(count - 1)]
        backward = [(target, source) for source, target in forward]
        low = lax.ppermute(
            lax.slice_in_dim(block, block.shape[dim] - width, None, axis=dim), axis, forward
        )
        high = lax.ppermute(lax.slice_in_dim(block, 0, width, axis=dim), axis, backward)
        block = jnp.concatenate([low, block, high], axis=dim)
    return block


def from_behind(x, axis, by):
    devices = lax.axis_size(axis)
    pairs = [(i, i + by) for i in range(devices) if 0 <= i + by < devices]
    return lax.ppermute(x, axis, pairs)


def bucket_of(distance, near_span, edge_list, sign_offset):
    magnitude = jnp.abs(distance)
    bucket = jnp.minimum(magnitude, near_span)
    for edge_value in edge_list:
        bucket = bucket + (magnitude >= edge_value).astype(jnp.int32)
    return bucket + jnp.where(distance > 0, sign_offset, 0)


def layer_norm(value, gain, shift):
    center = value - jnp.mean(value, axis=-1, keepdims=True)
    spread = jnp.mean(center * center, axis=-1, keepdims=True)
    return center * lax.rsqrt(spread + norm_eps) * gain + shift


def layout(row_ids, doc_ends):
    forwarded_value = row_ids[:, None] >= doc_ends[None, :]
    doc_ids = jnp.sum(forwarded_value.astype(jnp.int32), axis=1)
    starts = jnp.max(jnp.where(forwarded_value, doc_ends[None, :], 0), axis=1)
    offsets = row_ids - starts
    places = jnp.where(offsets < VISUAL, offsets, offsets - VISUAL)
    return (doc_ids, places)


def gelu_exact(value):
    return jax.nn.gelu(value, approximate=False)


def indicator_of(query_ids, key_ids, bias_lookup, setting):
    bucket = bucket_of(key_ids[None, :] - query_ids[:, None], setting[0], setting[1], setting[2])
    levels = jnp.arange(bias_lookup.shape[0], dtype=jnp.int32)
    return (levels[:, None, None] == bucket[None]).astype(jnp.bfloat16)


def on_device(
    hidden_in,
    doc_lengths,
    box_x,
    box_y,
    token_valid,
    w_query,
    b_query,
    w_key,
    w_value,
    b_value,
    w_out,
    b_out,
    gain_attn,
    shift_attn,
    w_up,
    b_up,
    w_down,
    b_down,
    gain_out,
    shift_out,
    table_seq,
    table_x,
    table_y,
    out_grad,
):
    rows = hidden_in.shape[0]
    width = hidden_in.shape[1]
    heads = table_seq.shape[1]
    head_size = width // heads
    group_rows = box_x.shape[0]
    span = 3 * rows
    block_list = span // KEY_BLOCK
    block_ids = jnp.arange(block_list, dtype=jnp.int32)
    first_row = lax.axis_index("ffn") * rows
    doc_ends = jnp.cumsum(doc_lengths[0])
    window_rows = first_row - rows + jnp.arange(span, dtype=jnp.int32)
    doc_ids, places = layout(window_rows, doc_ends)
    inside = (window_rows >= 0) & (window_rows < group_rows)

    def window_of(item):
        edge = jnp.zeros((rows,), item.dtype)
        padded = jnp.concatenate([edge, item, edge])
        return lax.dynamic_slice_in_dim(padded, first_row, span)

    key_meta_all = (places, window_of(box_x), window_of(box_y))
    key_open = (window_of(token_valid) == 1) & inside
    own_meta = tuple((item[rows : 2 * rows] for item in key_meta_all))
    own_docs = doc_ids[rows : 2 * rows]
    tables = (table_seq, table_x, table_y)
    query = (
        (jnp.dot(hidden_in, w_query, preferred_element_type=jnp.float32) + b_query) * 0.125
    ).astype(jnp.bfloat16)
    key = jnp.dot(hidden_in, w_key, preferred_element_type=jnp.float32).astype(jnp.bfloat16)
    value = (jnp.dot(hidden_in, w_value, preferred_element_type=jnp.float32) + b_value).astype(
        jnp.bfloat16
    )
    query_heads = query.reshape(rows, heads, head_size)
    packed = jnp.concatenate([key, value], axis=1)
    window_kv = padded_2(packed, (("ffn", 0),), rows)
    key_all = window_kv[:, :width]
    value_all = window_kv[:, width:]

    def block_slice(source, index):
        return lax.dynamic_slice_in_dim(source, index * KEY_BLOCK, KEY_BLOCK)

    def scores_at(index):
        key_block = block_slice(key_all, index).reshape(KEY_BLOCK, heads, head_size)
        allowed = (own_docs[:, None] == block_slice(doc_ids, index)[None, :]) & block_slice(
            key_open, index
        )[None, :]
        raw = jnp.einsum("qhd,khd->hqk", query_heads, key_block, preferred_element_type=jnp.float32)
        for query_ids, key_ids, bias_lookup, setting in zip(
            own_meta, key_meta_all, tables, bucket_settings
        ):
            member_flags = indicator_of(
                query_ids, block_slice(key_ids, index), bias_lookup, setting
            )
            raw = raw + jnp.einsum(
                "uld,ui->ild", member_flags, bias_lookup, preferred_element_type=jnp.float32
            )
        return jnp.where(allowed[None], raw, -jnp.inf)

    def forward_scores(carry, index):
        return (carry, scores_at(index))

    unused, stored = lax.scan(forward_scores, jnp.int32(0), block_ids)
    top = jnp.max(stored, axis=(0, 3))
    total = jnp.sum(jnp.exp(stored - top[None, :, :, None]), axis=(0, 3))

    def probs_at(index):
        return jnp.exp(stored[index] - top[:, :, None]) / total[:, :, None]

    def context_step(context, index):
        value_block = block_slice(value_all, index).reshape(KEY_BLOCK, heads, head_size)
        weights = probs_at(index).astype(jnp.bfloat16)
        return (
            context
            + jnp.einsum("hqk,khd->qhd", weights, value_block, preferred_element_type=jnp.float32),
            None,
        )

    context, unused = lax.scan(
        context_step, jnp.zeros((rows, heads, head_size), jnp.float32), block_ids
    )
    context_low = context.reshape(rows, width).astype(jnp.bfloat16)
    attn = jnp.dot(context_low, w_out, preferred_element_type=jnp.float32) + b_out
    inputs = hidden_in.astype(jnp.float32)
    normed, norm_pull = jax.vjp(
        layer_norm, inputs + attn, gain_attn.astype(jnp.float32), shift_attn.astype(jnp.float32)
    )
    normed_low = normed.astype(jnp.bfloat16)
    normed_all = lax.all_gather(normed_low, "ffn", axis=0, tiled=True)
    pre_act = jnp.dot(normed_all, w_up, preferred_element_type=jnp.float32) + b_up
    activated, gelu_pull = jax.vjp(gelu_exact, pre_act)
    active = activated.astype(jnp.bfloat16)
    branch = lax.psum_scatter(
        jnp.dot(active, w_down, preferred_element_type=jnp.float32),
        "ffn",
        scatter_dimension=0,
        tiled=True,
    )
    hidden_out, out_pull = jax.vjp(
        layer_norm,
        normed + (branch + b_down),
        gain_out.astype(jnp.float32),
        shift_out.astype(jnp.float32),
    )
    mid_grad, grad_gain_out, grad_shift_out = out_pull(out_grad.astype(jnp.float32))
    branch_grad = mid_grad.astype(jnp.bfloat16)
    grad_b_down = jnp.sum(branch_grad.astype(jnp.float32), axis=0)
    grad_all = lax.all_gather(branch_grad, "ffn", axis=0, tiled=True)
    act_grad = jnp.dot(grad_all, w_down.T, preferred_element_type=jnp.float32)
    pre_grad = gelu_pull(act_grad)[0].astype(jnp.bfloat16)
    up_grad = jnp.dot(normed_all.T, pre_grad, preferred_element_type=jnp.float32)
    up_bias_grad = jnp.sum(pre_grad.astype(jnp.float32), axis=0)
    down_grad = jnp.dot(active.T, grad_all, preferred_element_type=jnp.float32)
    normed_grad = mid_grad + lax.psum_scatter(
        jnp.dot(pre_grad, w_up.T, preferred_element_type=jnp.float32),
        "ffn",
        scatter_dimension=0,
        tiled=True,
    )
    grad_w_up, grad_b_up, grad_w_down = (
        lax.psum(up_grad.astype(jnp.bfloat16), "seq").astype(jnp.float32),
        lax.psum(up_bias_grad.astype(jnp.bfloat16), "seq").astype(jnp.float32),
        lax.psum(down_grad.astype(jnp.bfloat16), "seq").astype(jnp.float32),
    )
    mid1_grad, grad_gain_attn, grad_shift_attn = norm_pull(normed_grad)
    attn_grad = mid1_grad.astype(jnp.bfloat16)
    grad_b_out = jnp.sum(attn_grad.astype(jnp.float32), axis=0)
    grad_w_out = jnp.dot(context_low.T, attn_grad, preferred_element_type=jnp.float32)
    context_grad = jnp.dot(attn_grad, w_out.T, preferred_element_type=jnp.float32).astype(
        jnp.bfloat16
    )
    context_grad = context_grad.reshape(rows, heads, head_size)

    def delta_step(delta, index):
        value_block = block_slice(value_all, index).reshape(KEY_BLOCK, heads, head_size)
        prob_grad = jnp.einsum(
            "qhd,khd->hqk", context_grad, value_block, preferred_element_type=jnp.float32
        )
        return (delta + jnp.sum(probs_at(index) * prob_grad, axis=2), None)

    delta, unused = lax.scan(delta_step, jnp.zeros((heads, rows), jnp.float32), block_ids)

    def grad_step(carry, index):
        query_grad, table_grads = carry
        key_block = block_slice(key_all, index).reshape(KEY_BLOCK, heads, head_size)
        value_block = block_slice(value_all, index).reshape(KEY_BLOCK, heads, head_size)
        probs = probs_at(index)
        prob_grad = jnp.einsum(
            "qhd,khd->hqk", context_grad, value_block, preferred_element_type=jnp.float32
        )
        scores_gradient = (probs * (prob_grad - delta[:, :, None])).astype(jnp.bfloat16)
        query_grad = query_grad + jnp.einsum(
            "hqk,khd->qhd", scores_gradient, key_block, preferred_element_type=jnp.float32
        )
        key_term = jnp.einsum(
            "hqk,qhd->khd", scores_gradient, query_heads, preferred_element_type=jnp.float32
        )
        value_term = jnp.einsum(
            "hqk,qhd->khd",
            probs.astype(jnp.bfloat16),
            context_grad,
            preferred_element_type=jnp.float32,
        )
        updated = []
        for grad, query_ids, key_ids, bias_lookup, setting in zip(
            table_grads, own_meta, key_meta_all, tables, bucket_settings
        ):
            member_flags = indicator_of(
                query_ids, block_slice(key_ids, index), bias_lookup, setting
            )
            updated.append(
                grad
                + jnp.einsum(
                    "usy,dsy->ud", member_flags, scores_gradient, preferred_element_type=jnp.float32
                )
            )
        joined = jnp.concatenate(
            [key_term.reshape(KEY_BLOCK, width), value_term.reshape(KEY_BLOCK, width)], axis=1
        )
        return ((query_grad, tuple(updated)), joined)

    start_carry = (
        jnp.zeros((rows, heads, head_size), jnp.float32),
        tuple((jnp.zeros(bias_lookup.shape, jnp.float32) for bias_lookup in tables)),
    )
    (query_sum, table_grads), kv_terms = lax.scan(grad_step, start_carry, block_ids)
    kv_terms = kv_terms.reshape(span, 2 * width)
    gradient_from_lower = from_behind(kv_terms[2 * rows :].astype(jnp.bfloat16), "ffn", 1).astype(
        jnp.float32
    )
    from_above = from_behind(kv_terms[:rows].astype(jnp.bfloat16), "ffn", -1).astype(jnp.float32)
    key_value_total = kv_terms[rows : 2 * rows] + gradient_from_lower + from_above
    key_grad = key_value_total[:, :width].astype(jnp.bfloat16)
    value_grad = key_value_total[:, width:].astype(jnp.bfloat16)
    query_grad = query_sum.reshape(rows, width).astype(jnp.bfloat16)
    hidden_grad = (
        mid1_grad
        + jnp.dot(query_grad, w_query.T, preferred_element_type=jnp.float32) * 0.125
        + jnp.dot(key_grad, w_key.T, preferred_element_type=jnp.float32)
        + jnp.dot(value_grad, w_value.T, preferred_element_type=jnp.float32)
    )
    local_sums = (
        jnp.dot(hidden_in.T, query_grad, preferred_element_type=jnp.float32) * 0.125,
        jnp.sum(query_grad.astype(jnp.float32), axis=0) * 0.125,
        jnp.dot(hidden_in.T, key_grad, preferred_element_type=jnp.float32),
        jnp.dot(hidden_in.T, value_grad, preferred_element_type=jnp.float32),
        jnp.sum(value_grad.astype(jnp.float32), axis=0),
        grad_w_out,
        grad_b_out,
        grad_gain_attn,
        grad_shift_attn,
        grad_b_down,
        grad_gain_out,
        grad_shift_out,
        table_grads[0],
        table_grads[1],
        table_grads[2],
    )
    summed = lax.psum(
        (
            local_sums[0],
            local_sums[1],
            local_sums[2],
            local_sums[3],
            local_sums[4],
            local_sums[5],
            local_sums[6],
            local_sums[7],
            local_sums[8],
            local_sums[9],
            local_sums[10],
            local_sums[11],
            local_sums[12],
            local_sums[13],
            local_sums[14],
        ),
        ("seq", "ffn"),
    )
    return (
        hidden_out,
        hidden_grad,
        summed[0],
        summed[1],
        summed[2],
        summed[3],
        summed[4],
        summed[5],
        summed[6],
        summed[7],
        summed[8],
        grad_w_up,
        grad_b_up,
        grad_w_down,
        summed[9],
        summed[10],
        summed[11],
        summed[12],
        summed[13],
        summed[14],
    )


def solution(mesh):
    in_specs = (
        P(("seq", "ffn"), None),
        P("seq", None),
        P("seq"),
        P("seq"),
        P("seq"),
        P(),
        P(),
        P(),
        P(),
        P(),
        P(),
        P(),
        P(),
        P(),
        P(None, "ffn"),
        P("ffn"),
        P("ffn", None),
        P(),
        P(),
        P(),
        P(),
        P(),
        P(),
        P(("seq", "ffn"), None),
    )
    out_specs = (
        P(("seq", "ffn"), None),
        P(("seq", "ffn"), None),
        P(),
        P(),
        P(),
        P(),
        P(),
        P(),
        P(),
        P(),
        P(),
        P(None, "ffn"),
        P("ffn"),
        P("ffn", None),
        P(),
        P(),
        P(),
        P(),
        P(),
        P(),
    )
    return jax.shard_map(
        on_device, mesh=mesh, in_specs=in_specs, out_specs=out_specs, check_vma=False
    )
```

profile of v0, /device:TPU:0, one launch (start us, length us, event | category | flops | bytes accessed | tf_op | source)
XLA Modules:
  0.0 2353.8 jit_solution(15291600758579194994)
XLA Ops:
  38.2 513.5 %while.51 = (s32[]{:T(128)}, f32[3,12,640,640]{2,3,1,0:T(8,128)}, s32[640]{0:T(1024)S(1)}, s32[3]{0:T(128)S(1)}, s32[1920]{0:T(1024)S(1)}, /*index=5*/pred[1920]...) while((s32[]{:T(128)}, f32[3,12,640,640]{2,3,1,0:T(8,128)}, ...), condition=%wide.region_4.5_spmd, body=%wide.region_3.4_spmd.sunk | while | flops 2340864000 | bytes 270219616 | solution.py:154
  45.7 18.5 fusion.333
  64.2 26.9 %copy.118 = f32[640,640,12]{0,1,2:T(8,128)} copy(f32[640,640,12]{1,2,0:T(8,128)} %fusion.333) | data formatting | bytes 39321600 | tf_op jit(solution)/shard_map/while/body/eval_jaxpr/uld,ui->ild/dot_general | solution.py:146
  91.1 18.5 fusion.334
  109.6 26.9 %copy.119 = f32[640,640,12]{0,1,2:T(8,128)} copy(f32[640,640,12]{1,2,0:T(8,128)} %fusion.334) | data formatting | bytes 39321600 | tf_op jit(solution)/shard_map/while/body/eval_jaxpr/uld,ui->ild/dot_general | solution.py:146
  138.8 12.9 fusion.336
  151.7 26.9 %copy.120 = f32[640,640,12]{0,1,2:T(8,128)} copy(f32[640,640,12]{1,2,0:T(8,128)} %fusion.336) | data formatting | bytes 39321600 | tf_op jit(solution)/shard_map/while/body/eval_jaxpr/uld,ui->ild/dot_general | solution.py:146
  179.9 26.8 %bitcast_dynamic-update-slice_fusion.2 = f32[3,12,640,640]{2,3,1,0:T(8,128)} fusion(f32[3,12,640,640]{2,3,1,0:T(8,128)} %get-tuple-element.1162, s32[]{:T(128)} %get-tuple-element.1161, f32[640,640,12]{0,1,2:T(8,128)} %copy.118, f32[640,640,12]{0,1,2:T(8,128)} %copy.119, f32[640,640,12]{0,1,2:T(8,128)} %copy.120, ...), kind=kOutput, calls=%fused_computation.9.clone.1 | convolution fusion | flops 648806400 | bytes 81019392 | tf_op jit(solution)/shard_map/while/body/eval_jaxpr/qhd,khd->hqk/dot_general | solution.py:139
  213.9 18.5 fusion.333
  232.4 26.9 %copy.118 = f32[640,640,12]{0,1,2:T(8,128)} copy(f32[640,640,12]{1,2,0:T(8,128)} %fusion.333) | data formatting | bytes 39321600 | tf_op jit(solution)/shard_map/while/body/eval_jaxpr/uld,ui->ild/dot_general | solution.py:146
  259.3 18.5 fusion.334
  277.8 26.9 %copy.119 = f32[640,640,12]{0,1,2:T(8,128)} copy(f32[640,640,12]{1,2,0:T(8,128)} %fusion.334) | data formatting | bytes 39321600 | tf_op jit(solution)/shard_map/while/body/eval_jaxpr/uld,ui->ild/dot_general | solution.py:146
  307.0 12.9 fusion.336
  320.0 26.9 %copy.120 = f32[640,640,12]{0,1,2:T(8,128)} copy(f32[640,640,12]{1,2,0:T(8,128)} %fusion.336) | data formatting | bytes 39321600 | tf_op jit(solution)/shard_map/while/body/eval_jaxpr/uld,ui->ild/dot_general | solution.py:146
  348.2 26.9 %bitcast_dynamic-update-slice_fusion.2 = f32[3,12,640,640]{2,3,1,0:T(8,128)} fusion(f32[3,12,640,640]{2,3,1,0:T(8,128)} %get-tuple-element.1162, s32[]{:T(128)} %get-tuple-element.1161, f32[640,640,12]{0,1,2:T(8,128)} %copy.118, f32[640,640,12]{0,1,2:T(8,128)} %copy.119, f32[640,640,12]{0,1,2:T(8,128)} %copy.120, ...), kind=kOutput, calls=%fused_computation.9.clone.1 | convolution fusion | flops 648806400 | bytes 81019392 | tf_op jit(solution)/shard_map/while/body/eval_jaxpr/qhd,khd->hqk/dot_general | solution.py:139
  382.2 18.5 fusion.333
  400.7 26.9 %copy.118 = f32[640,640,12]{0,1,2:T(8,128)} copy(f32[640,640,12]{1,2,0:T(8,128)} %fusion.333) | data formatting | bytes 39321600 | tf_op jit(solution)/shard_map/while/body/eval_jaxpr/uld,ui->ild/dot_general | solution.py:146
  427.6 18.5 fusion.334
  446.1 26.9 %copy.119 = f32[640,640,12]{0,1,2:T(8,128)} copy(f32[640,640,12]{1,2,0:T(8,128)} %fusion.334) | data formatting | bytes 39321600 | tf_op jit(solution)/shard_map/while/body/eval_jaxpr/uld,ui->ild/dot_general | solution.py:146
  475.3 12.9 fusion.336
  488.3 26.9 %copy.120 = f32[640,640,12]{0,1,2:T(8,128)} copy(f32[640,640,12]{1,2,0:T(8,128)} %fusion.336) | data formatting | bytes 39321600 | tf_op jit(solution)/shard_map/while/body/eval_jaxpr/uld,ui->ild/dot_general | solution.py:146
  516.5 26.8 %bitcast_dynamic-update-slice_fusion.2 = f32[3,12,640,640]{2,3,1,0:T(8,128)} fusion(f32[3,12,640,640]{2,3,1,0:T(8,128)} %get-tuple-element.1162, s32[]{:T(128)} %get-tuple-element.1161, f32[640,640,12]{0,1,2:T(8,128)} %copy.118, f32[640,640,12]{0,1,2:T(8,128)} %copy.119, f32[640,640,12]{0,1,2:T(8,128)} %copy.120, ...), kind=kOutput, calls=%fused_computation.9.clone.1 | convolution fusion | flops 648806400 | bytes 81019392 | tf_op jit(solution)/shard_map/while/body/eval_jaxpr/qhd,khd->hqk/dot_general | solution.py:139
  551.8 18.7 reduce_max.19
  570.5 18.9 exponential_reduce_fusion
  594.1 155.3 %while.52 = (s32[]{:T(128)}, f32[640,12,64]{0,2,1:T(8,128)}, s32[3]{0:T(128)S(1)}, bf16[1920,768]{0,1:T(8,128)(2,1)}, f32[3,12,640,640]{2,3,1,0:T(8,128)}, /*ind...) while((s32[]{:T(128)}, f32[640,12,64]{0,2,1:T(8,128)}, ...), condition=%wide.region_8.9_spmd.clone, body=%wide.region_7.8_spmd.clone.sunk | while | flops 644874240 | bytes 105246944 | solution.py:170
  598.6 15.1 constant_dynamic-slice_fusion.13
  613.7 21.6 copy.121
  635.3 10.4 bitcast_add_fusion.8
  650.1 15.1 constant_dynamic-slice_fusion.13
  665.2 21.6 copy.121
  686.8 10.7 bitcast_add_fusion.8
  702.0 15.1 constant_dynamic-slice_fusion.13
  717.1 21.6 copy.121
  738.7 10.7 bitcast_add_fusion.8
  754.5 155.9 %all-gather.3.cloned.1.call-done = bf16[10240,768]{1,0:T(8,128)(2,1)} async-done(((bf16[640,768]{1,0:T(8,128)(2,1)}), bf16[10240,768]{1,0:T(8,128)(2,1)}) %all-gather.3.cloned.1.call-update) | async-done | bytes 15728656 | tf_op jit(solution)/shard_map/all_gather | solution.py:180
  910.4 24.6 %multiply_convert_fusion = (bf16[10240,192]{0,1:T(8,128)(2,1)S(1)}, f32[10240,192]{0,1:T(8,128)}, f32[10240,192]{0,1:T(8,128)}) fusion(f32[192]{0:T(256)S(1)} %convert_element_type.668, bf16[10240,768]{1,0:T(8,128)(2,1)} %all-gather.3.cloned.1.call-done, bf16[768,192]{0,1:T(8,128)(2,1)} %param.46), kind=kOutput, calls=%fused_computation.239 | convolution fusion | flops 3149660160 | bytes 35685120 | tf_op jit(solution)/shard_map/dot_general | solution.py:181
  936.9 12.5 fusion.241
  950.1 292.5 %reduce-scatter.3.cloned.1.call-done = f32[640,768]{1,0:T(8,128)} async-done(((f32[10240,768]{1,0:T(8,128)}), f32[640,768]{1,0:T(8,128)}) %reduce-scatter.3.cloned.1.call-update) | async-done | bytes 1966096 | tf_op jit(solution)/shard_map/reduce_scatter | solution.py:184
  1252.6 119.5 %all-gather.5.cloned.1.call-done = bf16[10240,768]{1,0:T(8,128)(2,1)} async-done(((bf16[640,768]{1,0:T(8,128)(2,1)}), bf16[10240,768]{1,0:T(8,128)(2,1)}) %all-gather.5.cloned.1.call-update) | async-done | bytes 15728656 | tf_op jit(solution)/shard_map/all_gather | solution.py:199
  1372.1 13.9 fusion.233
  1387.8 12.5 fusion.242
  1400.9 13.4 convolution_convert_fusion.3
  1414.3 279.1 %reduce-scatter.5.cloned.1.call-done = f32[640,768]{1,0:T(8,128)} async-done(((f32[10240,768]{1,0:T(8,128)}), f32[640,768]{1,0:T(8,128)}) %reduce-scatter.5.cloned.1.call-update) | async-done | bytes 1966096 | tf_op jit(solution)/shard_map/reduce_scatter | solution.py:205
  1703.3 41.4 %while.53 = (s32[]{:T(128)}, f32[12,640]{1,0:T(8,128)S(1)}, s32[3]{0:T(128)S(1)}, f32[3,12,640,640]{2,3,1,0:T(8,128)}, f32[12,640]{1,0:T(8,128)S(1)}, /*index=5*...) while((s32[]{:T(128)}, f32[12,640]{1,0:T(8,128)S(1)}, ...), condition=%wide.region_21.22_spmd.clone, body=%wide.region_19.21_spmd.clone.sunk | while | flops 648814080 | bytes 23777512 | solution.py:232
  1721.6 9.3 fusion.341
  1735.4 9.3 fusion.341
  1744.7 335.3 %while.54 = (s32[]{:T(128)}, f32[640,12,64]{0,2,1:T(8,128)}, f32[32,12]{0,1:T(8,128)S(1)}, f32[64,12]{0,1:T(8,128)S(1)}, f32[64,12]{0,1:T(8,128)S(1)}, /*index=5...) while((s32[]{:T(128)}, f32[640,12,64]{0,2,1:T(8,128)}, ...), condition=%wide.region_23.24_spmd.clone, body=%wide.region_22.23_spmd.clone.sunk | while | flops 4249112320 | bytes 197791712 | solution.py:277
  1749.8 11.7 fusion.353
  1761.5 19.7 copy.122
  1788.2 18.4 fusion.357
  1806.6 18.6 fusion.358
  1842.4 10.9 fusion.355
  1861.5 11.7 fusion.353
  1873.2 19.7 copy.122
  1899.9 18.4 fusion.357
  1918.3 18.6 fusion.358
  1954.0 10.9 fusion.355
  1973.1 11.7 fusion.353
  1984.8 19.7 copy.122
  2011.5 18.4 fusion.357
  2030.0 18.6 fusion.358
  2065.6 10.9 fusion.355
  2138.6 62.2 %all-reduce = (f32[768]{0:T(1024)}, f32[768]{0:T(1024)}, f32[768]{0:T(1024)}, f32[768]{0:T(1024)}, f32[768]{0:T(1024)}, /*index=5*/f32[768]{0:T(1024)}, f32[768]...) all-reduce(f32[768]{0:T(1024)S(1)} %mul.233, ...), channel_id=1, replica_groups=mesh['seq'=2,'ffn'=16] {'seq','ffn'}, use_global_device_ids=true, to_apply=%region_26.27 | all-reduce | flops 8064 | bytes 64512 | tf_op jit(solution)/shard_map/psum | solution.py:310
  2206.3 129.8 %all-reduce.6.cloned.1.call-done = (f32[768,768]{0,1:T(8,128)}, f32[768,768]{0,1:T(8,128)}, f32[768,768]{0,1:T(8,128)}, f32[768,768]{1,0:T(8,128)}) async-done(((f32[768,768]{0,1:T(8,128)}, f32[768,768]{0,1:T(8,128)}, f32[768,768]{0,1:T(8,128)}, f32[768,768]{1,0:T(8,128)}), (f32[768,768]{0,1:T(8,128)}, f32[768,768]{0,1:T(8,128)}, f32[768,768]{0,1:T(8,128)}, ...) | async-done | bytes 9437200 | tf_op jit(solution)/shard_map/psum | solution.py:310
  (362 shorter events, 278.6 us)
Async XLA Ops:
  7.2 744.0 %copy-start = (bf16[768,768]{1,0:T(8,128)(2,1)S(1)}, bf16[768,768]{1,0:T(8,128)(2,1)}, u32[]{:S(2)}) copy-start(bf16[768,768]{1,0:T(8,128)(2,1)} %param.42) | copy-start | bytes 3538948
  7.2 903.2 %all-gather.3.cloned.1.call-start = ((), (), s32[]{:S(2)}) async-start(), calls=%async_computation.2 | async-start | bytes 16711680 | tf_op jit(solution)/shard_map/all_gather | solution.py:180
  8.0 2.7 copy-start.15
  8.0 2.7 copy-start.68
  11.6 6.4 copy-start.67
  11.7 6.9 copy-start.48
  11.7 6.9 copy-start.49
  11.7 7.6 copy-start.60
  13.1 13.8 collective-permute-start
  16.8 10.2 collective-permute-start.1
  22.8 2.9 copy-start.62
  22.8 3.5 copy-start.63
  22.8 4.1 copy-start.47
  33.4 4.8 copy-start.33
  33.4 4.8 copy-start.40
  33.4 4.8 copy-start.41
  33.4 4.8 copy-start.42
  33.4 4.8 copy-start.43
  551.8 18.7 copy-start.22
  551.8 18.7 copy-start.24
  551.8 18.7 copy-start.26
  551.8 18.7 copy-start.28
  551.8 18.7 copy-start.30
  754.4 488.2 %reduce-scatter.3.cloned.1.call-start = ((), (), s32[]{:S(2)}) async-start(), calls=%async_computation.3 | async-start | bytes 33423360 | tf_op jit(solution)/shard_map/reduce_scatter | solution.py:184
  754.5 182.4 %copy-start.35 = (bf16[192,768]{1,0:T(8,128)(2,1)S(1)}, bf16[192,768]{1,0:T(8,128)(2,1)}, u32[]{:S(2)}) copy-start(bf16[192,768]{1,0:T(8,128)(2,1)} %param.48) | copy-start | bytes 884740
  949.4 422.7 %all-gather.5.cloned.1.call-start = ((), (), s32[]{:S(2)}) async-start(), calls=%async_computation.4 | async-start | bytes 16711680 | tf_op jit(solution)/shard_map/all_gather | solution.py:199
  1252.5 440.9 %reduce-scatter.5.cloned.1.call-start = ((), (), s32[]{:S(2)}) async-start(), calls=%async_computation.5 | async-start | bytes 33423360 | tf_op jit(solution)/shard_map/reduce_scatter | solution.py:205
  1372.1 15.7 copy-start.36
  1400.4 730.3 %all-reduce.8.cloned.1.call-start = ((), (), s32[]{:S(2)}) async-start(), calls=%async_computation.7 | async-start | bytes 1179648 | tf_op jit(solution)/shard_map/psum | solution.py:212
  1703.2 41.5 %copy-start.23 = (s32[640]{0:T(1024)S(1)}, s32[640]{0:T(1024)}, u32[]{:S(2)}) copy-start(s32[640]{0:T(1024)} %copy-done.22) | copy-start | bytes 7684
  1703.2 41.5 %copy-start.25 = (s32[640]{0:T(1024)S(1)}, s32[640]{0:T(1024)}, u32[]{:S(2)}) copy-start(s32[640]{0:T(1024)} %copy-done.24) | copy-start | bytes 7684
  1703.2 41.5 %copy-start.27 = (s32[640]{0:T(1024)S(1)}, s32[640]{0:T(1024)}, u32[]{:S(2)}) copy-start(s32[640]{0:T(1024)} %copy-done.26) | copy-start | bytes 7684
  1703.2 41.5 %copy-start.29 = (s32[1920]{0:T(1024)S(1)}, s32[1920]{0:T(1024)}, u32[]{:S(2)}) copy-start(s32[1920]{0:T(1024)} %copy-done.28) | copy-start | bytes 23044
  1703.3 41.5 %copy-start.31 = (s32[1920]{0:T(1024)S(1)}, s32[1920]{0:T(1024)}, u32[]{:S(2)}) copy-start(s32[1920]{0:T(1024)} %copy-done.30) | copy-start | bytes 23044
  1703.3 41.5 %copy-start.34 = (s32[1920]{0:T(1024)S(1)}, s32[1920]{0:T(1024)}, u32[]{:S(2)}) copy-start(s32[1920]{0:T(1024)} %copy-done.32) | copy-start | bytes 23044
  1788.2 37.1 %slice-start = ((s8[9830400]{0:T(1024)(128)(4,1)}), s8[4194304]{0:T(1024)(128)(4,1)S(1)}, s32[]{:S(2)}) async-start(s8[9830400]{0:T(1024)(128)(4,1)} %bitcast.260), calls=%async_computation.8 | async-start | bytes 8388608 | tf_op jit(solution)/shard_map/while
  1788.2 37.1 %slice-start.1 = ((s8[9830400]{0:T(1024)(128)(4,1)}), s8[4194304]{0:T(1024)(128)(4,1)S(1)}, s32[]{:S(2)}) async-start(s8[9830400]{0:T(1024)(128)(4,1)} %bitcast.260), calls=%async_computation.9 | async-start | bytes 8388608 | tf_op jit(solution)/shard_map/while
  1806.6 18.7 slice-start.2
  1842.4 11.0 copy-start.2
  1899.8 37.1 %slice-start = ((s8[9830400]{0:T(1024)(128)(4,1)}), s8[4194304]{0:T(1024)(128)(4,1)S(1)}, s32[]{:S(2)}) async-start(s8[9830400]{0:T(1024)(128)(4,1)} %bitcast.260), calls=%async_computation.8 | async-start | bytes 8388608 | tf_op jit(solution)/shard_map/while
  1899.8 37.1 %slice-start.1 = ((s8[9830400]{0:T(1024)(128)(4,1)}), s8[4194304]{0:T(1024)(128)(4,1)S(1)}, s32[]{:S(2)}) async-start(s8[9830400]{0:T(1024)(128)(4,1)} %bitcast.260), calls=%async_computation.9 | async-start | bytes 8388608 | tf_op jit(solution)/shard_map/while
  1918.3 18.7 slice-start.2
  1954.0 11.0 copy-start.2
  2011.5 37.1 %slice-start = ((s8[9830400]{0:T(1024)(128)(4,1)}), s8[4194304]{0:T(1024)(128)(4,1)S(1)}, s32[]{:S(2)}) async-start(s8[9830400]{0:T(1024)(128)(4,1)} %bitcast.260), calls=%async_computation.8 | async-start | bytes 8388608 | tf_op jit(solution)/shard_map/while
  2011.5 37.1 %slice-start.1 = ((s8[9830400]{0:T(1024)(128)(4,1)}), s8[4194304]{0:T(1024)(128)(4,1)S(1)}, s32[]{:S(2)}) async-start(s8[9830400]{0:T(1024)(128)(4,1)} %bitcast.260), calls=%async_computation.9 | async-start | bytes 8388608 | tf_op jit(solution)/shard_map/while
  2029.9 18.7 slice-start.2
  2065.6 11.0 copy-start.2
  2085.0 7.0 copy-start.9
  2087.3 19.2 collective-permute-start.2
  2090.6 9.5 copy-start.4
  2090.6 15.9 collective-permute-start.3
  2100.0 236.1 %all-reduce.6.cloned.1.call-start = ((), (), s32[]{:S(2)}) async-start(), calls=%async_computation.6 | async-start | bytes 18874368 | tf_op jit(solution)/shard_map/psum | solution.py:310
  2101.5 2.5 copy-start.70
  2134.4 4.1 copy-start.53
  2134.4 4.2 copy-start.54
  2134.4 4.2 copy-start.55
  2134.4 4.2 copy-start.56
  2134.4 4.2 copy-start.57
  2134.4 4.2 copy-start.58
  2134.4 68.8 %copy-start.16 = (bf16[768,768]{1,0:T(8,128)(2,1)S(1)}, bf16[768,768]{1,0:T(8,128)(2,1)}, u32[]{:S(2)}) copy-start(bf16[768,768]{1,0:T(8,128)(2,1)} %param.40) | copy-start | bytes 3538948
  2200.7 2.9 copy-start.14
  2200.8 2.9 copy-start.51
  2336.0 3.2 copy-start.13
  2341.2 3.2 copy-start.12
  (32 other events, 44.2 us)
Sparse Core Ops, SparseCore 0:
  754.5 155.8 all-gather.2
  949.5 292.9 reduce-scatter.2
  1252.7 119.3 all-gather.4
  1400.5 292.9 reduce-scatter.4
  2100.1 30.5 all-reduce.7
  2138.4 197.5 all-reduce.5
where the time goes:
time: 2370 us; the launch traced here: 2350 us
  waiting for transfers between devices  986 us (42%)
  matrix products  627 us (26%)
  local copies, waits for them, and re-layouts  482 us (20%)
  other arithmetic  131 us (6%)
  blocking collectives  67.1 us (3%)
  loops' own time  35 us (1%)
    reduce_scatter x1, waiting for transfers between devices, on_device(): lax.psum_scatter(jnp.dot(active, w_down, preferred_element_type=jnp.float...  292 us
    reduce_scatter x1, waiting for transfers between devices, on_device(): lax.psum_scatter(jnp.dot(pre_grad, w_up.T, preferred_element_type=jnp.flo...  279 us
    dot_general x9, local copies, waits for them, and re-layouts, scores_at(): jnp.einsum('uld,ui->ild', member_flags, bias_lookup, preferred_element_ty...  243 us
    all_gather x1, waiting for transfers between devices, on_device(): normed_all = lax.all_gather(normed_low, 'ffn', axis=0, tiled=True)  156 us
    dot_general x9, matrix products, scores_at(): jnp.einsum('uld,ui->ild', member_flags, bias_lookup, preferred_element_ty...  150 us
    dot_general x9, matrix products, grad_step(): jnp.einsum('usy,dsy->ud', member_flags, scores_gradient, preferred_elemen...  144 us
    psum x1, waiting for transfers between devices, on_device(): lax.psum((local_sums[0], local_sums[1], local_sums[2], local_sums[3], loc...  130 us
    all_gather x1, waiting for transfers between devices, on_device(): grad_all = lax.all_gather(branch_grad, 'ffn', axis=0, tiled=True)  120 us
  transfers between devices with their start and end apart: 10, of which 6 were waited for; matrix products, arithmetic and copies ran while one was open for 2% of the time, Pallas kernels for 0%

commit v1 on v0

v1 whole, which is shorter than its diff:
```python
import functools

import jax
import jax.numpy as jnp
from jax import lax
from jax.experimental import pallas as pl
from jax.experimental.pallas import tpu as pltpu
from jax.sharding import PartitionSpec as P

VISUAL = 49
norm_eps = 1e-12
F32 = jnp.float32
BF16 = jnp.bfloat16
QB = 128
KB = 128
RB = 16
PAIRS = 6
NEG = -1e30
TILES = 12


def nn(a, b):
    return lax.dot_general(a, b, (((1,), (0,)), ((), ())), preferred_element_type=F32)


def nt(a, b):
    return lax.dot_general(a, b, (((1,), (1,)), ((), ())), preferred_element_type=F32)


def log_bucket(d, near, per_octave, sign):
    mag = jnp.abs(d)
    far = jnp.floor(jnp.log2(jnp.maximum(mag, 1.0) * (1.0 / near)) * per_octave + 0.0002) + near
    far = jnp.minimum(far, 2.0 * near - 1.0)
    return jnp.where(mag < near, mag, far) + jnp.where(d > 0, F32(sign), F32(0))


def put_buckets(b_ref, kmeta, qmeta, doc):
    key_doc = jnp.where(kmeta[:, 3:4] == doc.astype(F32), kmeta[:, 3:4], -1.0)
    same = key_doc == qmeta[3:4, :]
    b_ref[0] = jnp.where(same, log_bucket(kmeta[:, 0:1] - qmeta[0:1, :], 8.0, 2.0, 16.0), 16.0)
    b_ref[1] = log_bucket(kmeta[:, 1:2] - qmeta[1:2, :], 16.0, 4.0, 32.0)
    b_ref[2] = log_bucket(kmeta[:, 2:3] - qmeta[2:3, :], 16.0, 4.0, 32.0)


def one_hot(b_ref, row, count):
    cols = []
    for r in range(count):
        parts = []
        for t, size in ((0, 32), (1, 64), (2, 64)):
            v = jnp.broadcast_to(b_ref[t, pl.ds(row + r, 1), :], (size, QB)).astype(BF16)
            levels = lax.broadcasted_iota(jnp.int32, (size, QB), 0).astype(F32).astype(BF16)
            parts.append(jnp.where(v == levels, BF16(1), BF16(0)))
        cols.append(jnp.concatenate(parts, axis=0))
    return jnp.concatenate(cols, axis=1)


def fill_stack(stack, src):
    lane = lax.broadcasted_iota(jnp.int32, (QB, 128), 1)
    for p in range(PAIRS):
        x = src[:, 128 * p : 128 * p + 128].astype(F32)
        stack[p, 0:QB, :] = jnp.where(lane < 64, x, 0.0).astype(BF16)
        stack[p, QB : 2 * QB, :] = jnp.where(lane < 64, 0.0, x).astype(BF16)


def window_copies(pieces, keys, values, sems):
    rows = pieces[0].shape[0]
    return [
        pltpu.make_async_copy(piece, (keys, values)[i % 2].at[pl.ds(i // 2 * rows, rows), :], sems.at[i])
        for i, piece in enumerate(pieces)
    ]


def clear_tail(keys, values):
    for ref in (keys, values):
        ref[ref.shape[0] - KB :, :] = jnp.zeros((KB, ref.shape[1]), ref.dtype)


def tile_of(tiles, qb, t):
    return pl.multiple_of(tiles[qb, 1 + t], 16), tiles[qb, 1 + TILES + t]


def fwd_kernel(tiles, q_ref, k_low, v_low, k_own, v_own, k_high, v_high, kmeta_ref, qmeta_ref, tab_ref, ctx_ref, inv_ref, p_hbm,
               keys, values, s_scr, b_scr, bias_scr, qstack, ctx_t, m_scr, l_scr, pbuf, sems, in_sems):
    qb = pl.program_id(0)
    count = tiles[qb, 0]

    @pl.when(qb == 0)
    def _():
        copies = window_copies((k_low, v_low, k_own, v_own, k_high, v_high), keys, values, in_sems)
        for copy in copies:
            copy.start()
        clear_tail(keys, values)
        for copy in copies:
            copy.wait()

    fill_stack(qstack, q_ref)
    m_scr[...] = jnp.full_like(m_scr, -3e38)
    l_scr[...] = jnp.zeros_like(l_scr)
    ctx_t[...] = jnp.zeros_like(ctx_t)
    tab = tab_ref[...]

    def pass1(c, carry):
        base, doc = tile_of(tiles, qb, c)
        put_buckets(b_scr, kmeta_ref[pl.ds(base, KB), :], qmeta_ref[...], doc)

        def rows(g, carry):
            j = g * RB
            out = nn(tab, one_hot(b_scr, j, RB))
            for r in range(RB):
                bias_scr[pl.ds(j + r, 16, stride=KB), :] = out[:, r * QB : (r + 1) * QB]
            return carry

        lax.fori_loop(0, KB // RB, rows, 0, unroll=KB // RB)
        for p in range(PAIRS):
            raw = nt(keys[pl.ds(base, KB), 128 * p : 128 * p + 128], qstack[p])
            o = 8 + p
            s = raw + jnp.concatenate([bias_scr[p * KB : (p + 1) * KB, :], bias_scr[o * KB : (o + 1) * KB, :]], axis=1)
            s_scr[c, p] = s
            m_scr[p] = jnp.maximum(m_scr[p], jnp.max(s.reshape(KB // 8, 8, 2 * QB), axis=0))
        return carry

    lax.fori_loop(0, count, pass1, 0)
    for p in range(PAIRS):
        m_scr[p] = jnp.broadcast_to(jnp.max(m_scr[p], axis=0, keepdims=True), (8, 2 * QB))

    def pcopy(slot, c):
        return pltpu.make_async_copy(pbuf.at[slot], p_hbm.at[qb, c], sems.at[slot])

    def pass2(c, carry):
        base, _ = tile_of(tiles, qb, c)
        slot = lax.rem(c, 2)

        @pl.when(c >= 2)
        def _():
            pcopy(slot, c).wait()

        for p in range(PAIRS):
            e = jnp.exp(s_scr[c, p] - m_scr[p, 0:1, :])
            l_scr[p] = l_scr[p] + jnp.sum(e.reshape(KB // 8, 8, 2 * QB), axis=0)
            pb = e.astype(BF16)
            pbuf[slot, p] = pb
            value_t = values[pl.ds(base, KB), 128 * p : 128 * p + 128].T
            for h in range(2):
                r = 128 * p + 64 * h
                ctx_t[r : r + 64, :] = ctx_t[r : r + 64, :] + nn(value_t[64 * h : 64 * h + 64], pb[:, h * QB : (h + 1) * QB])
        pcopy(slot, c).start()
        return carry

    lax.fori_loop(0, count, pass2, 0)
    for p in range(PAIRS):
        inv = 1.0 / jnp.sum(l_scr[p], axis=0, keepdims=True)
        wide = jnp.concatenate([jnp.broadcast_to(inv[:, :QB], (64, QB)), jnp.broadcast_to(inv[:, QB:], (64, QB))], axis=0)
        w = slice(128 * p, 128 * p + 128)
        ctx_ref[:, w] = (ctx_t[w, :] * wide).T
        inv_ref[:, w] = wide.T

    @pl.when(count >= 2)
    def _():
        pcopy(lax.rem(count, 2), 0).wait()

    pcopy(lax.rem(count + 1, 2), 0).wait()


def attention_fwd(tiles, q, pieces, kmeta, qmeta, tab):
    rows, width = q.shape
    span = kmeta.shape[0]
    nq, nc = rows // QB, TILES
    vm = pltpu.VMEM
    hbm = pl.BlockSpec(memory_space=pl.ANY)
    full = lambda *s: pl.BlockSpec(s, lambda i, r: (0,) * len(s))
    block = pl.BlockSpec((QB, width), lambda i, r: (i, 0))
    return pl.pallas_call(
        fwd_kernel,
        grid_spec=pltpu.PrefetchScalarGridSpec(
            num_scalar_prefetch=1, grid=(nq,),
            in_specs=[block] + [hbm] * 6 + [full(span, 128), pl.BlockSpec((8, QB), lambda i, r: (0, i)), full(16, 160)],
            out_specs=[block, block, hbm],
            scratch_shapes=[
                vm((span, width), BF16), vm((span, width), BF16),
                vm((nc, PAIRS, KB, 2 * QB), F32), vm((3, KB, QB), F32), vm((16 * KB, QB), F32),
                vm((PAIRS, 2 * QB, 128), BF16), vm((width, QB), F32), vm((PAIRS, 8, 2 * QB), F32),
                vm((PAIRS, 8, 2 * QB), F32), vm((2, PAIRS, KB, 2 * QB), BF16),
                pltpu.SemaphoreType.DMA((2,)), pltpu.SemaphoreType.DMA((6,))]),
        out_shape=[jax.ShapeDtypeStruct((rows, width), F32), jax.ShapeDtypeStruct((rows, width), F32),
                   jax.ShapeDtypeStruct((nq, nc, PAIRS, KB, 2 * QB), BF16)],
        compiler_params=pltpu.CompilerParams(vmem_limit_bytes=56 * 2**20, dimension_semantics=("arbitrary",)),
        cost_estimate=pl.CostEstimate(flops=25 * 10**9, bytes_accessed=30 * 2**20, transcendentals=5 * 10**6),
        name="attention_forward",
    )(tiles, q, *pieces, kmeta, qmeta, tab)


def order_tables(ts, tx, ty):
    t = jnp.concatenate([ts.at[16].set(NEG), tx, ty], axis=0).T
    z = jnp.zeros((2, 160), t.dtype)
    return jnp.concatenate([t[0::2], z, t[1::2], z], axis=0)


def bwd_kernel(tiles, q_ref, dc_ref, ctx_ref, k_low, v_low, k_own, v_own, k_high, v_high, kmeta_ref, qmeta_ref, p_hbm,
               dq_ref, low_ref, own_k, own_v, high_ref, dtab_ref,
               keys, values, dk, dv, dq_t, b_scr, ds_scr, delta, qstack, cstack, pbuf, sems, in_sems):
    qb = pl.program_id(0)
    last = pl.num_programs(0) - 1
    count = tiles[qb, 0]

    def pcopy(c):
        slot = lax.rem(c, 2)
        return pltpu.make_async_copy(p_hbm.at[qb, c], pbuf.at[slot], sems.at[slot])

    pcopy(0).start()

    @pl.when(qb == 0)
    def _():
        copies = window_copies((k_low, v_low, k_own, v_own, k_high, v_high), keys, values, in_sems)
        for copy in copies:
            copy.start()
        clear_tail(keys, values)
        dk[...] = jnp.zeros_like(dk)
        dv[...] = jnp.zeros_like(dv)
        dtab_ref[...] = jnp.zeros_like(dtab_ref)
        ds_scr[...] = jnp.zeros_like(ds_scr)
        for copy in copies:
            copy.wait()

    fill_stack(qstack, q_ref)
    fill_stack(cstack, dc_ref)
    for p in range(PAIRS):
        w = slice(128 * p, 128 * p + 128)
        both = (dc_ref[:, w].astype(F32) * ctx_ref[:, w]).T
        delta[p : p + 1, :] = jnp.concatenate(
            [jnp.sum(both[:64], axis=0, keepdims=True), jnp.sum(both[64:], axis=0, keepdims=True)], axis=1)
    dq_t[...] = jnp.zeros_like(dq_t)

    def tile(c, carry):
        base, doc = tile_of(tiles, qb, c)
        slot = lax.rem(c, 2)
        put_buckets(b_scr, kmeta_ref[pl.ds(base, KB), :], qmeta_ref[...], doc)

        @pl.when(c + 1 < count)
        def _():
            pcopy(c + 1).start()

        pcopy(c).wait()
        for p in range(PAIRS):
            w = slice(128 * p, 128 * p + 128)
            dp = nt(values[pl.ds(base, KB), w], cstack[p])
            pb = pbuf[slot, p]
            ds = pb.astype(F32) * (dp - delta[p : p + 1, :])
            ds_scr[p * KB : (p + 1) * KB, :] = ds[:, :QB]
            ds_scr[(8 + p) * KB : (9 + p) * KB, :] = ds[:, QB:]
            dsb = ds.astype(BF16)
            dk[pl.ds(base, KB), w] = dk[pl.ds(base, KB), w] + nn(dsb, qstack[p])
            dv[pl.ds(base, KB), w] = dv[pl.ds(base, KB), w] + nn(pb, cstack[p])
            key_t = keys[pl.ds(base, KB), w].T
            for h in range(2):
                r = 128 * p + 64 * h
                dq_t[r : r + 64, :] = dq_t[r : r + 64, :] + nn(key_t[64 * h : 64 * h + 64], dsb[:, h * QB : (h + 1) * QB])

        def rows(g, acc):
            j = g * RB
            d = jnp.concatenate([ds_scr[pl.ds(j + r, 16, stride=KB), :] for r in range(RB)], axis=1).astype(BF16)
            return acc + nt(d, one_hot(b_scr, j, RB))

        dtab_ref[...] = lax.fori_loop(0, KB // RB, rows, dtab_ref[...], unroll=KB // RB)
        return carry

    lax.fori_loop(0, count, tile, 0)
    for p in range(PAIRS):
        w = slice(128 * p, 128 * p + 128)
        dq_ref[:, w] = dq_t[w, :].T.astype(BF16)

    @pl.when(qb == last)
    def _():
        rows = own_k.shape[0]
        width = dk.shape[1]
        own = [
            pltpu.make_async_copy(dk.at[pl.ds(rows, rows), :], own_k, in_sems.at[0]),
            pltpu.make_async_copy(dv.at[pl.ds(rows, rows), :], own_v, in_sems.at[1]),
        ]
        for copy in own:
            copy.start()

        def move(i, carry):
            r = pl.multiple_of(i * 32, 32)
            for src, col in ((dk, 0), (dv, width)):
                low_ref[pl.ds(r, 32), col : col + width] = src[pl.ds(r, 32), :].astype(BF16)
                high_ref[pl.ds(r, 32), col : col + width] = src[pl.ds(pl.multiple_of(2 * rows + r, 32), 32), :].astype(BF16)
            return carry

        lax.fori_loop(0, rows // 32, move, 0)
        for copy in own:
            copy.wait()


def attention_bwd(tiles, q, dc, ctx, pieces, kmeta, qmeta, probs):
    rows, width = q.shape
    span = kmeta.shape[0]
    nq, nc = rows // QB, TILES
    vm = pltpu.VMEM
    hbm = pl.BlockSpec(memory_space=pl.ANY)
    full = lambda *s: pl.BlockSpec(s, lambda i, r: (0,) * len(s))
    block = pl.BlockSpec((QB, width), lambda i, r: (i, 0))
    shape = jax.ShapeDtypeStruct
    return pl.pallas_call(
        bwd_kernel,
        grid_spec=pltpu.PrefetchScalarGridSpec(
            num_scalar_prefetch=1, grid=(nq,),
            in_specs=[block] * 3 + [hbm] * 6 + [full(span, 128), pl.BlockSpec((8, QB), lambda i, r: (0, i)), hbm],
            out_specs=[block, full(rows, 2 * width), hbm, hbm, full(rows, 2 * width), full(16, 160)],
            scratch_shapes=[
                vm((span, width), BF16), vm((span, width), BF16),
                vm((span, width), F32), vm((span, width), F32), vm((width, QB), F32),
                vm((3, KB, QB), F32), vm((16 * KB, QB), F32), vm((8, 2 * QB), F32),
                vm((PAIRS, 2 * QB, 128), BF16), vm((PAIRS, 2 * QB, 128), BF16),
                vm((2, PAIRS, KB, 2 * QB), BF16), pltpu.SemaphoreType.DMA((2,)), pltpu.SemaphoreType.DMA((6,))]),
        out_shape=[shape((rows, width), BF16), shape((rows, 2 * width), BF16), shape((rows, width), F32), shape((rows, width), F32),
                   shape((rows, 2 * width), BF16), shape((16, 160), F32)],
        compiler_params=pltpu.CompilerParams(vmem_limit_bytes=56 * 2**20, dimension_semantics=("arbitrary",)),
        cost_estimate=pl.CostEstimate(flops=40 * 10**9, bytes_accessed=40 * 2**20, transcendentals=0),
        name="attention_backward",
    )(tiles, q, dc, ctx, *pieces, kmeta, qmeta, probs)


def exchange_plan(n_seq, n_ffn, half):
    seq_bits = [("seq", 1 << b) for b in range(n_seq.bit_length() - 1)]
    ffn_bits = [("ffn", 1 << b) for b in range(1, n_ffn.bit_length() - 1)]
    unit = 16 * n_seq * n_ffn // 2
    if half % (3 * unit) == 0:
        orders = [seq_bits + ffn_bits, ffn_bits + seq_bits, ffn_bits[1:] + seq_bits + ffn_bits[:1]]
        return orders, half // 3
    return [seq_bits + ffn_bits], half


def sum_kernel(orders, length, a_ref, small_ref, unit_ref, out_ref, small_out, unit_out, work, core_in, slots, sums, small_in,
               core_sems, core_back, send_sems, recv_sems, back_send, back_recv, small_send, small_recv, unit_in, unit_mid, unit_send, unit_recv):
    seq, ffn = lax.axis_index("seq"), lax.axis_index("ffn")
    half = work.shape[0]
    streams = len(orders)
    steps = len(orders[0])
    core = lax.rem(ffn, 2)

    def bit_of(axis, bit):
        return lax.rem((seq if axis == "seq" else ffn) // bit, 2)

    def partner(axis, bit):
        flip = bit * (1 - 2 * bit_of(axis, bit))
        return {axis: (seq if axis == "seq" else ffn) + flip}

    peers = [("ffn", 1)] + sorted(orders[0])
    barrier = pltpu.get_barrier_semaphore()
    for axis, bit in peers:
        pl.semaphore_signal(barrier, inc=1, device_id=partner(axis, bit), device_id_type=pl.DeviceIdType.MESH)
    pl.semaphore_wait(barrier, len(peers))

    def remote(src, dst, send, recv, axis, bit):
        return pltpu.make_async_remote_copy(src_ref=src, dst_ref=dst, send_sem=send, recv_sem=recv,
                                            device_id=partner(axis, bit), device_id_type=pl.DeviceIdType.MESH)

    def at(ref, start, size):
        return ref.at[pl.ds(start if isinstance(start, int) else pl.multiple_of(start, 16), size), :]

    def add(dst, dst_lo, one, one_lo, two, two_lo, size):
        def body(i, carry):
            r = i * 16
            dst[pl.ds(pl.multiple_of(dst_lo + r, 16), 16), :] = (
                one[pl.ds(pl.multiple_of(one_lo + r, 16), 16), :].astype(F32)
                + two[pl.ds(pl.multiple_of(two_lo + r, 16), 16), :].astype(F32)
            ).astype(BF16)
            return carry
        lax.fori_loop(0, size // 16, body, 0)

    pending = []
    firsts = []
    for s in range(streams):
        copy = remote(at(a_ref, (1 - core) * half + s * length, length), at(core_in, s * length, length),
                      core_sems.at[s], core_sems.at[streams + s], "ffn", 1)
        copy.start()
        firsts.append(copy)
    sums[0] = small_ref[...]

    def small_copy(k):
        axis, bit = peers[k]
        return remote(sums.at[k], small_in.at[k], small_send.at[k], small_recv.at[k], axis, bit)
    small_copy(0).start()
    seq_peers = [peer for peer in peers if peer[0] == "seq"]

    def unit_copy(k):
        src = unit_ref if k == 0 else unit_mid.at[k - 1]
        return remote(src, unit_in.at[k], unit_send.at[k], unit_recv.at[k], *seq_peers[k])

    def unit_step(k):
        unit_copy(k).wait_recv()

        def body(i, carry):
            rows = pl.ds(pl.multiple_of(i * 16, 16), 16)
            src = unit_ref[rows, :] if k == 0 else unit_mid[k - 1, rows, :]
            total = src.astype(F32) + unit_in[k, rows, :].astype(F32)
            if k == len(seq_peers) - 1:
                unit_out[rows, :] = total
            else:
                unit_mid[k, rows, :] = total.astype(BF16)
            return carry
        lax.fori_loop(0, unit_ref.shape[0] // 16, body, 0)
        if k < len(seq_peers) - 1:
            unit_copy(k + 1).start()

    lows = [s * length for s in range(streams)]
    sizes = [length] * streams
    offs = []
    base = 0
    for s in range(streams):
        own = []
        size = length
        for k in range(steps):
            size //= 2
            own.append((base, size))
            base += size
        offs.append(own)

    def scatter(s, k):
        axis, bit = orders[s][k]
        size = sizes[s] // 2
        mine = lows[s] + bit_of(axis, bit) * size
        theirs = lows[s] + (1 - bit_of(axis, bit)) * size
        slot, _ = offs[s][k]
        copy = remote(at(work, theirs, size), at(slots, slot, size), send_sems.at[s, k], recv_sems.at[s, k], axis, bit)
        copy.start()
        return copy, mine, size

    flying = []
    for s in range(streams):
        firsts[s].wait_recv()
        add(work, s * length, a_ref, core * half + s * length, core_in, s * length, length)
        flying.append(scatter(s, 0))
    for k in range(steps):
        for s in range(streams):
            copy, mine, size = flying[s]
            copy.wait_recv()
            slot, _ = offs[s][k]
            last = k == steps - 1
            if last:
                add(out_ref, core * half + mine, work, mine, slots, slot, size)
            else:
                add(work, mine, work, mine, slots, slot, size)
            pending.append(copy)
            lows[s], sizes[s] = mine, size
            if not last:
                flying[s] = scatter(s, k + 1)
            else:
                flying[s] = gather(s, k, lows, sizes, orders, remote, at, out_ref, core, half, back_send, back_recv)
        if k == 0:
            unit_copy(0).start()
        elif k <= len(seq_peers):
            unit_step(k - 1)
        small_copy(k).wait_recv()
        sums[k + 1] = sums[k] + small_in[k]
        small_copy(k + 1).start()
    small_copy(steps).wait_recv()
    small_out[...] = sums[steps] + small_in[steps]
    finals = []
    for k in range(steps - 1, -1, -1):
        for s in range(streams):
            copy = flying[s]
            copy.wait_recv()
            pending.append(copy)
            axis, bit = orders[s][k]
            lows[s] = lows[s] - bit_of(axis, bit) * sizes[s]
            sizes[s] = 2 * sizes[s]
            if k:
                flying[s] = gather(s, k - 1, lows, sizes, orders, remote, at, out_ref, core, half, back_send, back_recv)
            else:
                copy = remote(at(out_ref, core * half + s * length, length), at(out_ref, core * half + s * length, length),
                              core_back.at[s], core_back.at[streams + s], "ffn", 1)
                copy.start()
                finals.append(copy)
    for copy in finals:
        copy.wait_recv()
    for copy in firsts + pending + finals:
        copy.wait_send()
    for k in range(steps + 1):
        small_copy(k).wait_send()
    for k in range(len(seq_peers)):
        unit_copy(k).wait_send()


def gather(s, k, lows, sizes, orders, remote, at, out_ref, core, half, back_send, back_recv):
    axis, bit = orders[s][k]
    place = at(out_ref, core * half + lows[s], sizes[s])
    copy = remote(place, place, back_send.at[s, k], back_recv.at[s, k], axis, bit)
    copy.start()
    return copy


def sum_everywhere(a, small, unit):
    n_seq, n_ffn = lax.axis_size("seq"), lax.axis_size("ffn")
    grain = 16 * n_seq * n_ffn // 2
    rows, width = a.shape
    half = -(-(rows // 2) // grain) * grain
    if 2 * half > rows:
        a = jnp.pad(a, ((0, 2 * half - rows), (0, 0)))
    orders, length = exchange_plan(n_seq, n_ffn, half)
    streams, steps = len(orders), len(orders[0])
    vm, dma = pltpu.VMEM, pltpu.SemaphoreType.DMA
    slot_rows = streams * (length - length // (1 << steps))
    bits = n_seq.bit_length() - 1
    out, small_out, unit_out = pl.pallas_call(
        functools.partial(sum_kernel, orders, length),
        out_shape=[jax.ShapeDtypeStruct(a.shape, BF16), jax.ShapeDtypeStruct(small.shape, F32), jax.ShapeDtypeStruct(unit.shape, F32)],
        in_specs=[pl.BlockSpec(memory_space=vm)] * 3,
        out_specs=[pl.BlockSpec(memory_space=vm)] * 3,
        scratch_shapes=[
            vm((half, width), BF16), vm((half, width), BF16), vm((slot_rows, width), BF16),
            vm((steps + 1,) + small.shape, F32), vm((steps + 1,) + small.shape, F32),
            dma((2 * streams,)), dma((2 * streams,)), dma((streams, steps)), dma((streams, steps)),
            dma((streams, steps)), dma((streams, steps)), dma((steps + 1,)), dma((steps + 1,)),
            vm((bits,) + unit.shape, BF16), vm((bits,) + unit.shape, BF16), dma((bits,)), dma((bits,)),
        ],
        compiler_params=pltpu.CompilerParams(collective_id=0, has_side_effects=True, vmem_limit_bytes=48 * 2**20),
        name="sum_everywhere",
    )(a, small, unit)
    return out[:rows], small_out, unit_out


UB = 512


def gelu_and_slope(x):
    z = jnp.abs(x) * 0.7071067811865476
    t = 1.0 / (1.0 + 0.3275911 * z)
    poly = ((((1.061405429 * t - 1.453152027) * t + 1.421413741) * t - 0.284496736) * t + 0.254829592) * t
    bell = jnp.exp(-z * z)
    tail = 0.5 * poly * bell
    phi = jnp.where(x < 0, tail, 1.0 - tail)
    return x * phi, phi + x * bell * 0.3989422804014327


def tn(a, b):
    return lax.dot_general(a, b, (((0,), (0,)), ((), ())), preferred_element_type=F32)


def ffn_up_kernel(normed_ref, up_ref, down_ref, active_ref, slope_ref, branch_ref):
    @pl.when(pl.program_id(0) == 0)
    def _():
        branch_ref[...] = jnp.zeros_like(branch_ref)

    rows = normed_ref.shape[0]
    size = rows // 2
    for r in range(0, rows, size):
        w = slice(r, r + size)
        act, slope = gelu_and_slope(nt(normed_ref[w, :], up_ref[...]))
        act = act.astype(BF16)
        active_ref[w, :] = act
        slope_ref[w, :] = slope.astype(BF16)
        branch_ref[w, :] = branch_ref[w, :] + nn(act, down_ref[...])


def ffn_up(normed, up, down):
    rows, wide = normed.shape
    units, width = down.shape
    full = lambda *s: pl.BlockSpec(s, lambda i: (0,) * len(s))
    col = pl.BlockSpec((rows, UB), lambda i: (0, i))
    shape = jax.ShapeDtypeStruct
    return pl.pallas_call(
        ffn_up_kernel,
        grid=(units // UB,),
        in_specs=[full(rows, wide), pl.BlockSpec((UB, wide), lambda i: (i, 0)), pl.BlockSpec((UB, width), lambda i: (i, 0))],
        out_specs=[col, col, full(rows, width)],
        out_shape=[shape((rows, units), BF16), shape((rows, units), BF16), shape((rows, width), F32)],
        compiler_params=pltpu.CompilerParams(vmem_limit_bytes=48 * 2**20, dimension_semantics=("arbitrary",)),
        cost_estimate=pl.CostEstimate(flops=2 * rows * units * (wide + width), bytes_accessed=20 * 2**20, transcendentals=2 * rows * units),
        name="ffn_up",
    )(normed, up, down)


def ffn_back_kernel(grad_ref, normed_ref, up_ref, down_ref, active_ref, slope_ref, unit_ref, normed_grad_ref):
    @pl.when(pl.program_id(0) == 0)
    def _():
        normed_grad_ref[...] = jnp.zeros_like(normed_grad_ref)

    grad = grad_ref[...]
    wide = normed_ref.shape[1]
    width = grad.shape[1]
    unit_ref[:, wide:] = tn(active_ref[...], grad).astype(BF16)
    pre = (nt(grad, down_ref[...]) * slope_ref[...].astype(F32)).astype(BF16)
    unit_ref[:, :wide] = tn(pre, normed_ref[...]).astype(BF16)
    normed_grad_ref[...] = normed_grad_ref[...] + nn(pre, up_ref[:, :width])


def ffn_back(grad, normed, up, down, active, slope):
    rows, wide = normed.shape
    units, width = down.shape
    full = lambda *s: pl.BlockSpec(s, lambda i: (0,) * len(s))
    col = pl.BlockSpec((rows, UB), lambda i: (0, i))
    row = lambda n: pl.BlockSpec((UB, n), lambda i: (i, 0))
    shape = jax.ShapeDtypeStruct
    return pl.pallas_call(
        ffn_back_kernel,
        grid=(units // UB,),
        in_specs=[full(rows, width), full(rows, wide), row(wide), row(width), col, col],
        out_specs=[row(wide + width), full(rows, width)],
        out_shape=[shape((units, wide + width), BF16), shape((rows, width), F32)],
        compiler_params=pltpu.CompilerParams(vmem_limit_bytes=48 * 2**20, dimension_semantics=("arbitrary",)),
        cost_estimate=pl.CostEstimate(flops=4 * rows * units * (wide + width), bytes_accessed=30 * 2**20, transcendentals=0),
        name="ffn_back",
    )(grad, normed, up, down, active, slope)


def from_behind(x, axis, by):
    devices = lax.axis_size(axis)
    pairs = [(i, i + by) for i in range(devices) if 0 <= i + by < devices]
    return lax.ppermute(x, axis, pairs)


def layer_norm(value, gain, shift):
    center = value - jnp.mean(value, axis=-1, keepdims=True)
    spread = jnp.mean(center * center, axis=-1, keepdims=True)
    return center * lax.rsqrt(spread + norm_eps) * gain + shift


def layout(row_ids, doc_ends):
    forwarded_value = row_ids[:, None] >= doc_ends[None, :]
    doc_ids = jnp.sum(forwarded_value.astype(jnp.int32), axis=1)
    starts = jnp.max(jnp.where(forwarded_value, doc_ends[None, :], 0), axis=1)
    offsets = row_ids - starts
    places = jnp.where(offsets < VISUAL, offsets, offsets - VISUAL)
    return (doc_ids, places)


def tile_table(starts, doc_ids, key_docs, window_start, rows):
    docs = jnp.arange(starts.shape[0] - 1, dtype=jnp.int32)
    place = jnp.arange(doc_ids.shape[0], dtype=jnp.int32)
    ends = jnp.max(jnp.where(key_docs[None, :] == docs[:, None], place[None, :] + 1, 0), axis=1)
    own = doc_ids[rows : 2 * rows]
    segments = own[0::QB, None] + jnp.arange(3, dtype=jnp.int32)[None, :]
    active = segments <= own[QB - 1 :: QB, None]
    hit = segments[:, :, None] == docs[None, None, :]
    low = jnp.sum(jnp.where(hit, starts[None, None, :-1], 0), axis=2) - window_start
    low = jnp.maximum(low, 0) // 16 * 16
    high = jnp.sum(jnp.where(hit, ends[None, None, :], 0), axis=2)
    count = jnp.where(active, jnp.maximum(high - low + KB - 1, 0) // KB, 0)
    before = jnp.cumsum(count, axis=1) - count
    index = jnp.arange(TILES, dtype=jnp.int32)[None, None, :] - before[:, :, None]
    inside = (index >= 0) & (index < count[:, :, None])
    base = jnp.sum(jnp.where(inside, low[:, :, None] + KB * index, 0), axis=1)
    doc = jnp.sum(jnp.where(inside, segments[:, :, None], 0), axis=1)
    return jnp.concatenate([jnp.sum(count, axis=1, keepdims=True), base, doc], axis=1).astype(jnp.int32)


def on_device(
    hidden_in, doc_lengths, box_x, box_y, token_valid, w_query, b_query, w_key, w_value, b_value,
    w_out, b_out, gain_attn, shift_attn, w_up, b_up, w_down, b_down, gain_out, shift_out,
    table_seq, table_x, table_y, out_grad,
):
    rows = hidden_in.shape[0]
    width = hidden_in.shape[1]
    heads = table_seq.shape[1]
    group_rows = box_x.shape[0]
    span = 3 * rows
    first_row = lax.axis_index("ffn") * rows
    doc_ends = jnp.cumsum(doc_lengths[0])

    n_ffn = lax.axis_size("ffn")
    up = [(i, i + 1) for i in range(n_ffn - 1)]
    hidden_low = lax.ppermute(hidden_in, "ffn", up)
    hidden_high = lax.ppermute(hidden_in, "ffn", [(j, i) for i, j in up])

    units = b_up.shape[0]
    up_ext = jnp.concatenate([w_up.T, b_up[:, None], jnp.zeros((units, 127), BF16)], axis=1)
    up_all = lax.all_gather(up_ext, "ffn", axis=0, tiled=True)
    down_all = lax.all_gather(w_down, "ffn", axis=0, tiled=True)

    window_rows = first_row - rows + jnp.arange(span, dtype=jnp.int32)
    doc_ids, places = layout(window_rows, doc_ends)
    inside = (window_rows >= 0) & (window_rows < group_rows)

    def window_of(item):
        edge = jnp.zeros((rows,), item.dtype)
        padded = jnp.concatenate([edge, item, edge])
        return lax.dynamic_slice_in_dim(padded, first_row, span)

    win_x, win_y = window_of(box_x), window_of(box_y)
    key_open = (window_of(token_valid) == 1) & inside
    key_docs = jnp.where(key_open, doc_ids, -1)
    kmeta = jnp.stack([places, win_x, win_y, key_docs], axis=1).astype(F32)
    kmeta = jnp.pad(kmeta, ((0, KB), (0, 124)), constant_values=-1.0)
    own = slice(rows, 2 * rows)
    qmeta = jnp.stack([places[own], win_x[own], win_y[own], doc_ids[own]], axis=0).astype(F32)
    qmeta = jnp.pad(qmeta, ((0, 4), (0, 0)))
    starts = jnp.concatenate([jnp.zeros((1,), doc_ends.dtype), doc_ends])
    tiles = tile_table(starts, doc_ids, key_docs, first_row - rows, rows)
    tables = order_tables(table_seq, table_x, table_y)

    query = ((jnp.dot(hidden_in, w_query, preferred_element_type=F32) + b_query) * 0.125).astype(BF16)
    pieces = []
    for part in (hidden_low, hidden_in, hidden_high):
        pieces.append(jnp.dot(part, w_key, preferred_element_type=F32).astype(BF16))
        pieces.append((jnp.dot(part, w_value, preferred_element_type=F32) + b_value).astype(BF16))

    context, inv, probs = attention_fwd(tiles, query, pieces, kmeta, qmeta, tables)
    context_low = context.astype(BF16)
    attn = jnp.dot(context_low, w_out, preferred_element_type=F32) + b_out
    inputs = hidden_in.astype(F32)
    normed, norm_pull = jax.vjp(
        layer_norm, inputs + attn, gain_attn.astype(F32), shift_attn.astype(F32)
    )
    normed_low = normed.astype(BF16)
    ones = jnp.concatenate([jnp.ones((rows, 1), BF16), jnp.zeros((rows, 127), BF16)], axis=1)
    normed_ext = jnp.concatenate([normed_low, ones], axis=1)
    active, slope, branch = ffn_up(normed_ext, up_all, down_all)
    hidden_out, out_pull = jax.vjp(
        layer_norm, normed + (branch + b_down), gain_out.astype(F32), shift_out.astype(F32)
    )
    mid_grad, grad_gain_out, grad_shift_out = out_pull(out_grad.astype(F32))
    branch_grad = mid_grad.astype(BF16)
    grad_b_down = jnp.sum(branch_grad.astype(F32), axis=0)
    unit_part, branch_back = ffn_back(branch_grad, normed_ext, up_all, down_all, active, slope)
    unit_grad = lax.psum_scatter(unit_part, "ffn", scatter_dimension=0, tiled=True)
    normed_grad = mid_grad + branch_back
    mid1_grad, grad_gain_attn, grad_shift_attn = norm_pull(normed_grad)
    attn_grad = mid1_grad.astype(BF16)
    grad_b_out = jnp.sum(attn_grad.astype(F32), axis=0)
    grad_w_out = jnp.dot(context_low.T, attn_grad, preferred_element_type=F32)
    scaled = (nt(attn_grad, w_out) * inv).astype(BF16)
    query_grad, low_terms, own_key, own_value, high_terms, table_sum = attention_bwd(
        tiles, query, scaled, context, pieces, kmeta, qmeta, probs
    )
    from_below = from_behind(high_terms, "ffn", 1).astype(F32)
    from_above = from_behind(low_terms, "ffn", -1).astype(F32)
    key_grad = (own_key + from_below[:, :width] + from_above[:, :width]).astype(BF16)
    value_grad = (own_value + from_below[:, width:] + from_above[:, width:]).astype(BF16)
    hidden_grad = (
        mid1_grad + nt(query_grad, w_query) * 0.125 + nt(key_grad, w_key) + nt(value_grad, w_value)
    )
    big = jnp.concatenate(
        [
            (jnp.dot(hidden_in.T, query_grad, preferred_element_type=F32) * 0.125).astype(BF16),
            jnp.dot(hidden_in.T, key_grad, preferred_element_type=F32).astype(BF16),
            jnp.dot(hidden_in.T, value_grad, preferred_element_type=F32).astype(BF16),
            grad_w_out.astype(BF16),
        ],
        axis=0,
    )
    small = jnp.stack(
        [
            jnp.sum(query_grad.astype(F32), axis=0) * 0.125,
            jnp.sum(value_grad.astype(F32), axis=0),
            grad_b_out,
            grad_gain_attn,
            grad_shift_attn,
            grad_b_down,
            grad_gain_out,
            grad_shift_out,
        ]
    )
    levels = table_sum.shape[1]
    small = jnp.concatenate([small, jnp.pad(table_sum, ((0, 0), (0, width - levels)))], axis=0)
    big, small, unit_grad = sum_everywhere(big, small, unit_grad)
    grad_w_up = unit_grad[:, :width].T
    grad_b_up = unit_grad[:, width]
    grad_w_down = unit_grad[:, width + 128 :]
    grads = [big[i * width : (i + 1) * width].astype(F32) for i in range(4)]
    vec = [small[i] for i in range(8)]
    table_all = jnp.stack([small[8 + h // 2 + 8 * (h % 2), :levels] for h in range(heads)], axis=1)
    return (
        hidden_out, hidden_grad, grads[0], vec[0], grads[1], grads[2], vec[1], grads[3], vec[2], vec[3], vec[4],
        grad_w_up, grad_b_up, grad_w_down, vec[5], vec[6], vec[7],
        table_all[:32], table_all[32:96], table_all[96:],
    )


def solution(mesh):
    in_specs = (
        P(("seq", "ffn"), None),
        P("seq", None),
        P("seq"),
        P("seq"),
        P("seq"),
        P(),
        P(),
        P(),
        P(),
        P(),
        P(),
        P(),
        P(),
        P(),
        P(None, "ffn"),
        P("ffn"),
        P("ffn", None),
        P(),
        P(),
        P(),
        P(),
        P(),
        P(),
        P(("seq", "ffn"), None),
    )
    out_specs = (
        P(("seq", "ffn"), None),
        P(("seq", "ffn"), None),
        P(),
        P(),
        P(),
        P(),
        P(),
        P(),
        P(),
        P(),
        P(),
        P(None, "ffn"),
        P("ffn"),
        P("ffn", None),
        P(),
        P(),
        P(),
        P(),
        P(),
        P(),
    )
    return jax.shard_map(
        on_device, mesh=mesh, in_specs=in_specs, out_specs=out_specs, check_vma=False
    )
```

time: 2370 us -> 418 us (0.18)
  waiting for transfers between devices: 986 us -> 76.7 us
  matrix products: 627 us -> 39.2 us
  local copies, waits for them, and re-layouts: 482 us -> 18.5 us
  Pallas kernels: 0 us -> 224 us
  other arithmetic: 131 us -> 34.3 us
  blocking collectives: 67.1 us -> 0 us
  loops' own time: 35 us -> 0 us
    dot_general x57 -> x16, matrix products: 627 us -> 39.2 us  [the longest x3 9.5 us: on_device(): pieces.append(jnp.dot(part, w_key, preferred_element_type=F32).astype(BF16))]
    reduce_scatter x2 -> x1, waiting for transfers between devices: 572 us -> 42.8 us  [on_device(): lax.psum_scatter(unit_part, 'ffn', scatter_dimension=0, tiled=True)]
    dot_general x9 -> x0, local copies, waits for them, and re-layouts: 243 us -> none  [scores_at(): jnp.einsum('uld,ui->ild', member_flags, bias_lookup, preferred_element_ty...]
    all_gather x2, waiting for transfers between devices: 275 us -> 33.9 us  [the longest x1 33.8 us: on_device(): up_all = lax.all_gather(up_ext, 'ffn', axis=0, tiled=True)]
    pallas_call x0 -> x5, Pallas kernels: none -> 224 us  [the longest x1 78.1 us: sum_everywhere(): pl.pallas_call(functools.partial(sum_kernel, orders, length), out_shape=[...]
    psum x2 -> x0, waiting for transfers between devices: 139 us -> none  [the longest x1 130 us: on_device(): lax.psum((local_sums[0], local_sums[1], local_sums[2], local_sums[3], loc...]
    dynamic_slice x54 -> x0, local copies, waits for them, and re-layouts: 136 us -> none  [the longest x6 110 us: probs_at(): return jnp.exp(stored[index] - top[:, :, None]) / total[:, :, None]]
    psum x2 -> x0, blocking collectives: 67.1 us -> none  [the longest x1 62.2 us: on_device(): lax.psum((local_sums[0], local_sums[1], local_sums[2], local_sums[3], loc...]
  transfers between devices with their start and end apart: 10 -> 7, of which waited for: 6 -> 2; matrix products, arithmetic and copies ran while one was open for 2% -> 16% of each run, Pallas kernels for 0% -> 26%
where the time goes in v1:
time: 418 us; the launch traced here: 416 us
  Pallas kernels  224 us (54%)
  waiting for transfers between devices  76.7 us (18%)
  matrix products  39.2 us (9%)
  other arithmetic  34.3 us (8%)
  local copies, waits for them, and re-layouts  18.5 us (4%)
  between operations  14.3 us (3%)
  starting transfers between devices  8.13 us (2%)
    pallas_call x1, Pallas kernels, sum_everywhere(): pl.pallas_call(functools.partial(sum_kernel, orders, length), out_shape=[...  78.1 us
    pallas_call x1, Pallas kernels, attention_bwd(): pl.pallas_call(bwd_kernel, grid_spec=pltpu.PrefetchScalarGridSpec(num_sca...  64 us
    pallas_call x1, Pallas kernels, attention_fwd(): pl.pallas_call(fwd_kernel, grid_spec=pltpu.PrefetchScalarGridSpec(num_sca...  43.6 us
    reduce_scatter x1, waiting for transfers between devices, on_device(): lax.psum_scatter(unit_part, 'ffn', scatter_dimension=0, tiled=True)  42.8 us
    all_gather x1, waiting for transfers between devices, on_device(): up_all = lax.all_gather(up_ext, 'ffn', axis=0, tiled=True)  33.8 us
    pallas_call x1, Pallas kernels, ffn_back(): pl.pallas_call(ffn_back_kernel, grid=(units // UB,), in_specs=[full(rows,...  21.3 us
    pallas_call x1, Pallas kernels, ffn_up(): pl.pallas_call(ffn_up_kernel, grid=(units // UB,), in_specs=[full(rows, w...  17.4 us
    unnamed x57, local copies, waits for them, and re-layouts  9.84 us
  transfers between devices with their start and end apart: 7, of which 2 were waited for; matrix products, arithmetic and copies ran while one was open for 16% of the time, Pallas kernels for 26%

profile of v1, /device:TPU:0, one launch (start us, length us, event | category | flops | bytes accessed | tf_op | source)
XLA Modules:
  0.0 415.6 jit_solution(7601650193688983820)
XLA Ops:
  7.3 0.8 copy.70
  8.1 0.7 broadcast_in_dim.138
  8.9 1.8 maximum_maximum_fusion.1
  10.8 1.3 collective-permute-start.1
  12.1 4.0 collective-permute-start
  16.2 0.8 maximum_bitcast_fusion
  17.0 0.7 copy.62
  18.3 0.8 fusion.21
  19.2 0.7 convert_element_type.153
  19.9 0.7 convert_element_type.143
  20.6 0.7 convert_element_type.154
  21.3 0.7 convert_element_type.157
  21.9 0.7 convert_element_type.140
  22.6 0.7 convert_element_type.152
  23.3 0.7 convert_element_type.156
  24.0 0.7 convert_element_type.158
  26.9 1.0 pad.14.kmeta_ref
  28.6 3.3 convolution_convert_fusion.4.k_own
  31.9 0.7 pad_add_fusion.tiles
  32.6 1.9 multiply_convert_fusion.2.q_ref
  34.5 1.9 add_convert_fusion.1.v_own
  36.3 3.1 convolution_convert_fusion.3.k_high
  39.5 3.1 convolution_convert_fusion.5.k_low
  42.6 3.1 add_convert_fusion.v_high
  45.7 3.1 add_convert_fusion.2.v_low
  48.8 43.6 %attention_forward.1 = (f32[640,768]{1,0:T(8,128)}, f32[640,768]{1,0:T(8,128)}, bf16[5,12,6,128,256]{4,3,2,1,0:T(8,128)(2,1)}) custom-call(s32[5,25]{1,0:T(8,128)} %pad_add_fusion.tiles, bf16[640,768]{1,0:T(8,128)(2,1)} %multiply_convert_fusion.2.q_ref, bf16[640,768]{1,0:T(8,128)(2,1)} %convolution_convert_fusion.5.k_low, ...), custom_call_target="tpu_custom_call" | custom-call | flops 24999999488 | bytes 31457280 | tf_op jit(solution)/shard_map/attention_forward/pallas_call | solution.py:172
  92.4 2.6 fusion.39
  96.6 33.8 %all-gather.3.cloned.1.call-done.up_ref = bf16[3072,896]{1,0:T(8,128)(2,1)} async-done(((bf16[192,896]{1,0:T(8,128)(2,1)}), bf16[3072,896]{1,0:T(8,128)(2,1)}) %all-gather.3.cloned.1.call-update) | async-done | bytes 5505040 | tf_op jit(solution)/shard_map/all_gather | solution.py:668
  130.5 17.4 %ffn_up.1 = (bf16[640,3072]{1,0:T(8,128)(2,1)}, bf16[640,3072]{1,0:T(8,128)(2,1)}, f32[640,768]{1,0:T(8,128)S(1)}) custom-call(bf16[640,896]{1,0:T(8,128)(2,1)S(1)} %maximum_maximum_fusion.normed_ref, bf16[3072,896]{1,0:T(8,128)(2,1)} %all-gather.3.cloned.1.call-done.up_ref, bf16[3072,768]{1,0:T(8,128)(2,1)} %all-gather.5.cloned.1.call-done.down_ref), custom_call_target="tpu_custom_call" | custom-call | flops 6543114240 | bytes 20971520 | tf_op jit(solution)/shard_map/ffn_up/pallas_call | solution.py:562
  147.8 0.7 fusion.33
  148.9 0.8 copy-done.8
  149.7 0.9 fusion.3
  150.6 2.1 fusion.32
  153.0 1.0 copy-done.7
  154.0 0.7 copy-done.2
  154.7 21.3 %ffn_back.1 = (bf16[3072,1664]{1,0:T(8,128)(2,1)}, f32[640,768]{1,0:T(8,128)S(1)}) custom-call(bf16[640,768]{1,0:T(8,128)(2,1)S(1)} %get-tuple-element.87.grad_ref, bf16[640,896]{1,0:T(8,128)(2,1)S(1)} %copy-done.2, bf16[3072,896]{1,0:T(8,128)(2,1)} %all-gather.3.cloned.1.call-done.up_ref, bf16[3072,768]{1,0:T(8,128)(2,1)} %all-gather.5.cloned.1.call-done.down_ref, ...), custom_call_target="tpu_custom_call" | custom-call | flops 13086228480 | bytes 31457280 | tf_op jit(solution)/shard_map/ffn_back/pallas_call | solution.py:595
  176.1 3.2 multiply_reduce_fusion
  179.3 0.7 fusion.31
  180.9 0.8 copy-done.12
  181.7 2.0 multiply_convert_fusion.1.dc_ref
  183.6 64.0 %attention_backward.1 = (bf16[640,768]{1,0:T(8,128)(2,1)}, bf16[640,1536]{1,0:T(8,128)(2,1)}, f32[640,768]{1,0:T(8,128)}, f32[640,768]{1,0:T(8,128)}, bf16[640,1536]{1,0:T(8,128)(2,1)}, /*index=5*/f32[16,160]{1,0:T(8,128)}) custom-call(s32[5,25]{1,0:T(8,128)} %pad_add_fusion.tiles, bf16[640,768]{1,0:T(8,128)(2,1)} %multiply_convert_fusion.2.q_ref, ...), custom_call_target="tpu_custom_call" | custom-call | flops 40000000000 | bytes 41943040 | tf_op jit(solution)/shard_map/attention_backward/pallas_call | solution.py:303
  247.7 1.4 collective-permute-start.2
  249.1 1.3 collective-permute-start.3
  250.5 1.4 convert_reduce_fusion.4
  251.9 0.7 pad.16
  252.6 3.6 fusion.9
  256.2 2.1 convolution_convert_fusion
  258.3 2.2 fusion.40
  261.7 1.0 copy-done.10
  263.2 2.0 convert_reduce_fusion.3
  265.4 2.8 fusion.8
  268.1 1.1 fusion.7
  269.3 1.0 fusion.41
  270.9 2.6 pad_maximum_fusion.a_ref
  273.6 0.8 copy-done.13
  274.8 2.4 add_add_fusion.2
  277.2 42.8 %reduce-scatter.2.cloned.1.call-done.unit_ref = bf16[192,1664]{1,0:T(8,128)(2,1)} async-done(((bf16[3072,1664]{1,0:T(8,128)(2,1)}), bf16[192,1664]{1,0:T(8,128)(2,1)}) %reduce-scatter.2.cloned.1.call-update) | async-done | bytes 638992 | tf_op jit(solution)/shard_map/reduce_scatter | solution.py:716
  320.0 1.1 copy-done.3
  321.1 78.1 %sum_everywhere.1 = (bf16[3072,768]{1,0:T(8,128)(2,1)}, f32[24,768]{1,0:T(8,128)S(1)}, f32[192,1664]{1,0:T(8,128)S(1)}) custom-call(bf16[3072,768]{1,0:T(8,128)(2,1)} %pad_maximum_fusion.a_ref, f32[24,768]{1,0:T(8,128)S(1)} %concatenate.45.small_ref, bf16[192,1664]{1,0:T(8,128)(2,1)S(1)} %copy-done.3), custom_call_target="tpu_custom_call" | custom-call | tf_op jit(solution)/shard_map/sum_everywhere/pallas_call | solution.py:505
  399.2 0.7 slice_reduce_fusion
  399.8 1.1 fusion.37
  400.9 0.7 slice_reduce_fusion.1
  402.3 0.7 fusion.38
  402.9 6.2 %slice_convert_fusion = (f32[768,768]{1,0:T(8,128)}, f32[768,768]{1,0:T(8,128)}, f32[768,768]{1,0:T(8,128)}, f32[768,768]{1,0:T(8,128)}) fusion(bf16[3072,768]{1,0:T(8,128)(2,1)} %get-tuple-element.63), kind=kLoop, calls=%fused_computation.48 | loop fusion | flops 2359296 | bytes 14155776 | tf_op jit(solution)/shard_map/convert_element_type | solution.py:760
  (130 shorter events, 10.4 us)
Async XLA Ops:
  7.2 21.4 %copy-start = (bf16[768,768]{1,0:T(8,128)(2,1)S(1)}, bf16[768,768]{1,0:T(8,128)(2,1)}, u32[]{:S(2)}) copy-start(bf16[768,768]{1,0:T(8,128)(2,1)} %param.33) | copy-start | bytes 3538948
  7.2 89.4 %all-gather.5.cloned.1.call-start = ((), (), s32[]{:S(2)}) async-start(), calls=%async_computation.2 | async-start | bytes 5013504 | tf_op jit(solution)/shard_map/all_gather | solution.py:669
  8.1 122.4 %all-gather.3.cloned.1.call-start = ((), (), s32[]{:S(2)}) async-start(), calls=%async_computation.1 | async-start | bytes 5849088 | tf_op jit(solution)/shard_map/all_gather | solution.py:668
  10.7 309.3 %reduce-scatter.2.cloned.1.call-start = ((), (), s32[]{:S(2)}) async-start(), calls=%async_computation.3 | async-start | bytes 10862592 | tf_op jit(solution)/shard_map/reduce_scatter | solution.py:716
  10.8 25.6 %collective-permute-start.1 = (bf16[640,768]{1,0:T(8,128)(2,1)}, bf16[640,768]{1,0:T(8,128)(2,1)}, u32[]{:S(2)}, u32[]{:S(2)}) collective-permute-start(bf16[640,768]{1,0:T(8,128)(2,1)} %param.26), channel_id=1, source_target_pairs={{1,0},{2,1},{3,2},{4,3},{5,4},{6,5},{7,6},{8,7},{9,8},{10,9},{11,1... | collective-permute-start | bytes 2949128 | tf_op jit(solution)/shard_map/ppermute | solution.py:664
  12.1 27.4 %collective-permute-start = (bf16[640,768]{1,0:T(8,128)(2,1)}, bf16[640,768]{1,0:T(8,128)(2,1)}, u32[]{:S(2)}, u32[]{:S(2)}) collective-permute-start(bf16[640,768]{1,0:T(8,128)(2,1)} %param.26), channel_id=1, source_target_pairs={{0,1},{1,2},{2,3},{3,4},{4,5},{5,6},{6,7},{7,8},{8,9},{9,10},{10,1... | collective-permute-start | bytes 2949128 | tf_op jit(solution)/shard_map/ppermute | solution.py:663
  28.6 4.0 copy-start.22
  28.6 3.9 copy-start.24
  32.6 1.9 copy-start.14
  48.8 43.6 %copy-start.18 = (bf16[768,768]{1,0:T(8,128)(2,1)S(1)}, bf16[768,768]{1,0:T(8,128)(2,1)}, u32[]{:S(2)}) copy-start(bf16[768,768]{1,0:T(8,128)(2,1)} %param.36) | copy-start | bytes 3538948
  95.0 1.3 copy-start.4
  96.6 51.3 %copy-start.1 = (bf16[640,896]{1,0:T(8,128)(2,1)}, bf16[640,896]{1,0:T(8,128)(2,1)S(1)}, u32[]{:S(2)}) copy-start(bf16[640,896]{1,0:T(8,128)(2,1)S(1)} %maximum_maximum_fusion.normed_ref) | copy-start | bytes 3440644
  130.5 17.4 %copy-start.5 = (f32[640,768]{1,0:T(8,128)S(1)}, f32[640,768]{1,0:T(8,128)}, u32[]{:S(2)}) copy-start(f32[640,768]{1,0:T(8,128)} %copy-done.4) | copy-start | bytes 5898244
  148.5 1.2 copy-start.8
  152.7 1.3 copy-start.7
  152.7 2.0 copy-start.2
  176.0 3.2 copy-start.6
  179.3 1.6 copy-start.19
  180.0 1.7 copy-start.12
  183.6 69.0 %copy-start.25 = (bf16[640,768]{1,0:T(8,128)(2,1)S(1)}, bf16[640,768]{1,0:T(8,128)(2,1)}, u32[]{:S(2)}) copy-start(bf16[640,768]{1,0:T(8,128)(2,1)} %param.26) | copy-start | bytes 2949124
  247.7 12.9 %collective-permute-start.2 = (bf16[640,1536]{1,0:T(8,128)(2,1)}, bf16[640,1536]{1,0:T(8,128)(2,1)S(1)}, u32[]{:S(2)}, u32[]{:S(2)}) collective-permute-start(bf16[640,1536]{1,0:T(8,128)(2,1)} %get-tuple-element.58), channel_id=1, source_target_pairs={{0,1},{1,2},{2,3},{3,4},{4,5},{5,6},{6,7},{7,8},{8,9},{9,10},{10,1... | collective-permute-start | bytes 5898248 | tf_op jit(solution)/shard_map/ppermute | solution.py:610
  249.1 12.0 %collective-permute-start.3 = (bf16[640,1536]{1,0:T(8,128)(2,1)}, bf16[640,1536]{1,0:T(8,128)(2,1)S(1)}, u32[]{:S(2)}, u32[]{:S(2)}) collective-permute-start(bf16[640,1536]{1,0:T(8,128)(2,1)} %get-tuple-element.59), channel_id=1, source_target_pairs={{1,0},{2,1},{3,2},{4,3},{5,4},{6,5},{7,6},{8,7},{9,8},{10,9},{11,1... | collective-permute-start | bytes 5898248 | tf_op jit(solution)/shard_map/ppermute | solution.py:610
  252.6 3.6 copy-start.27
  256.2 2.1 copy-start.20
  256.2 2.1 copy-start.23
  261.1 1.6 copy-start.10
  261.1 2.1 copy-start.11
  265.3 2.8 copy-start.21
  265.3 2.8 copy-start.26
  269.3 1.3 copy-start.16
  269.3 1.6 copy-start.17
  270.9 2.6 copy-start.9
  270.9 3.4 copy-start.13
  270.9 3.9 copy-start.15
  320.0 1.1 copy-start.3
Sparse Core Ops, SparseCore 0:
  10.3 61.2 all-gather.4
  74.5 55.9 all-gather.2
  176.2 143.7 reduce-scatter.1

commit v2 on v1

--- a/solution.py
+++ b/solution.py
@@ -62,11 +62,11 @@
         stack[p, QB : 2 * QB, :] = jnp.where(lane < 64, 0.0, x).astype(BF16)
 
 
-def window_copies(pieces, keys, values, sems):
-    rows = pieces[0].shape[0]
+def window_copies(k_hbm, v_hbm, keys, values, sems):
+    rows = k_hbm.shape[0]
     return [
-        pltpu.make_async_copy(piece, (keys, values)[i % 2].at[pl.ds(i // 2 * rows, rows), :], sems.at[i])
-        for i, piece in enumerate(pieces)
+        pltpu.make_async_copy(k_hbm, keys.at[pl.ds(0, rows), :], sems.at[0]),
+        pltpu.make_async_copy(v_hbm, values.at[pl.ds(0, rows), :], sems.at[1]),
     ]
 
 
@@ -79,14 +79,14 @@
     return pl.multiple_of(tiles[qb, 1 + t], 16), tiles[qb, 1 + TILES + t]
 
 
-def fwd_kernel(tiles, q_ref, k_low, v_low, k_own, v_own, k_high, v_high, kmeta_ref, qmeta_ref, tab_ref, ctx_ref, inv_ref, p_hbm,
+def fwd_kernel(tiles, q_ref, k_hbm, v_hbm, kmeta_ref, qmeta_ref, tab_ref, ctx_ref, inv_ref, p_hbm,
                keys, values, s_scr, b_scr, bias_scr, qstack, ctx_t, m_scr, l_scr, pbuf, sems, in_sems):
     qb = pl.program_id(0)
     count = tiles[qb, 0]
 
     @pl.when(qb == 0)
     def _():
-        copies = window_copies((k_low, v_low, k_own, v_own, k_high, v_high), keys, values, in_sems)
+        copies = window_copies(k_hbm, v_hbm, keys, values, in_sems)
         for copy in copies:
             copy.start()
         clear_tail(keys, values)
@@ -161,7 +161,7 @@
     pcopy(lax.rem(count + 1, 2), 0).wait()
 
 
-def attention_fwd(tiles, q, pieces, kmeta, qmeta, tab):
+def attention_fwd(tiles, q, k, v, kmeta, qmeta, tab):
     rows, width = q.shape
     span = kmeta.shape[0]
     nq, nc = rows // QB, TILES
@@ -173,7 +173,7 @@
         fwd_kernel,
         grid_spec=pltpu.PrefetchScalarGridSpec(
             num_scalar_prefetch=1, grid=(nq,),
-            in_specs=[block] + [hbm] * 6 + [full(span, 128), pl.BlockSpec((8, QB), lambda i, r: (0, i)), full(16, 160)],
+            in_specs=[block] + [hbm] * 2 + [full(span, 128), pl.BlockSpec((8, QB), lambda i, r: (0, i)), full(16, 160)],
             out_specs=[block, block, hbm],
             scratch_shapes=[
                 vm((span, width), BF16), vm((span, width), BF16),
@@ -186,7 +186,7 @@
         compiler_params=pltpu.CompilerParams(vmem_limit_bytes=56 * 2**20, dimension_semantics=("arbitrary",)),
         cost_estimate=pl.CostEstimate(flops=25 * 10**9, bytes_accessed=30 * 2**20, transcendentals=5 * 10**6),
         name="attention_forward",
-    )(tiles, q, *pieces, kmeta, qmeta, tab)
+    )(tiles, q, k, v, kmeta, qmeta, tab)
 
 
 def order_tables(ts, tx, ty):
@@ -195,8 +195,8 @@
     return jnp.concatenate([t[0::2], z, t[1::2], z], axis=0)
 
 
-def bwd_kernel(tiles, q_ref, dc_ref, ctx_ref, k_low, v_low, k_own, v_own, k_high, v_high, kmeta_ref, qmeta_ref, p_hbm,
-               dq_ref, low_ref, own_k, own_v, high_ref, dtab_ref,
+def bwd_kernel(tiles, q_ref, dc_ref, ctx_ref, k_hbm, v_hbm, kmeta_ref, qmeta_ref, p_hbm,
+               dq_ref, dk_hbm, dv_hbm, dtab_ref,
                keys, values, dk, dv, dq_t, b_scr, ds_scr, delta, qstack, cstack, pbuf, sems, in_sems):
     qb = pl.program_id(0)
     last = pl.num_programs(0) - 1
@@ -210,7 +210,7 @@
 
     @pl.when(qb == 0)
     def _():
-        copies = window_copies((k_low, v_low, k_own, v_own, k_high, v_high), keys, values, in_sems)
+        copies = window_copies(k_hbm, v_hbm, keys, values, in_sems)
         for copy in copies:
             copy.start()
         clear_tail(keys, values)
@@ -270,28 +270,26 @@
 
     @pl.when(qb == last)
     def _():
-        rows = own_k.shape[0]
-        width = dk.shape[1]
-        own = [
-            pltpu.make_async_copy(dk.at[pl.ds(rows, rows), :], own_k, in_sems.at[0]),
-            pltpu.make_async_copy(dv.at[pl.ds(rows, rows), :], own_v, in_sems.at[1]),
-        ]
-        for copy in own:
+        part = dk_hbm.shape[0] // 3
+        copies = []
+        for i in range(6):
+            src, dst, out = ((dk, keys, dk_hbm), (dv, values, dv_hbm))[i % 2]
+            start = i // 2 * part
+
+            def move(j, carry):
+                r = pl.multiple_of(start + j * 32, 32)
+                dst[pl.ds(r, 32), :] = src[pl.ds(r, 32), :].astype(BF16)
+                return carry
+
+            lax.fori_loop(0, part // 32, move, 0)
+            copy = pltpu.make_async_copy(dst.at[pl.ds(start, part), :], out.at[pl.ds(start, part), :], in_sems.at[i])
             copy.start()
-
-        def move(i, carry):
-            r = pl.multiple_of(i * 32, 32)
-            for src, col in ((dk, 0), (dv, width)):
-                low_ref[pl.ds(r, 32), col : col + width] = src[pl.ds(r, 32), :].astype(BF16)
-                high_ref[pl.ds(r, 32), col : col + width] = src[pl.ds(pl.multiple_of(2 * rows + r, 32), 32), :].astype(BF16)
-            return carry
-
-        lax.fori_loop(0, rows // 32, move, 0)
-        for copy in own:
+            copies.append(copy)
+        for copy in copies:
             copy.wait()
 
 
-def attention_bwd(tiles, q, dc, ctx, pieces, kmeta, qmeta, probs):
+def attention_bwd(tiles, q, dc, ctx, k, v, kmeta, qmeta, probs):
     rows, width = q.shape
     span = kmeta.shape[0]
     nq, nc = rows // QB, TILES
@@ -304,20 +302,19 @@
         bwd_kernel,
         grid_spec=pltpu.PrefetchScalarGridSpec(
             num_scalar_prefetch=1, grid=(nq,),
-            in_specs=[block] * 3 + [hbm] * 6 + [full(span, 128), pl.BlockSpec((8, QB), lambda i, r: (0, i)), hbm],
-            out_specs=[block, full(rows, 2 * width), hbm, hbm, full(rows, 2 * width), full(16, 160)],
+            in_specs=[block] * 3 + [hbm] * 2 + [full(span, 128), pl.BlockSpec((8, QB), lambda i, r: (0, i)), hbm],
+            out_specs=[block, hbm, hbm, full(16, 160)],
             scratch_shapes=[
                 vm((span, width), BF16), vm((span, width), BF16),
                 vm((span, width), F32), vm((span, width), F32), vm((width, QB), F32),
                 vm((3, KB, QB), F32), vm((16 * KB, QB), F32), vm((8, 2 * QB), F32),
                 vm((PAIRS, 2 * QB, 128), BF16), vm((PAIRS, 2 * QB, 128), BF16),
                 vm((2, PAIRS, KB, 2 * QB), BF16), pltpu.SemaphoreType.DMA((2,)), pltpu.SemaphoreType.DMA((6,))]),
-        out_shape=[shape((rows, width), BF16), shape((rows, 2 * width), BF16), shape((rows, width), F32), shape((rows, width), F32),
-                   shape((rows, 2 * width), BF16), shape((16, 160), F32)],
+        out_shape=[shape((rows, width), BF16), shape(k.shape, BF16), shape(k.shape, BF16), shape((16, 160), F32)],
         compiler_params=pltpu.CompilerParams(vmem_limit_bytes=56 * 2**20, dimension_semantics=("arbitrary",)),
         cost_estimate=pl.CostEstimate(flops=40 * 10**9, bytes_accessed=40 * 2**20, transcendentals=0),
         name="attention_backward",
-    )(tiles, q, dc, ctx, *pieces, kmeta, qmeta, probs)
+    )(tiles, q, dc, ctx, k, v, kmeta, qmeta, probs)
 
 
 def exchange_plan(n_seq, n_ffn, half):
@@ -330,8 +327,8 @@
     return [seq_bits + ffn_bits], half
 
 
-def sum_kernel(orders, length, a_ref, small_ref, unit_ref, out_ref, small_out, unit_out, work, core_in, slots, sums, small_in,
-               core_sems, core_back, send_sems, recv_sems, back_send, back_recv, small_send, small_recv, unit_in, unit_mid, unit_send, unit_recv):
+def sum_kernel(orders, length, a_ref, small_ref, out_ref, small_out, work, core_in, slots, sums, small_in,
+               core_sems, core_back, send_sems, recv_sems, back_send, back_recv, small_send, small_recv):
     seq, ffn = lax.axis_index("seq"), lax.axis_index("ffn")
     half = work.shape[0]
     streams = len(orders)
@@ -381,27 +378,6 @@
         axis, bit = peers[k]
         return remote(sums.at[k], small_in.at[k], small_send.at[k], small_recv.at[k], axis, bit)
     small_copy(0).start()
-    seq_peers = [peer for peer in peers if peer[0] == "seq"]
-
-    def unit_copy(k):
-        src = unit_ref if k == 0 else unit_mid.at[k - 1]
-        return remote(src, unit_in.at[k], unit_send.at[k], unit_recv.at[k], *seq_peers[k])
-
-    def unit_step(k):
-        unit_copy(k).wait_recv()
-
-        def body(i, carry):
-            rows = pl.ds(pl.multiple_of(i * 16, 16), 16)
-            src = unit_ref[rows, :] if k == 0 else unit_mid[k - 1, rows, :]
-            total = src.astype(F32) + unit_in[k, rows, :].astype(F32)
-            if k == len(seq_peers) - 1:
-                unit_out[rows, :] = total
-            else:
-                unit_mid[k, rows, :] = total.astype(BF16)
-            return carry
-        lax.fori_loop(0, unit_ref.shape[0] // 16, body, 0)
-        if k < len(seq_peers) - 1:
-            unit_copy(k + 1).start()
 
     lows = [s * length for s in range(streams)]
     sizes = [length] * streams
@@ -447,10 +423,6 @@
                 flying[s] = scatter(s, k + 1)
             else:
                 flying[s] = gather(s, k, lows, sizes, orders, remote, at, out_ref, core, half, back_send, back_recv)
-        if k == 0:
-            unit_copy(0).start()
-        elif k <= len(seq_peers):
-            unit_step(k - 1)
         small_copy(k).wait_recv()
         sums[k + 1] = sums[k] + small_in[k]
         small_copy(k + 1).start()
@@ -478,8 +450,6 @@
         copy.wait_send()
     for k in range(steps + 1):
         small_copy(k).wait_send()
-    for k in range(len(seq_peers)):
-        unit_copy(k).wait_send()
 
 
 def gather(s, k, lows, sizes, orders, remote, at, out_ref, core, half, back_send, back_recv):
@@ -490,7 +460,7 @@
     return copy
 
 
-def sum_everywhere(a, small, unit):
+def sum_everywhere(a, small):
     n_seq, n_ffn = lax.axis_size("seq"), lax.axis_size("ffn")
     grain = 16 * n_seq * n_ffn // 2
     rows, width = a.shape
@@ -501,23 +471,21 @@
     streams, steps = len(orders), len(orders[0])
     vm, dma = pltpu.VMEM, pltpu.SemaphoreType.DMA
     slot_rows = streams * (length - length // (1 << steps))
-    bits = n_seq.bit_length() - 1
-    out, small_out, unit_out = pl.pallas_call(
+    out, small_out = pl.pallas_call(
         functools.partial(sum_kernel, orders, length),
-        out_shape=[jax.ShapeDtypeStruct(a.shape, BF16), jax.ShapeDtypeStruct(small.shape, F32), jax.ShapeDtypeStruct(unit.shape, F32)],
-        in_specs=[pl.BlockSpec(memory_space=vm)] * 3,
-        out_specs=[pl.BlockSpec(memory_space=vm)] * 3,
+        out_shape=[jax.ShapeDtypeStruct(a.shape, BF16), jax.ShapeDtypeStruct(small.shape, F32)],
+        in_specs=[pl.BlockSpec(memory_space=vm)] * 2,
+        out_specs=[pl.BlockSpec(memory_space=vm)] * 2,
         scratch_shapes=[
             vm((half, width), BF16), vm((half, width), BF16), vm((slot_rows, width), BF16),
             vm((steps + 1,) + small.shape, F32), vm((steps + 1,) + small.shape, F32),
             dma((2 * streams,)), dma((2 * streams,)), dma((streams, steps)), dma((streams, steps)),
             dma((streams, steps)), dma((streams, steps)), dma((steps + 1,)), dma((steps + 1,)),
-            vm((bits,) + unit.shape, BF16), vm((bits,) + unit.shape, BF16), dma((bits,)), dma((bits,)),
         ],
         compiler_params=pltpu.CompilerParams(collective_id=0, has_side_effects=True, vmem_limit_bytes=48 * 2**20),
         name="sum_everywhere",
-    )(a, small, unit)
-    return out[:rows], small_out, unit_out
+    )(a, small)
+    return out[:rows], small_out
 
 
 UB = 512
@@ -537,51 +505,46 @@
     return lax.dot_general(a, b, (((0,), (0,)), ((), ())), preferred_element_type=F32)
 
 
-def ffn_up_kernel(normed_ref, up_ref, down_ref, active_ref, slope_ref, branch_ref):
-    @pl.when(pl.program_id(0) == 0)
-    def _():
-        branch_ref[...] = jnp.zeros_like(branch_ref)
-
+def ffn_up_kernel(normed_ref, up_ref, active_ref, slope_ref):
     rows = normed_ref.shape[0]
     size = rows // 2
     for r in range(0, rows, size):
         w = slice(r, r + size)
         act, slope = gelu_and_slope(nt(normed_ref[w, :], up_ref[...]))
-        act = act.astype(BF16)
-        active_ref[w, :] = act
+        active_ref[w, :] = act.astype(BF16)
         slope_ref[w, :] = slope.astype(BF16)
-        branch_ref[w, :] = branch_ref[w, :] + nn(act, down_ref[...])
-
-
-def ffn_up(normed, up, down):
+
+
+def ffn_up(normed, up):
     rows, wide = normed.shape
-    units, width = down.shape
+    units = up.shape[0]
     full = lambda *s: pl.BlockSpec(s, lambda i: (0,) * len(s))
     col = pl.BlockSpec((rows, UB), lambda i: (0, i))
     shape = jax.ShapeDtypeStruct
     return pl.pallas_call(
         ffn_up_kernel,
         grid=(units // UB,),
-        in_specs=[full(rows, wide), pl.BlockSpec((UB, wide), lambda i: (i, 0)), pl.BlockSpec((UB, width), lambda i: (i, 0))],
-        out_specs=[col, col, full(rows, width)],
-        out_shape=[shape((rows, units), BF16), shape((rows, units), BF16), shape((rows, width), F32)],
+        in_specs=[full(rows, wide), pl.BlockSpec((UB, wide), lambda i: (i, 0))],
+        out_specs=[col, col],
+        out_shape=[shape((rows, units), BF16), shape((rows, units), BF16)],
         compiler_params=pltpu.CompilerParams(vmem_limit_bytes=48 * 2**20, dimension_semantics=("arbitrary",)),
-        cost_estimate=pl.CostEstimate(flops=2 * rows * units * (wide + width), bytes_accessed=20 * 2**20, transcendentals=2 * rows * units),
+        cost_estimate=pl.CostEstimate(flops=2 * rows * units * wide, bytes_accessed=15 * 2**20, transcendentals=2 * rows * units),
         name="ffn_up",
-    )(normed, up, down)
-
-
-def ffn_back_kernel(grad_ref, normed_ref, up_ref, down_ref, active_ref, slope_ref, unit_ref, normed_grad_ref):
+    )(normed, up)
+
+
+def ffn_back_kernel(grad_ref, normed_ref, up_ref, down_ref, active_ref, slope_ref, unit_ref, bias_ref, normed_grad_ref):
     @pl.when(pl.program_id(0) == 0)
     def _():
         normed_grad_ref[...] = jnp.zeros_like(normed_grad_ref)
 
     grad = grad_ref[...]
-    wide = normed_ref.shape[1]
     width = grad.shape[1]
-    unit_ref[:, wide:] = tn(active_ref[...], grad).astype(BF16)
+    unit_ref[:, width:] = tn(active_ref[...], grad).astype(BF16)
     pre = (nt(grad, down_ref[...]) * slope_ref[...].astype(F32)).astype(BF16)
-    unit_ref[:, :wide] = tn(pre, normed_ref[...]).astype(BF16)
+    up_grad = tn(pre, normed_ref[...])
+    unit_ref[:, :width] = up_grad[:, :width].astype(BF16)
+    bias_ref[...] = up_grad[:, width:]
     normed_grad_ref[...] = normed_grad_ref[...] + nn(pre, up_ref[:, :width])
 
 
@@ -596,8 +559,8 @@
         ffn_back_kernel,
         grid=(units // UB,),
         in_specs=[full(rows, width), full(rows, wide), row(wide), row(width), col, col],
-        out_specs=[row(wide + width), full(rows, width)],
-        out_shape=[shape((units, wide + width), BF16), shape((rows, width), F32)],
+        out_specs=[row(2 * width), row(wide - width), full(rows, width)],
+        out_shape=[shape((units, 2 * width), BF16), shape((units, wide - width), F32), shape((rows, width), F32)],
         compiler_params=pltpu.CompilerParams(vmem_limit_bytes=48 * 2**20, dimension_semantics=("arbitrary",)),
         cost_estimate=pl.CostEstimate(flops=4 * rows * units * (wide + width), bytes_accessed=30 * 2**20, transcendentals=0),
         name="ffn_back",
@@ -659,14 +622,16 @@
     doc_ends = jnp.cumsum(doc_lengths[0])
 
     n_ffn = lax.axis_size("ffn")
+    n_seq = lax.axis_size("seq")
     up = [(i, i + 1) for i in range(n_ffn - 1)]
     hidden_low = lax.ppermute(hidden_in, "ffn", up)
     hidden_high = lax.ppermute(hidden_in, "ffn", [(j, i) for i, j in up])
 
     units = b_up.shape[0]
     up_ext = jnp.concatenate([w_up.T, b_up[:, None], jnp.zeros((units, 127), BF16)], axis=1)
+    later, up_ext = lax.optimization_barrier((w_down, up_ext))
     up_all = lax.all_gather(up_ext, "ffn", axis=0, tiled=True)
-    down_all = lax.all_gather(w_down, "ffn", axis=0, tiled=True)
+    down_all = lax.all_gather(later, "ffn", axis=0, tiled=True)
 
     window_rows = first_row - rows + jnp.arange(span, dtype=jnp.int32)
     doc_ids, places = layout(window_rows, doc_ends)
@@ -690,12 +655,11 @@
     tables = order_tables(table_seq, table_x, table_y)
 
     query = ((jnp.dot(hidden_in, w_query, preferred_element_type=F32) + b_query) * 0.125).astype(BF16)
-    pieces = []
-    for part in (hidden_low, hidden_in, hidden_high):
-        pieces.append(jnp.dot(part, w_key, preferred_element_type=F32).astype(BF16))
-        pieces.append((jnp.dot(part, w_value, preferred_element_type=F32) + b_value).astype(BF16))
-
-    context, inv, probs = attention_fwd(tiles, query, pieces, kmeta, qmeta, tables)
+    window = jnp.concatenate([hidden_low, hidden_in, hidden_high], axis=0)
+    key = jnp.dot(window, w_key, preferred_element_type=F32).astype(BF16)
+    value = (jnp.dot(window, w_value, preferred_element_type=F32) + b_value).astype(BF16)
+
+    context, inv, probs = attention_fwd(tiles, query, key, value, kmeta, qmeta, tables)
     context_low = context.astype(BF16)
     attn = jnp.dot(context_low, w_out, preferred_element_type=F32) + b_out
     inputs = hidden_in.astype(F32)
@@ -705,14 +669,15 @@
     normed_low = normed.astype(BF16)
     ones = jnp.concatenate([jnp.ones((rows, 1), BF16), jnp.zeros((rows, 127), BF16)], axis=1)
     normed_ext = jnp.concatenate([normed_low, ones], axis=1)
-    active, slope, branch = ffn_up(normed_ext, up_all, down_all)
+    active, slope = ffn_up(normed_ext, up_all)
+    branch = jnp.dot(active, down_all, preferred_element_type=F32)
     hidden_out, out_pull = jax.vjp(
         layer_norm, normed + (branch + b_down), gain_out.astype(F32), shift_out.astype(F32)
     )
     mid_grad, grad_gain_out, grad_shift_out = out_pull(out_grad.astype(F32))
     branch_grad = mid_grad.astype(BF16)
     grad_b_down = jnp.sum(branch_grad.astype(F32), axis=0)
-    unit_part, branch_back = ffn_back(branch_grad, normed_ext, up_all, down_all, active, slope)
+    unit_part, bias_part, branch_back = ffn_back(branch_grad, normed_ext, up_all, down_all, active, slope)
     unit_grad = lax.psum_scatter(unit_part, "ffn", scatter_dimension=0, tiled=True)
     normed_grad = mid_grad + branch_back
     mid1_grad, grad_gain_attn, grad_shift_attn = norm_pull(normed_grad)
@@ -720,21 +685,19 @@
     grad_b_out = jnp.sum(attn_grad.astype(F32), axis=0)
     grad_w_out = jnp.dot(context_low.T, attn_grad, preferred_element_type=F32)
     scaled = (nt(attn_grad, w_out) * inv).astype(BF16)
-    query_grad, low_terms, own_key, own_value, high_terms, table_sum = attention_bwd(
-        tiles, query, scaled, context, pieces, kmeta, qmeta, probs
-    )
-    from_below = from_behind(high_terms, "ffn", 1).astype(F32)
-    from_above = from_behind(low_terms, "ffn", -1).astype(F32)
-    key_grad = (own_key + from_below[:, :width] + from_above[:, :width]).astype(BF16)
-    value_grad = (own_value + from_below[:, width:] + from_above[:, width:]).astype(BF16)
-    hidden_grad = (
-        mid1_grad + nt(query_grad, w_query) * 0.125 + nt(key_grad, w_key) + nt(value_grad, w_value)
-    )
+    query_grad, key_grad, value_grad, table_sum = attention_bwd(
+        tiles, query, scaled, context, key, value, kmeta, qmeta, probs
+    )
+    def through(part):
+        return nt(key_grad[part], w_key) + nt(value_grad[part], w_value)
+
+    from_below = from_behind(through(slice(2 * rows, span)).astype(BF16), "ffn", 1)
+    from_above = from_behind(through(slice(0, rows)).astype(BF16), "ffn", -1)
     big = jnp.concatenate(
         [
             (jnp.dot(hidden_in.T, query_grad, preferred_element_type=F32) * 0.125).astype(BF16),
-            jnp.dot(hidden_in.T, key_grad, preferred_element_type=F32).astype(BF16),
-            jnp.dot(hidden_in.T, value_grad, preferred_element_type=F32).astype(BF16),
+            jnp.dot(window.T, key_grad, preferred_element_type=F32).astype(BF16),
+            jnp.dot(window.T, value_grad, preferred_element_type=F32).astype(BF16),
             grad_w_out.astype(BF16),
         ],
         axis=0,
@@ -752,11 +715,22 @@
         ]
     )
     levels = table_sum.shape[1]
-    small = jnp.concatenate([small, jnp.pad(table_sum, ((0, 0), (0, width - levels)))], axis=0)
-    big, small, unit_grad = sum_everywhere(big, small, unit_grad)
+    small = jnp.concatenate(
+        [small, jnp.pad(table_sum, ((0, 0), (0, width - levels))), bias_part[:, 0].reshape(-1, width)], axis=0
+    )
+    big, small = sum_everywhere(big, small)
+    big, small, unit_grad, query_grad, key_grad, value_grad, from_below, from_above = lax.optimization_barrier(
+        (big, small, unit_grad, query_grad, key_grad, value_grad, from_below, from_above)
+    )
+    for b in range(n_seq.bit_length() - 1):
+        unit_grad = unit_grad + lax.ppermute(unit_grad, "seq", [(i, i ^ (1 << b)) for i in range(n_seq)])
+    unit_grad = unit_grad.astype(F32)
+    hidden_grad = (
+        mid1_grad + nt(query_grad, w_query) * 0.125 + through(own) + from_below.astype(F32) + from_above.astype(F32)
+    )
     grad_w_up = unit_grad[:, :width].T
-    grad_b_up = unit_grad[:, width]
-    grad_w_down = unit_grad[:, width + 128 :]
+    grad_w_down = unit_grad[:, width:]
+    grad_b_up = lax.dynamic_slice_in_dim(small[24:].reshape(-1), lax.axis_index("ffn") * units, units)
     grads = [big[i * width : (i + 1) * width].astype(F32) for i in range(4)]
     vec = [small[i] for i in range(8)]
     table_all = jnp.stack([small[8 + h // 2 + 8 * (h % 2), :levels] for h in range(heads)], axis=1)

time: 418 us -> 393 us (0.940); the launches traced: 416 us -> 386 us
  waiting for transfers between devices: 76.7 us -> 36.3 us
  Pallas kernels: 224 us -> 203 us
  starting transfers between devices: 8.13 us -> 24.2 us
  local copies, waits for them, and re-layouts: 18.5 us -> 23.9 us
  matrix products: 39.2 us -> 44.4 us
  other arithmetic: 34.3 us -> 38.5 us
    reduce_scatter x1, waiting for transfers between devices: 42.8 us -> 0.01 us  [on_device(): lax.psum_scatter(unit_part, 'ffn', scatter_dimension=0, tiled=True)]
    all_gather x1, waiting for transfers between devices: 0.02 us -> 35.5 us  [on_device(): down_all = lax.all_gather(later, 'ffn', axis=0, tiled=True)]
    all_gather x1, waiting for transfers between devices: 33.8 us -> 0.02 us  [on_device(): up_all = lax.all_gather(up_ext, 'ffn', axis=0, tiled=True)]
    pallas_call x1, Pallas kernels: 64 us -> 48.1 us  [attention_bwd(): pl.pallas_call(bwd_kernel, grid_spec=pltpu.PrefetchScalarGridSpec(num_sca...]
    ppermute x2, starting transfers between devices: 2.71 us -> 18.5 us  [from_behind(): return lax.ppermute(x, axis, pairs)]
    pallas_call x1, Pallas kernels: 43.6 us -> 32.7 us  [attention_fwd(): pl.pallas_call(fwd_kernel, grid_spec=pltpu.PrefetchScalarGridSpec(num_sca...]
    pallas_call x1, Pallas kernels: 78.1 us -> 87.1 us  [sum_everywhere(): pl.pallas_call(functools.partial(sum_kernel, orders, length), out_shape=[...]
    dot_general x4 -> x8, matrix products: 7.54 us -> 14.8 us  [nt(): lax.dot_general(a, b, (((1,), (1,)), ((), ())), preferred_element_type=F32)]
  transfers between devices with their start and end apart: 7 -> 8, of which waited for: 2 -> 1; matrix products, arithmetic and copies ran while one was open for 16% -> 20% of each run, Pallas kernels for 26% -> 47%
where the time goes in v2:
time: 393 us; the launch traced here: 386 us
  Pallas kernels  203 us (52%)
  matrix products  44.4 us (11%)
  other arithmetic  38.5 us (10%)
  waiting for transfers between devices  36.3 us (9%)
  starting transfers between devices  24.2 us (6%)
  local copies, waits for them, and re-layouts  23.9 us (6%)
  between operations  15 us (4%)
    pallas_call x1, Pallas kernels, sum_everywhere(): pl.pallas_call(functools.partial(sum_kernel, orders, length), out_shape=[...  87.1 us
    pallas_call x1, Pallas kernels, attention_bwd(): pl.pallas_call(bwd_kernel, grid_spec=pltpu.PrefetchScalarGridSpec(num_sca...  48.1 us
    all_gather x1, waiting for transfers between devices, on_device(): down_all = lax.all_gather(later, 'ffn', axis=0, tiled=True)  35.5 us
    pallas_call x1, Pallas kernels, attention_fwd(): pl.pallas_call(fwd_kernel, grid_spec=pltpu.PrefetchScalarGridSpec(num_sca...  32.7 us
    pallas_call x1, Pallas kernels, ffn_back(): pl.pallas_call(ffn_back_kernel, grid=(units // UB,), in_specs=[full(rows,...  21.6 us
    ppermute x2, starting transfers between devices, from_behind(): return lax.ppermute(x, axis, pairs)  18.5 us
    dot_general x8, matrix products, nt(): lax.dot_general(a, b, (((1,), (1,)), ((), ())), preferred_element_type=F32)  14.8 us
    unnamed x65, local copies, waits for them, and re-layouts  14.2 us
  transfers between devices with their start and end apart: 8, of which 1 were waited for; matrix products, arithmetic and copies ran while one was open for 20% of the time, Pallas kernels for 47%

profile of v2, /device:TPU:0, one launch (start us, length us, event | category | flops | bytes accessed | tf_op | source)
XLA Modules:
  0.0 385.6 jit_solution(99361636176363935)
XLA Ops:
  7.3 0.8 copy.72
  8.0 0.7 broadcast_in_dim.136
  8.9 1.8 maximum_maximum_fusion.1
  10.7 0.7 all-gather.5.cloned.1.call-update
  11.5 1.4 collective-permute-start.1
  12.9 4.0 %collective-permute-start = (bf16[640,768]{1,0:T(8,128)(2,1)}, bf16[640,768]{1,0:T(8,128)(2,1)}, u32[]{:S(2)}, u32[]{:S(2)}) collective-permute-start(bf16[640,768]{1,0:T(8,128)(2,1)} %param.26), channel_id=1, source_target_pairs={{0,1},{1,2},{2,3},{3,4},{4,5},{5,6},{6,7},{7,8},{8,9},{9,10},{10,1... | collective-permute-start | bytes 2949128 | tf_op jit(solution)/shard_map/ppermute | solution.py:627
  17.0 0.8 maximum_bitcast_fusion
  17.8 0.7 copy.62
  19.1 0.8 fusion.27
  20.0 0.7 convert_element_type.132
  20.7 0.7 convert_element_type.133
  21.4 0.7 convert_element_type.136
  22.1 0.7 convert_element_type.123
  22.8 0.7 convert_element_type.126
  23.4 0.7 convert_element_type.131
  24.1 0.7 convert_element_type.135
  24.8 0.7 convert_element_type.137
  27.7 1.1 pad.14.kmeta_ref
  30.2 1.9 multiply_convert_fusion.2.q_ref
  32.1 1.3 constant_dynamic-update-slice_fusion.2
  33.4 1.3 constant_dynamic-update-slice_fusion
  34.7 4.1 %convolution_convert_fusion.k_hbm = bf16[1920,768]{1,0:T(8,128)(2,1)} fusion(bf16[1920,768]{1,0:T(8,128)(2,1)S(1)} %constant_dynamic-update-slice_fusion, bf16[768,768]{1,0:T(8,128)(2,1)S(1)} %copy-done), kind=kOutput, calls=%fused_computation.3 | convolution fusion | flops 2266398720 | bytes 7077888 | tf_op jit(solution)/shard_map/dot_general | solution.py:659
  38.8 4.1 %add_convert_fusion.v_hbm = bf16[1920,768]{1,0:T(8,128)(2,1)} fusion(bf16[1920,768]{1,0:T(8,128)(2,1)S(1)} %constant_dynamic-update-slice_fusion, bf16[768,768]{1,0:T(8,128)(2,1)S(1)} %copy-done.23, f32[768]{0:T(1024)S(1)} %convert_element_type.126), kind=kOutput, calls=%fused_computation.1 | convolution fusion | flops 2267873280 | bytes 7080960 | tf_op jit(solution)/shard_map/dot_general | solution.py:660
  43.0 32.7 %attention_forward.1 = (f32[640,768]{1,0:T(8,128)}, f32[640,768]{1,0:T(8,128)}, bf16[5,12,6,128,256]{4,3,2,1,0:T(8,128)(2,1)}) custom-call(s32[5,25]{1,0:T(8,128)} %pad_add_fusion.tiles, bf16[640,768]{1,0:T(8,128)(2,1)} %multiply_convert_fusion.2.q_ref, bf16[1920,768]{1,0:T(8,128)(2,1)} %convolution_convert_fusion.k_hbm, ...), custom_call_target="tpu_custom_call" | custom-call | flops 24999999488 | bytes 31457280 | tf_op jit(solution)/shard_map/attention_forward/pallas_call | solution.py:172
  75.7 2.6 fusion.43
  79.8 13.9 %ffn_up.1 = (bf16[640,3072]{1,0:T(8,128)(2,1)S(1)}, bf16[640,3072]{1,0:T(8,128)(2,1)}) custom-call(bf16[640,896]{1,0:T(8,128)(2,1)S(1)} %maximum_maximum_fusion.normed_ref, bf16[3072,896]{1,0:T(8,128)(2,1)} %all-gather.3.cloned.1.call-done.up_ref), custom_call_target="tpu_custom_call" | custom-call | flops 3523215360 | bytes 15728640 | tf_op jit(solution)/shard_map/ffn_up/pallas_call | solution.py:524
  93.7 1.9 copy-done.6
  95.6 35.5 %all-gather.5.cloned.1.call-done.down_ref = bf16[3072,768]{1,0:T(8,128)(2,1)} async-done(((bf16[192,768]{1,0:T(8,128)(2,1)}), bf16[3072,768]{1,0:T(8,128)(2,1)}) %all-gather.5.cloned.1.call-update) | async-done | bytes 4718608 | tf_op jit(solution)/shard_map/all_gather | solution.py:634
  131.1 7.5 %fusion.44 = (f32[640]{0:T(1024)S(1)}, f32[640,768]{1,0:T(8,128)S(1)}) fusion(f32[768]{0:T(1024)S(1)} %convert_element_type.135, bf16[640,3072]{1,0:T(8,128)(2,1)} %copy-done.6, bf16[3072,768]{1,0:T(8,128)(2,1)} %all-gather.5.cloned.1.call-done.down_ref, f32[768]{0:T(1024)S(1)} %convert_element_type.133, f32[768]{0:T(1024)S(1)} %convert_element_type.132, ...), kind=kOutput, calls=%fused_computation.151 | convolution fusion | flops 3023339008 | bytes 12599808 | tf_op jit(solution)/shard_map/dot_general | solution.py:673
  139.0 0.8 copy-done.11
  139.8 0.9 fusion.3
  140.7 2.1 fusion.37
  143.1 1.0 copy-done.8
  144.1 0.7 copy-done.5
  144.8 21.6 %ffn_back.1 = (bf16[3072,1536]{1,0:T(8,128)(2,1)}, f32[3072,128]{1,0:T(8,128)S(1)}, f32[640,768]{1,0:T(8,128)S(1)}) custom-call(bf16[640,768]{1,0:T(8,128)(2,1)S(1)} %get-tuple-element.101.grad_ref, bf16[640,896]{1,0:T(8,128)(2,1)S(1)} %copy-done.5, bf16[3072,896]{1,0:T(8,128)(2,1)} %all-gather.3.cloned.1.call-done.up_ref, ...), custom_call_target="tpu_custom_call" | custom-call | flops 13086228480 | bytes 31457280 | tf_op jit(solution)/shard_map/ffn_back/pallas_call | solution.py:558
  166.4 1.1 copy-done.2
  167.6 4.4 %multiply_reduce_fusion = (f32[768]{0:T(1024)S(1)}, f32[640]{0:T(1024)S(1)}, f32[768]{0:T(1024)S(1)}, f32[640,768]{1,0:T(8,128)}) fusion(f32[640,768]{1,0:T(8,128)} %copy-done.7, f32[640]{0:T(1024)S(1)} %fusion.34, f32[640]{0:T(1024)S(1)} %broadcast_multiply_fusion.2, f32[768]{0:T(1024)S(1)} %convert_element_type.132, f32[640,768]{1,0:T(8,128)S(1)} %get-tuple-element.61, ...), kind=kLoop, calls=%fused_computation.18 | loop fusion | flops 4913024 | bytes 7883776 | tf_op jit(solution)/shard_map/transpose(jvp())/reduce_sum | solution.py:579
  172.5 3.4 fusion.36
  176.2 1.8 copy-done.14
  178.0 1.9 multiply_convert_fusion.1.dc_ref
  179.9 48.1 %attention_backward.1 = (bf16[640,768]{1,0:T(8,128)(2,1)}, bf16[1920,768]{1,0:T(8,128)(2,1)}, bf16[1920,768]{1,0:T(8,128)(2,1)}, f32[16,160]{1,0:T(8,128)}) custom-call(s32[5,25]{1,0:T(8,128)} %pad_add_fusion.tiles, bf16[640,768]{1,0:T(8,128)(2,1)} %multiply_convert_fusion.2.q_ref, bf16[640,768]{1,0:T(8,128)(2,1)} %multiply_convert_fusion.1.dc_ref, ...), custom_call_target="tpu_custom_call" | custom-call | flops 40000000000 | bytes 41943040 | tf_op jit(solution)/shard_map/attention_backward/pallas_call | solution.py:301
  228.1 1.5 convert_reduce_fusion.4
  229.6 2.3 convert_reduce_fusion
  232.0 1.0 fusion.11
  233.0 0.9 copy-done.12
  234.2 1.9 add_convert_fusion.1
  236.1 1.5 collective-permute-start.3
  237.6 1.0 fusion.14
  238.6 1.9 add_convert_fusion.2
  240.5 17.0 %collective-permute-start.2 = (bf16[640,768]{1,0:T(8,128)(2,1)}, bf16[640,768]{1,0:T(8,128)(2,1)}, u32[]{:S(2)}, u32[]{:S(2)}) collective-permute-start(bf16[640,768]{1,0:T(8,128)(2,1)} %add_convert_fusion.2), channel_id=1, source_target_pairs={{0,1},{1,2},{2,3},{3,4},{4,5},{5,6},{6,7},{7,8},{8,9},{9,10},{10,1... | collective-permute-start | bytes 2949128 | tf_op jit(solution)/shard_map/ppermute | solution.py:573
  257.6 2.8 fusion.5
  260.4 1.2 convolution_convert_fusion.3
  261.6 0.8 copy-done.20
  262.4 2.7 convolution_convert_fusion.2
  265.2 2.8 convolution_convert_fusion.1
  267.9 2.8 pad_maximum_fusion.a_ref
  270.8 87.1 %sum_everywhere.1 = (bf16[3072,768]{1,0:T(8,128)(2,1)S(1)}, f32[28,768]{1,0:T(8,128)S(1)}) custom-call(bf16[3072,768]{1,0:T(8,128)(2,1)} %pad_maximum_fusion.a_ref, f32[28,768]{1,0:T(8,128)S(1)} %concatenate.49.small_ref), custom_call_target="tpu_custom_call" | custom-call | tf_op jit(solution)/shard_map/sum_everywhere/pallas_call | solution.py:474
  357.8 2.1 copy-done.1
  361.4 2.7 fusion.45
  364.1 2.3 fusion.8
  366.4 2.2 fusion.6
  368.6 3.8 slice_convert_fusion
  373.8 3.6 convert_add_fusion
  377.5 1.1 fusion.41
  (146 shorter events, 10.7 us)
Async XLA Ops:
  7.2 27.5 %copy-start = (bf16[768,768]{1,0:T(8,128)(2,1)S(1)}, bf16[768,768]{1,0:T(8,128)(2,1)}, u32[]{:S(2)}) copy-start(bf16[768,768]{1,0:T(8,128)(2,1)} %param.33) | copy-start | bytes 3538948
  7.2 72.6 %all-gather.3.cloned.1.call-start = ((), (), s32[]{:S(2)}) async-start(), calls=%async_computation.1 | async-start | bytes 5849088 | tf_op jit(solution)/shard_map/all_gather | solution.py:633
  10.6 120.5 %all-gather.5.cloned.1.call-start = ((), (), s32[]{:S(2)}) async-start(), calls=%async_computation.2 | async-start | bytes 5013504 | tf_op jit(solution)/shard_map/all_gather | solution.py:634
  11.4 18.8 %copy-start.17 = (bf16[640,768]{1,0:T(8,128)(2,1)S(1)}, bf16[640,768]{1,0:T(8,128)(2,1)}, u32[]{:S(2)}) copy-start(bf16[640,768]{1,0:T(8,128)(2,1)} %param.26) | copy-start | bytes 2949124
  11.4 348.5 %reduce-scatter.2.cloned.1.call-start = ((), (), s32[]{:S(2)}) async-start(), calls=%async_computation.3 | async-start | bytes 10027008 | tf_op jit(solution)/shard_map/reduce_scatter | solution.py:681
  11.5 22.0 %collective-permute-start.1 = (bf16[640,768]{1,0:T(8,128)(2,1)}, bf16[640,768]{1,0:T(8,128)(2,1)}, u32[]{:S(2)}, u32[]{:S(2)}) collective-permute-start(bf16[640,768]{1,0:T(8,128)(2,1)} %param.26), channel_id=1, source_target_pairs={{1,0},{2,1},{3,2},{4,3},{5,4},{6,5},{7,6},{8,7},{9,8},{10,9},{11,1... | collective-permute-start | bytes 2949128 | tf_op jit(solution)/shard_map/ppermute | solution.py:628
  12.9 19.2 %collective-permute-start = (bf16[640,768]{1,0:T(8,128)(2,1)}, bf16[640,768]{1,0:T(8,128)(2,1)}, u32[]{:S(2)}, u32[]{:S(2)}) collective-permute-start(bf16[640,768]{1,0:T(8,128)(2,1)} %param.26), channel_id=1, source_target_pairs={{0,1},{1,2},{2,3},{3,4},{4,5},{5,6},{6,7},{7,8},{8,9},{9,10},{10,1... | collective-permute-start | bytes 2949128 | tf_op jit(solution)/shard_map/ppermute | solution.py:627
  27.0 3.1 copy-start.22
  34.7 4.1 %copy-start.19 = (bf16[1920,768]{1,0:T(8,128)(2,1)}, bf16[1920,768]{1,0:T(8,128)(2,1)S(1)}, u32[]{:S(2)}) copy-start(bf16[1920,768]{1,0:T(8,128)(2,1)S(1)} %constant_dynamic-update-slice_fusion) | copy-start | bytes 8847364
  34.7 4.1 %copy-start.23 = (bf16[768,768]{1,0:T(8,128)(2,1)S(1)}, bf16[768,768]{1,0:T(8,128)(2,1)}, u32[]{:S(2)}) copy-start(bf16[768,768]{1,0:T(8,128)(2,1)} %param.34) | copy-start | bytes 3538948
  43.0 32.7 %copy-start.15 = (bf16[768,768]{1,0:T(8,128)(2,1)S(1)}, bf16[768,768]{1,0:T(8,128)(2,1)}, u32[]{:S(2)}) copy-start(bf16[768,768]{1,0:T(8,128)(2,1)} %param.36) | copy-start | bytes 3538948
  78.3 1.3 copy-start.7
  79.8 13.9 %copy-start.4 = (bf16[640,896]{1,0:T(8,128)(2,1)}, bf16[640,896]{1,0:T(8,128)(2,1)S(1)}, u32[]{:S(2)}) copy-start(bf16[640,896]{1,0:T(8,128)(2,1)S(1)} %maximum_maximum_fusion.normed_ref) | copy-start | bytes 3440644
  93.7 1.9 copy-start.6
  138.6 1.2 copy-start.11
  142.8 1.3 copy-start.8
  142.8 2.0 copy-start.5
  166.4 1.1 copy-start.2
  167.6 4.4 %copy-start.3 = (f32[3072,128]{1,0:T(8,128)S(1)}, f32[3072,128]{1,0:T(8,128)}, u32[]{:S(2)}) copy-start(f32[3072,128]{1,0:T(8,128)} %copy-done.2) | copy-start | bytes 4718596
  172.5 3.7 copy-start.16
  175.9 2.1 copy-start.14
  176.2 3.8 copy-start.9
  228.1 3.9 %copy-start.21 = (f32[16,160]{1,0:T(8,128)S(1)}, f32[16,160]{1,0:T(8,128)}, u32[]{:S(2)}) copy-start(f32[16,160]{1,0:T(8,128)} %get-tuple-element.67) | copy-start | bytes 30724
  228.1 3.9 %copy-start.27 = (bf16[1920,768]{1,0:T(8,128)(2,1)S(1)}, bf16[1920,768]{1,0:T(8,128)(2,1)}, u32[]{:S(2)}) copy-start(bf16[1920,768]{1,0:T(8,128)(2,1)} %get-tuple-element.73) | copy-start | bytes 8847364
  232.0 1.8 copy-start.12
  232.0 2.2 copy-start.24
  236.1 123.9 %collective-permute-start.3 = (bf16[640,768]{1,0:T(8,128)(2,1)}, bf16[640,768]{1,0:T(8,128)(2,1)}, u32[]{:S(2)}, u32[]{:S(2)}) collective-permute-start(bf16[640,768]{1,0:T(8,128)(2,1)} %add_convert_fusion.1), channel_id=1, source_target_pairs={{1,0},{2,1},{3,2},{4,3},{5,4},{6,5},{7,6},{8,7},{9,8},{10,9},{11,1... | collective-permute-start | bytes 2949128 | tf_op jit(solution)/shard_map/ppermute | solution.py:573
  240.5 119.4 %collective-permute-start.2 = (bf16[640,768]{1,0:T(8,128)(2,1)}, bf16[640,768]{1,0:T(8,128)(2,1)}, u32[]{:S(2)}, u32[]{:S(2)}) collective-permute-start(bf16[640,768]{1,0:T(8,128)(2,1)} %add_convert_fusion.2), channel_id=1, source_target_pairs={{0,1},{1,2},{2,3},{3,4},{4,5},{5,6},{6,7},{7,8},{8,9},{9,10},{10,1... | collective-permute-start | bytes 2949128 | tf_op jit(solution)/shard_map/ppermute | solution.py:573
  257.6 2.8 copy-start.10
  257.6 2.8 copy-start.26
  257.6 4.0 %copy-start.28 = (bf16[1920,768]{1,0:T(8,128)(2,1)S(1)}, bf16[1920,768]{1,0:T(8,128)(2,1)}, u32[]{:S(2)}) copy-start(bf16[1920,768]{1,0:T(8,128)(2,1)} %get-tuple-element.73) | copy-start | bytes 8847364
  260.4 2.0 copy-start.20
  262.4 2.7 copy-start.13
  357.8 2.1 copy-start.1
  361.3 16.0 %collective-permute-start.4 = (bf16[192,1536]{1,0:T(8,128)(2,1)}, bf16[192,1536]{1,0:T(8,128)(2,1)S(1)}, u32[]{:S(2)}, u32[]{:S(2)}) collective-permute-start(bf16[192,1536]{1,0:T(8,128)(2,1)} %reduce-scatter.2.cloned.1.call-done), channel_id=1, source_target_pairs={{0,16},{16,0},{1,17},{17,1},{2,18},{18,2},{3,19},{19,3},{4,20},{20... | collective-permute-start | bytes 1769480 | tf_op jit(solution)/shard_map/ppermute | solution.py:726
  361.4 7.2 %slice-start = ((s8[4718592]{0:T(1024)(128)(4,1)}), s8[4194304]{0:T(1024)(128)(4,1)S(1)}, s32[]{:S(2)}) async-start(s8[4718592]{0:T(1024)(128)(4,1)} %bitcast.61), calls=%async_computation.4 | async-start | bytes 8388608
  364.1 2.3 copy-start.25
  364.1 4.5 %slice-start.1 = ((s8[4718592]{0:T(1024)(128)(4,1)}), s8[524288]{0:T(1024)(128)(4,1)S(1)}, s32[]{:S(2)}) async-start(s8[4718592]{0:T(1024)(128)(4,1)} %bitcast.61), calls=%async_computation.5 | async-start | bytes 1048576
  373.8 3.6 copy-start.18
Sparse Core Ops, SparseCore 0:
  10.9 65.9 all-gather.2
  79.1 51.9 all-gather.4
  167.7 115.5 reduce-scatter.1

commit v3 on v2

--- a/solution.py
+++ b/solution.py
@@ -62,11 +62,17 @@
         stack[p, QB : 2 * QB, :] = jnp.where(lane < 64, 0.0, x).astype(BF16)
 
 
+PARTS = 8
+
+
 def window_copies(k_hbm, v_hbm, keys, values, sems):
-    rows = k_hbm.shape[0]
+    part = k_hbm.shape[0] // PARTS
     return [
-        pltpu.make_async_copy(k_hbm, keys.at[pl.ds(0, rows), :], sems.at[0]),
-        pltpu.make_async_copy(v_hbm, values.at[pl.ds(0, rows), :], sems.at[1]),
+        pltpu.make_async_copy(
+            (k_hbm, v_hbm)[j].at[pl.ds(i * part, part), :], (keys, values)[j].at[pl.ds(i * part, part), :], sems.at[2 * i + j]
+        )
+        for i in range(PARTS)
+        for j in range(2)
     ]
 
 
@@ -180,7 +186,7 @@
                 vm((nc, PAIRS, KB, 2 * QB), F32), vm((3, KB, QB), F32), vm((16 * KB, QB), F32),
                 vm((PAIRS, 2 * QB, 128), BF16), vm((width, QB), F32), vm((PAIRS, 8, 2 * QB), F32),
                 vm((PAIRS, 8, 2 * QB), F32), vm((2, PAIRS, KB, 2 * QB), BF16),
-                pltpu.SemaphoreType.DMA((2,)), pltpu.SemaphoreType.DMA((6,))]),
+                pltpu.SemaphoreType.DMA((2,)), pltpu.SemaphoreType.DMA((2 * PARTS,))]),
         out_shape=[jax.ShapeDtypeStruct((rows, width), F32), jax.ShapeDtypeStruct((rows, width), F32),
                    jax.ShapeDtypeStruct((nq, nc, PAIRS, KB, 2 * QB), BF16)],
         compiler_params=pltpu.CompilerParams(vmem_limit_bytes=56 * 2**20, dimension_semantics=("arbitrary",)),
@@ -202,14 +208,16 @@
     last = pl.num_programs(0) - 1
     count = tiles[qb, 0]
 
-    def pcopy(c):
-        slot = lax.rem(c, 2)
-        return pltpu.make_async_copy(p_hbm.at[qb, c], pbuf.at[slot], sems.at[slot])
-
-    pcopy(0).start()
+    before = jnp.int32(0)
+    for b in range(dk.shape[0] // (3 * QB)):
+        before = before + jnp.where(b < qb, tiles[b, 0], 0)
+
+    def pcopy(block, c, slot):
+        return pltpu.make_async_copy(p_hbm.at[block, c], pbuf.at[slot], sems.at[slot])
 
     @pl.when(qb == 0)
     def _():
+        pcopy(0, 0, 0).start()
         copies = window_copies(k_hbm, v_hbm, keys, values, in_sems)
         for copy in copies:
             copy.start()
@@ -232,14 +240,18 @@
 
     def tile(c, carry):
         base, doc = tile_of(tiles, qb, c)
-        slot = lax.rem(c, 2)
-        put_buckets(b_scr, kmeta_ref[pl.ds(base, KB), :], qmeta_ref[...], doc)
+        slot = lax.rem(before + c, 2)
 
         @pl.when(c + 1 < count)
         def _():
-            pcopy(c + 1).start()
-
-        pcopy(c).wait()
+            pcopy(qb, c + 1, 1 - slot).start()
+
+        @pl.when((c + 1 == count) & (qb < last))
+        def _():
+            pcopy(qb + 1, 0, 1 - slot).start()
+
+        put_buckets(b_scr, kmeta_ref[pl.ds(base, KB), :], qmeta_ref[...], doc)
+        pcopy(qb, c, slot).wait()
         for p in range(PAIRS):
             w = slice(128 * p, 128 * p + 128)
             dp = nt(values[pl.ds(base, KB), w], cstack[p])
@@ -270,18 +282,18 @@
 
     @pl.when(qb == last)
     def _():
-        part = dk_hbm.shape[0] // 3
+        part = dk_hbm.shape[0] // PARTS
         copies = []
-        for i in range(6):
+        for i in range(2 * PARTS):
             src, dst, out = ((dk, keys, dk_hbm), (dv, values, dv_hbm))[i % 2]
             start = i // 2 * part
 
             def move(j, carry):
-                r = pl.multiple_of(start + j * 32, 32)
-                dst[pl.ds(r, 32), :] = src[pl.ds(r, 32), :].astype(BF16)
+                r = pl.multiple_of(start + j * 16, 16)
+                dst[pl.ds(r, 16), :] = src[pl.ds(r, 16), :].astype(BF16)
                 return carry
 
-            lax.fori_loop(0, part // 32, move, 0)
+            lax.fori_loop(0, part // 16, move, 0)
             copy = pltpu.make_async_copy(dst.at[pl.ds(start, part), :], out.at[pl.ds(start, part), :], in_sems.at[i])
             copy.start()
             copies.append(copy)
@@ -309,7 +321,7 @@
                 vm((span, width), F32), vm((span, width), F32), vm((width, QB), F32),
                 vm((3, KB, QB), F32), vm((16 * KB, QB), F32), vm((8, 2 * QB), F32),
                 vm((PAIRS, 2 * QB, 128), BF16), vm((PAIRS, 2 * QB, 128), BF16),
-                vm((2, PAIRS, KB, 2 * QB), BF16), pltpu.SemaphoreType.DMA((2,)), pltpu.SemaphoreType.DMA((6,))]),
+                vm((2, PAIRS, KB, 2 * QB), BF16), pltpu.SemaphoreType.DMA((2,)), pltpu.SemaphoreType.DMA((2 * PARTS,))]),
         out_shape=[shape((rows, width), BF16), shape(k.shape, BF16), shape(k.shape, BF16), shape((16, 160), F32)],
         compiler_params=pltpu.CompilerParams(vmem_limit_bytes=56 * 2**20, dimension_semantics=("arbitrary",)),
         cost_estimate=pl.CostEstimate(flops=40 * 10**9, bytes_accessed=40 * 2**20, transcendentals=0),
@@ -317,19 +329,33 @@
     )(tiles, q, dc, ctx, k, v, kmeta, qmeta, probs)
 
 
+REACH = 560
+
+
 def exchange_plan(n_seq, n_ffn, half):
     seq_bits = [("seq", 1 << b) for b in range(n_seq.bit_length() - 1)]
     ffn_bits = [("ffn", 1 << b) for b in range(1, n_ffn.bit_length() - 1)]
     unit = 16 * n_seq * n_ffn // 2
-    if half % (3 * unit) == 0:
-        orders = [seq_bits + ffn_bits, ffn_bits + seq_bits, ffn_bits[1:] + seq_bits + ffn_bits[:1]]
-        return orders, half // 3
+    if (n_seq, n_ffn) == (2, 16) and half % (6 * unit) == 0:
+        x, y, z, far = seq_bits + ffn_bits
+        orders = [[x, y, z, far], [y, z, far, x], [far, x, y, z], [z, x, y, far], [x, z, far, y], [y, x, z, far]]
+        return orders, half // 6
     return [seq_bits + ffn_bits], half
 
 
-def sum_kernel(orders, length, a_ref, small_ref, out_ref, small_out, work, core_in, slots, sums, small_in,
-               core_sems, core_back, send_sems, recv_sems, back_send, back_recv, small_send, small_recv):
+def sum_kernel(orders, length, n_ffn, dq_ref, context_ref, attn_ref, small_ref, table_ref,
+               window_hbm, dk_hbm, dv_hbm, wq_hbm, wk_hbm, wv_hbm, mid_hbm, out_ref, small_out, hidden_ref,
+               window_ref, dk_ref, dv_ref, wq_ref, wk_ref, wv_ref, mid_ref, load_sems, a_ref, halo_out, halo_in, work, core_in, slots, sums, small_in,
+               halo_send, halo_recv, core_sems, core_back, send_sems, recv_sems, back_send, back_recv, small_send, small_recv):
     seq, ffn = lax.axis_index("seq"), lax.axis_index("ffn")
+    loads = [
+        pltpu.make_async_copy(src, dst, load_sems.at[i])
+        for i, (src, dst) in enumerate((
+            (window_hbm, window_ref), (dk_hbm, dk_ref), (dv_hbm, dv_ref), (wk_hbm, wk_ref), (wv_hbm, wv_ref), (wq_hbm, wq_ref), (mid_hbm, mid_ref),
+        ))
+    ]
+    for load in loads:
+        load.start()
     half = work.shape[0]
     streams = len(orders)
     steps = len(orders[0])
@@ -346,7 +372,36 @@
     barrier = pltpu.get_barrier_semaphore()
     for axis, bit in peers:
         pl.semaphore_signal(barrier, inc=1, device_id=partner(axis, bit), device_id_type=pl.DeviceIdType.MESH)
-    pl.semaphore_wait(barrier, len(peers))
+    has_low, has_high = ffn > 0, ffn < n_ffn - 1
+    pl.semaphore_signal(barrier, inc=1, device_id={"ffn": lax.rem(ffn + 2 * core - 1 + n_ffn, n_ffn)},
+                        device_id_type=pl.DeviceIdType.MESH)
+
+    rows = dq_ref.shape[0]
+    span, width = window_ref.shape
+    pairs = width // 256
+
+    def gradient(place, left, first, right, scale):
+        depth = right.shape[0]
+
+        def block(j, carry):
+            part = tn(left[first : first + depth, pl.ds(pl.multiple_of(j * 128, 128), 128)], right[...])
+            row = lax.rem(j, 2) * half + (place * pairs + j // 2) * 128
+            a_ref[pl.ds(pl.multiple_of(row, 128), 128), :] = (part * scale).astype(BF16)
+            return carry
+
+        lax.fori_loop(0, width // 128, block, 0)
+
+    gradient(0, context_ref, 0, attn_ref, 1.0)
+    for load in loads:
+        load.wait()
+    gradient(1, window_ref, rows, dq_ref, 0.125)
+    sums[0] = small_ref[...]
+    sums[0, 8:24, 0 : table_ref.shape[1]] = table_ref[...]
+    ones = jnp.ones((16, span), BF16)
+    sums[0, 0:1, :] = nn(ones[:, :rows], dq_ref[...])[0:1] * 0.125
+    sums[0, 1:2, :] = nn(ones, dv_ref[...])[0:1]
+
+    pl.semaphore_wait(barrier, len(peers) + 1)
 
     def remote(src, dst, send, recv, axis, bit):
         return pltpu.make_async_remote_copy(src_ref=src, dst_ref=dst, send_sem=send, recv_sem=recv,
@@ -367,17 +422,40 @@
 
     pending = []
     firsts = []
+    ready = 2 * pairs * 128
+    late = [lambda: gradient(2, window_ref, 0, dk_ref, 1.0), lambda: gradient(3, window_ref, 0, dv_ref, 1.0)]
     for s in range(streams):
+        while ready < (s + 1) * length and late:
+            late.pop(0)()
+            ready += pairs * 128
         copy = remote(at(a_ref, (1 - core) * half + s * length, length), at(core_in, s * length, length),
                       core_sems.at[s], core_sems.at[streams + s], "ffn", 1)
         copy.start()
         firsts.append(copy)
-    sums[0] = small_ref[...]
 
     def small_copy(k):
         axis, bit = peers[k]
         return remote(sums.at[k], small_in.at[k], small_send.at[k], small_recv.at[k], axis, bit)
     small_copy(0).start()
+
+    def halo_copy(side):
+        return pltpu.make_async_remote_copy(
+            src_ref=halo_out.at[side], dst_ref=halo_in.at[side], send_sem=halo_send.at[side], recv_sem=halo_recv.at[side],
+            device_id={"ffn": ffn + (2 * side - 1)}, device_id_type=pl.DeviceIdType.MESH)
+
+    for side, first in ((0, rows - REACH), (1, 2 * rows)):
+        def through(j, carry):
+            r = pl.multiple_of(j * 112, 16)
+            near = pl.ds(pl.multiple_of(first + r, 16), 112)
+            part = nt(dk_ref[near, :], wk_ref[...]) + nt(dv_ref[near, :], wv_ref[...])
+            halo_out[side, pl.ds(r, 112), :] = part.astype(BF16)
+            return carry
+
+        lax.fori_loop(0, REACH // 112, through, 0)
+
+        @pl.when((has_low, has_high)[side])
+        def _():
+            halo_copy(side).start()
 
     lows = [s * length for s in range(streams)]
     sizes = [length] * streams
@@ -407,6 +485,17 @@
         firsts[s].wait_recv()
         add(work, s * length, a_ref, core * half + s * length, core_in, s * length, length)
         flying.append(scatter(s, 0))
+
+    def own_rows(j, carry):
+        r = pl.multiple_of(j * 128, 128)
+        here, there = pl.ds(r, 128), pl.ds(pl.multiple_of(rows + r, 128), 128)
+        hidden_ref[here, :] = (
+            mid_ref[here, :] + nt(dq_ref[here, :], wq_ref[...]) * 0.125
+            + nt(dk_ref[there, :], wk_ref[...]) + nt(dv_ref[there, :], wv_ref[...])
+        )
+        return carry
+
+    lax.fori_loop(0, rows // 128, own_rows, 0)
     for k in range(steps):
         for s in range(streams):
             copy, mine, size = flying[s]
@@ -428,6 +517,20 @@
         small_copy(k + 1).start()
     small_copy(steps).wait_recv()
     small_out[...] = sums[steps] + small_in[steps]
+    for side, there in ((1, has_low), (0, has_high)):
+        @pl.when(there)
+        def _():
+            pltpu.make_async_remote_copy(
+                src_ref=halo_out.at[side], dst_ref=halo_in.at[side], send_sem=halo_send.at[side], recv_sem=halo_recv.at[side],
+                device_id={"ffn": ffn - (2 * side - 1)}, device_id_type=pl.DeviceIdType.MESH).wait_recv()
+
+            def merge(j, carry):
+                there = pl.ds(pl.multiple_of(j * 16, 16), 16)
+                r = pl.ds(pl.multiple_of((1 - side) * (rows - REACH) + j * 16, 16), 16)
+                hidden_ref[r, :] = hidden_ref[r, :] + halo_in[side, there, :].astype(F32)
+                return carry
+
+            lax.fori_loop(0, REACH // 16, merge, 0)
     finals = []
     for k in range(steps - 1, -1, -1):
         for s in range(streams):
@@ -450,6 +553,10 @@
         copy.wait_send()
     for k in range(steps + 1):
         small_copy(k).wait_send()
+    for side, there in ((0, has_low), (1, has_high)):
+        @pl.when(there)
+        def _():
+            halo_copy(side).wait_send()
 
 
 def gather(s, k, lows, sizes, orders, remote, at, out_ref, core, half, back_send, back_recv):
@@ -460,32 +567,35 @@
     return copy
 
 
-def sum_everywhere(a, small):
+def sum_everywhere(window, dq, dk, dv, context, attn, wq, wk, wv, mid, small, table):
     n_seq, n_ffn = lax.axis_size("seq"), lax.axis_size("ffn")
     grain = 16 * n_seq * n_ffn // 2
-    rows, width = a.shape
-    half = -(-(rows // 2) // grain) * grain
-    if 2 * half > rows:
-        a = jnp.pad(a, ((0, 2 * half - rows), (0, 0)))
+    rows, width = dq.shape
+    half = -(-(2 * width) // grain) * grain
     orders, length = exchange_plan(n_seq, n_ffn, half)
     streams, steps = len(orders), len(orders[0])
     vm, dma = pltpu.VMEM, pltpu.SemaphoreType.DMA
     slot_rows = streams * (length - length // (1 << steps))
-    out, small_out = pl.pallas_call(
-        functools.partial(sum_kernel, orders, length),
-        out_shape=[jax.ShapeDtypeStruct(a.shape, BF16), jax.ShapeDtypeStruct(small.shape, F32)],
-        in_specs=[pl.BlockSpec(memory_space=vm)] * 2,
-        out_specs=[pl.BlockSpec(memory_space=vm)] * 2,
+    shape = jax.ShapeDtypeStruct
+    held = lambda a: vm(a.shape, a.dtype)
+    return pl.pallas_call(
+        functools.partial(sum_kernel, orders, length, n_ffn),
+        out_shape=[shape((2 * half, width), BF16), shape(small.shape, F32), shape((rows, width), F32)],
+        in_specs=[pl.BlockSpec(memory_space=vm)] * 5 + [pl.BlockSpec(memory_space=pl.ANY)] * 7,
+        out_specs=[pl.BlockSpec(memory_space=vm)] * 3,
         scratch_shapes=[
+            held(window), held(dk), held(dv), held(wq), held(wk), held(wv), held(mid), dma((7,)),
+            vm((2 * half, width), BF16), vm((2, REACH, width), BF16), vm((2, REACH, width), BF16),
             vm((half, width), BF16), vm((half, width), BF16), vm((slot_rows, width), BF16),
             vm((steps + 1,) + small.shape, F32), vm((steps + 1,) + small.shape, F32),
+            dma((2,)), dma((2,)),
             dma((2 * streams,)), dma((2 * streams,)), dma((streams, steps)), dma((streams, steps)),
             dma((streams, steps)), dma((streams, steps)), dma((steps + 1,)), dma((steps + 1,)),
         ],
-        compiler_params=pltpu.CompilerParams(collective_id=0, has_side_effects=True, vmem_limit_bytes=48 * 2**20),
+        compiler_params=pltpu.CompilerParams(collective_id=0, has_side_effects=True, vmem_limit_bytes=58 * 2**20),
+        cost_estimate=pl.CostEstimate(flops=15 * 10**9, bytes_accessed=30 * 2**20, transcendentals=0),
         name="sum_everywhere",
-    )(a, small)
-    return out[:rows], small_out
+    )(dq, context, attn, small, table, window, dk, dv, wq, wk, wv, mid)
 
 
 UB = 512
@@ -565,12 +675,6 @@
         cost_estimate=pl.CostEstimate(flops=4 * rows * units * (wide + width), bytes_accessed=30 * 2**20, transcendentals=0),
         name="ffn_back",
     )(grad, normed, up, down, active, slope)
-
-
-def from_behind(x, axis, by):
-    devices = lax.axis_size(axis)
-    pairs = [(i, i + by) for i in range(devices) if 0 <= i + by < devices]
-    return lax.ppermute(x, axis, pairs)
 
 
 def layer_norm(value, gain, shift):
@@ -683,29 +787,14 @@
     mid1_grad, grad_gain_attn, grad_shift_attn = norm_pull(normed_grad)
     attn_grad = mid1_grad.astype(BF16)
     grad_b_out = jnp.sum(attn_grad.astype(F32), axis=0)
-    grad_w_out = jnp.dot(context_low.T, attn_grad, preferred_element_type=F32)
     scaled = (nt(attn_grad, w_out) * inv).astype(BF16)
     query_grad, key_grad, value_grad, table_sum = attention_bwd(
         tiles, query, scaled, context, key, value, kmeta, qmeta, probs
     )
-    def through(part):
-        return nt(key_grad[part], w_key) + nt(value_grad[part], w_value)
-
-    from_below = from_behind(through(slice(2 * rows, span)).astype(BF16), "ffn", 1)
-    from_above = from_behind(through(slice(0, rows)).astype(BF16), "ffn", -1)
-    big = jnp.concatenate(
-        [
-            (jnp.dot(hidden_in.T, query_grad, preferred_element_type=F32) * 0.125).astype(BF16),
-            jnp.dot(window.T, key_grad, preferred_element_type=F32).astype(BF16),
-            jnp.dot(window.T, value_grad, preferred_element_type=F32).astype(BF16),
-            grad_w_out.astype(BF16),
-        ],
-        axis=0,
-    )
     small = jnp.stack(
         [
-            jnp.sum(query_grad.astype(F32), axis=0) * 0.125,
-            jnp.sum(value_grad.astype(F32), axis=0),
+            jnp.zeros_like(grad_b_out),
+            jnp.zeros_like(grad_b_out),
             grad_b_out,
             grad_gain_attn,
             grad_shift_attn,
@@ -716,22 +805,23 @@
     )
     levels = table_sum.shape[1]
     small = jnp.concatenate(
-        [small, jnp.pad(table_sum, ((0, 0), (0, width - levels))), bias_part[:, 0].reshape(-1, width)], axis=0
-    )
-    big, small = sum_everywhere(big, small)
-    big, small, unit_grad, query_grad, key_grad, value_grad, from_below, from_above = lax.optimization_barrier(
-        (big, small, unit_grad, query_grad, key_grad, value_grad, from_below, from_above)
-    )
+        [small, jnp.zeros((16, width), F32), bias_part[:, 0].reshape(-1, width)], axis=0
+    )
+    big, small, hidden_grad = sum_everywhere(
+        window, query_grad, key_grad, value_grad, context_low, attn_grad, w_query, w_key, w_value, mid1_grad, small, table_sum
+    )
+    big, small, unit_grad = lax.optimization_barrier((big, small, unit_grad))
     for b in range(n_seq.bit_length() - 1):
         unit_grad = unit_grad + lax.ppermute(unit_grad, "seq", [(i, i ^ (1 << b)) for i in range(n_seq)])
     unit_grad = unit_grad.astype(F32)
-    hidden_grad = (
-        mid1_grad + nt(query_grad, w_query) * 0.125 + through(own) + from_below.astype(F32) + from_above.astype(F32)
-    )
     grad_w_up = unit_grad[:, :width].T
     grad_w_down = unit_grad[:, width:]
     grad_b_up = lax.dynamic_slice_in_dim(small[24:].reshape(-1), lax.axis_index("ffn") * units, units)
-    grads = [big[i * width : (i + 1) * width].astype(F32) for i in range(4)]
+    blocks = big.reshape(2, -1, width)[:, : 2 * width].reshape(2, 4, -1, 128, width)
+    g_out, g_query, g_key, g_value = [
+        jnp.stack([blocks[0, m], blocks[1, m]], axis=1).reshape(width, width).astype(F32) for m in range(4)
+    ]
+    grads = [g_query, g_key, g_value, g_out]
     vec = [small[i] for i in range(8)]
     table_all = jnp.stack([small[8 + h // 2 + 8 * (h % 2), :levels] for h in range(heads)], axis=1)
     return (

time: 393 us -> 375 us (0.954); the launches traced: 386 us -> 373 us
  Pallas kernels: 203 us -> 242 us
  matrix products: 44.4 us -> 22.3 us
  starting transfers between devices: 24.2 us -> 5.42 us
  other arithmetic: 38.5 us -> 21.3 us
  local copies, waits for them, and re-layouts: 23.9 us -> 31.4 us
    pallas_call x1, Pallas kernels: 87.1 us -> 107 us  [sum_everywhere(): pl.pallas_call(functools.partial(sum_kernel, orders, length, n_ffn), out_...]
    ppermute x2 -> x0, starting transfers between devices: 18.5 us -> none  [from_behind(): return lax.ppermute(x, axis, pairs)]
    dot_general x8 -> x1, matrix products: 14.8 us -> 3.67 us  [nt(): lax.dot_general(a, b, (((1,), (1,)), ((), ())), preferred_element_type=F32)]
    pallas_call x1, Pallas kernels: 48.1 us -> 57.6 us  [attention_bwd(): pl.pallas_call(bwd_kernel, grid_spec=pltpu.PrefetchScalarGridSpec(num_sca...]
    dot_general x4 -> x0, matrix products: 9.42 us -> none  [the longest x1 2.78 us: on_device(): jnp.dot(hidden_in.T, query_grad, preferred_element_type=F32) * 0.125]
    pallas_call x1, Pallas kernels: 32.7 us -> 41.7 us  [attention_fwd(): pl.pallas_call(fwd_kernel, grid_spec=pltpu.PrefetchScalarGridSpec(num_sca...]
    convert_element_type x0 -> x4, local copies, waits for them, and re-layouts: none -> 6.23 us  [on_device(): jnp.stack([blocks[0, m], blocks[1, m]], axis=1).reshape(width, width)]
    ppermute x1, waiting for transfers between devices: 0.01 us -> 5.65 us  [on_device(): lax.ppermute(unit_grad, 'seq', [(i, i ^ 1 << b) for i in range(n_seq)])]
  transfers between devices with their start and end apart: 8 -> 6, of which waited for: 1 -> 2; matrix products, arithmetic and copies ran while one was open for 20% -> 13% of each run, Pallas kernels for 47% -> 59%
where the time goes in v3:
time: 375 us; the launch traced here: 373 us
  Pallas kernels  242 us (65%)
  waiting for transfers between devices  36.6 us (10%)
  local copies, waits for them, and re-layouts  31.4 us (8%)
  matrix products  22.3 us (6%)
  other arithmetic  21.3 us (6%)
  between operations  14.4 us (4%)
  starting transfers between devices  5.42 us (1%)
    pallas_call x1, Pallas kernels, sum_everywhere(): pl.pallas_call(functools.partial(sum_kernel, orders, length, n_ffn), out_...  107 us
    pallas_call x1, Pallas kernels, attention_bwd(): pl.pallas_call(bwd_kernel, grid_spec=pltpu.PrefetchScalarGridSpec(num_sca...  57.6 us
    pallas_call x1, Pallas kernels, attention_fwd(): pl.pallas_call(fwd_kernel, grid_spec=pltpu.PrefetchScalarGridSpec(num_sca...  41.7 us
    all_gather x1, waiting for transfers between devices, on_device(): down_all = lax.all_gather(later, 'ffn', axis=0, tiled=True)  30.2 us
    pallas_call x1, Pallas kernels, ffn_back(): pl.pallas_call(ffn_back_kernel, grid=(units // UB,), in_specs=[full(rows,...  21.4 us
    pallas_call x1, Pallas kernels, ffn_up(): pl.pallas_call(ffn_up_kernel, grid=(units // UB,), in_specs=[full(rows, w...  13.9 us
    unnamed x54, local copies, waits for them, and re-layouts  10.7 us
  transfers between devices with their start and end apart: 6, of which 2 were waited for; matrix products, arithmetic and copies ran while one was open for 13% of the time, Pallas kernels for 59%

profile of v3, /device:TPU:0, one launch (start us, length us, event | category | flops | bytes accessed | tf_op | source)
XLA Modules:
  0.0 373.4 jit_solution(10223213341178491533)
XLA Ops:
  7.3 0.8 copy.93
  8.1 0.7 broadcast_in_dim.140
  8.9 1.8 maximum_maximum_fusion.1
  10.7 0.7 all-gather.5.cloned.1.call-update
  11.5 3.5 collective-permute-start
  14.9 1.3 collective-permute-start.1
  16.2 0.7 copy.78
  17.5 0.8 fusion.14
  18.5 0.8 maximum_bitcast_fusion
  19.4 0.7 convert_element_type.112
  20.1 0.7 convert_element_type.108
  21.8 0.7 convert_element_type.100
  22.5 0.7 convert_element_type.103
  23.2 0.4 copy.81
  23.8 1.1 pad.10.kmeta_ref
  24.9 0.6 pad.11.qmeta_ref
  25.6 0.7 pad_add_fusion.tiles
  26.3 0.6 pad_maximum_fusion.tab_ref
  26.9 1.9 multiply_convert_fusion.1.q_ref
  28.8 1.3 constant_dynamic-update-slice_fusion.2
  30.1 1.4 constant_dynamic-update-slice_fusion.window_hbm
  31.6 4.1 %convolution_convert_fusion.k_hbm = bf16[1920,768]{1,0:T(8,128)(2,1)} fusion(bf16[1920,768]{1,0:T(8,128)(2,1)S(1)} %constant_dynamic-update-slice_fusion.window_hbm, bf16[768,768]{1,0:T(8,128)(2,1)S(1)} %copy-done.23), kind=kOutput, calls=%fused_computation.1 | convolution fusion | flops 2266398720 | bytes 7077888 | tf_op jit(solution)/shard_map/dot_general | solution.py:763
  35.8 4.1 %add_convert_fusion.v_hbm = bf16[1920,768]{1,0:T(8,128)(2,1)} fusion(bf16[1920,768]{1,0:T(8,128)(2,1)S(1)} %constant_dynamic-update-slice_fusion.window_hbm, bf16[768,768]{1,0:T(8,128)(2,1)S(1)} %copy-done.24, f32[768]{0:T(1024)S(1)} %convert_element_type.103), kind=kOutput, calls=%fused_computation | convolution fusion | flops 2267873280 | bytes 7080960 | tf_op jit(solution)/shard_map/dot_general | solution.py:764
  39.9 41.7 %attention_forward.1 = (f32[640,768]{1,0:T(8,128)}, f32[640,768]{1,0:T(8,128)}, bf16[5,12,6,128,256]{4,3,2,1,0:T(8,128)(2,1)}) custom-call(s32[5,25]{1,0:T(8,128)} %pad_add_fusion.tiles, bf16[640,768]{1,0:T(8,128)(2,1)} %multiply_convert_fusion.1.q_ref, bf16[1920,768]{1,0:T(8,128)(2,1)} %convolution_convert_fusion.k_hbm, ...), custom_call_target="tpu_custom_call" | custom-call | flops 24999999488 | bytes 31457280 | tf_op jit(solution)/shard_map/attention_forward/pallas_call | solution.py:178
  81.6 1.6 convert_element_type.107.context_ref
  83.2 1.0 fusion.30
  84.3 0.4 multiply_reduce_fusion.3
  84.7 0.4 fusion.4
  85.1 0.5 copy-done.7
  85.9 13.9 %ffn_up.1 = (bf16[640,3072]{1,0:T(8,128)(2,1)S(1)}, bf16[640,3072]{1,0:T(8,128)(2,1)}) custom-call(bf16[640,896]{1,0:T(8,128)(2,1)S(1)} %maximum_maximum_fusion.normed_ref, bf16[3072,896]{1,0:T(8,128)(2,1)} %all-gather.3.cloned.1.call-done.up_ref), custom_call_target="tpu_custom_call" | custom-call | flops 3523215360 | bytes 15728640 | tf_op jit(solution)/shard_map/ffn_up/pallas_call | solution.py:634
  99.8 1.9 copy-done.6
  101.7 30.2 %all-gather.5.cloned.1.call-done.down_ref = bf16[3072,768]{1,0:T(8,128)(2,1)} async-done(((bf16[192,768]{1,0:T(8,128)(2,1)}), bf16[3072,768]{1,0:T(8,128)(2,1)}) %all-gather.5.cloned.1.call-update) | async-done | bytes 4718608 | tf_op jit(solution)/shard_map/all_gather | solution.py:738
  131.9 7.5 %fusion.31 = (f32[640]{0:T(1024)S(1)}, f32[640,768]{1,0:T(8,128)S(1)}) fusion(f32[768]{0:T(1024)S(1)} %convert_element_type.112, bf16[640,3072]{1,0:T(8,128)(2,1)} %copy-done.6, bf16[3072,768]{1,0:T(8,128)(2,1)} %all-gather.5.cloned.1.call-done.down_ref, f32[768]{0:T(1024)S(1)} %convert_element_type.110, f32[768]{0:T(1024)S(1)} %convert_element_type.109, ...), kind=kOutput, calls=%fused_computation.135 | convolution fusion | flops 3023339008 | bytes 12599808 | tf_op jit(solution)/shard_map/dot_general | solution.py:777
  139.4 0.4 multiply_reduce_fusion.2
  139.8 0.8 copy-done.11
  140.6 0.9 fusion.3
  141.4 2.1 fusion.24
  143.8 1.0 copy-done.9
  144.8 0.7 copy-done.5
  145.5 21.4 %ffn_back.1 = (bf16[3072,1536]{1,0:T(8,128)(2,1)}, f32[3072,128]{1,0:T(8,128)S(1)}, f32[640,768]{1,0:T(8,128)S(1)}) custom-call(bf16[640,768]{1,0:T(8,128)(2,1)S(1)} %get-tuple-element.93.grad_ref, bf16[640,896]{1,0:T(8,128)(2,1)S(1)} %copy-done.5, bf16[3072,896]{1,0:T(8,128)(2,1)} %all-gather.3.cloned.1.call-done.up_ref, ...), custom_call_target="tpu_custom_call" | custom-call | flops 13086228480 | bytes 31457280 | tf_op jit(solution)/shard_map/ffn_back/pallas_call | solution.py:668
  166.9 1.1 copy-done.2
  168.1 3.2 multiply_reduce_fusion
  171.3 0.7 fusion.23
  172.0 1.5 convert_reduce_fusion.2
  173.6 0.3 copy-done.3
  174.0 0.5 slice_reduce_fusion
  174.5 1.9 concatenate.49.small_ref
  176.4 3.7 multiply_convert_fusion.dc_ref
  180.0 57.6 %attention_backward.1 = (bf16[640,768]{1,0:T(8,128)(2,1)}, bf16[1920,768]{1,0:T(8,128)(2,1)}, bf16[1920,768]{1,0:T(8,128)(2,1)}, f32[16,160]{1,0:T(8,128)}) custom-call(s32[5,25]{1,0:T(8,128)} %pad_add_fusion.tiles, bf16[640,768]{1,0:T(8,128)(2,1)} %multiply_convert_fusion.1.q_ref, bf16[640,768]{1,0:T(8,128)(2,1)} %multiply_convert_fusion.dc_ref, ...), custom_call_target="tpu_custom_call" | custom-call | flops 40000000000 | bytes 41943040 | tf_op jit(solution)/shard_map/attention_backward/pallas_call | solution.py:313
  237.7 107.3 %sum_everywhere.1 = (bf16[3072,768]{1,0:T(8,128)(2,1)}, f32[28,768]{1,0:T(8,128)}, f32[640,768]{1,0:T(8,128)}) custom-call(bf16[640,768]{1,0:T(8,128)(2,1)} %get-tuple-element.60.dq_ref, bf16[640,768]{1,0:T(8,128)(2,1)} %copy-done.14, bf16[640,768]{1,0:T(8,128)(2,1)} %copy-done.10, f32[28,768]{1,0:T(8,128)} %concatenate.49.small_ref, ...), custom_call_target="tpu_custom_call" | custom-call | flops 15000000512 | bytes 31457280 | tf_op jit(solution)/shard_map/sum_everywhere/pallas_call | solution.py:581
  345.1 2.8 slice_bitcast_fusion.2
  347.9 0.6 collective-permute-start.2
  349.1 1.6 copy.83
  350.7 1.6 copy.84
  352.2 1.6 copy.85
  353.8 1.6 copy.86
  355.5 0.6 slice.207
  356.1 0.6 dynamic_slice.15
  356.7 0.7 slice_reduce_fusion.1
  357.4 0.7 fusion.29
  358.0 5.7 %collective-permute-done.2 = bf16[192,1536]{1,0:T(8,128)(2,1)S(1)} collective-permute-done((bf16[192,1536]{1,0:T(8,128)(2,1)S(1)}, bf16[192,1536]{1,0:T(8,128)(2,1)S(1)}, u32[]{:S(2)}, u32[]{:S(2)}) %collective-permute-start.2) | collective-permute-done | bytes 589856 | tf_op jit(solution)/shard_map/ppermute | solution.py:815
  363.8 1.1 fusion.28
  364.9 1.3 copy.94
  366.1 0.7 copy-done.1
  (122 shorter events, 3.9 us)
Async XLA Ops:
  7.2 76.0 %copy-start = (bf16[768,768]{1,0:T(8,128)(2,1)S(1)}, bf16[768,768]{1,0:T(8,128)(2,1)}, u32[]{:S(2)}) copy-start(bf16[768,768]{1,0:T(8,128)(2,1)} %param.36) | copy-start | bytes 3538948
  7.2 16.5 %copy-start.19 = (bf16[768]{0:T(1024)(128)(2,1)S(1)}, bf16[768]{0:T(1024)(128)(2,1)}, u32[]{:S(2)}) copy-start(bf16[768]{0:T(1024)(128)(2,1)} %param.38) | copy-start | bytes 4612
  7.2 16.4 %copy-start.18 = (bf16[768]{0:T(1024)(128)(2,1)S(1)}, bf16[768]{0:T(1024)(128)(2,1)}, u32[]{:S(2)}) copy-start(bf16[768]{0:T(1024)(128)(2,1)} %param.39) | copy-start | bytes 4612
  7.2 16.5 %copy-start.20 = (bf16[768]{0:T(1024)(128)(2,1)S(1)}, bf16[768]{0:T(1024)(128)(2,1)}, u32[]{:S(2)}) copy-start(bf16[768]{0:T(1024)(128)(2,1)} %param.44) | copy-start | bytes 4612
  7.2 16.5 %copy-start.21 = (bf16[768]{0:T(1024)(128)(2,1)S(1)}, bf16[768]{0:T(1024)(128)(2,1)}, u32[]{:S(2)}) copy-start(bf16[768]{0:T(1024)(128)(2,1)} %param.45) | copy-start | bytes 4612
  7.2 78.6 %all-gather.3.cloned.1.call-start = ((), (), s32[]{:S(2)}) async-start(), calls=%async_computation.1 | async-start | bytes 5849088 | tf_op jit(solution)/shard_map/all_gather | solution.py:737
  10.7 121.2 %all-gather.5.cloned.1.call-start = ((), (), s32[]{:S(2)}) async-start(), calls=%async_computation.2 | async-start | bytes 5013504 | tf_op jit(solution)/shard_map/all_gather | solution.py:738
  11.4 15.5 %copy-start.13 = (bf16[640,768]{1,0:T(8,128)(2,1)S(1)}, bf16[640,768]{1,0:T(8,128)(2,1)}, u32[]{:S(2)}) copy-start(bf16[640,768]{1,0:T(8,128)(2,1)} %param.26) | copy-start | bytes 2949124
  11.4 333.6 %reduce-scatter.2.cloned.1.call-start = ((), (), s32[]{:S(2)}) async-start(), calls=%async_computation.3 | async-start | bytes 10027008 | tf_op jit(solution)/shard_map/reduce_scatter | solution.py:785
  11.5 17.3 %collective-permute-start = (bf16[640,768]{1,0:T(8,128)(2,1)}, bf16[640,768]{1,0:T(8,128)(2,1)}, u32[]{:S(2)}, u32[]{:S(2)}) collective-permute-start(bf16[640,768]{1,0:T(8,128)(2,1)} %param.26), channel_id=1, source_target_pairs={{0,1},{1,2},{2,3},{3,4},{4,5},{5,6},{6,7},{7,8},{8,9},{9,10},{10,1... | collective-permute-start | bytes 2949128 | tf_op jit(solution)/shard_map/ppermute | solution.py:731
  14.9 15.2 %collective-permute-start.1 = (bf16[640,768]{1,0:T(8,128)(2,1)}, bf16[640,768]{1,0:T(8,128)(2,1)}, u32[]{:S(2)}, u32[]{:S(2)}) collective-permute-start(bf16[640,768]{1,0:T(8,128)(2,1)} %param.26), channel_id=1, source_target_pairs={{1,0},{2,1},{3,2},{4,3},{5,4},{6,5},{7,6},{8,7},{9,8},{10,9},{11,1... | collective-permute-start | bytes 2949128 | tf_op jit(solution)/shard_map/ppermute | solution.py:732
  23.6 3.3 copy-start.22
  30.0 1.6 copy-start.23
  31.6 4.1 %copy-start.16 = (bf16[1920,768]{1,0:T(8,128)(2,1)}, bf16[1920,768]{1,0:T(8,128)(2,1)S(1)}, u32[]{:S(2)}) copy-start(bf16[1920,768]{1,0:T(8,128)(2,1)S(1)} %constant_dynamic-update-slice_fusion.window_hbm) | copy-start | bytes 8847364
  31.6 4.1 %copy-start.24 = (bf16[768,768]{1,0:T(8,128)(2,1)S(1)}, bf16[768,768]{1,0:T(8,128)(2,1)}, u32[]{:S(2)}) copy-start(bf16[768,768]{1,0:T(8,128)(2,1)} %wv_hbm.1) | copy-start | bytes 3538948
  83.2 1.1 copy-start.14
  84.3 1.3 copy-start.7
  85.8 13.9 %copy-start.4 = (bf16[640,896]{1,0:T(8,128)(2,1)}, bf16[640,896]{1,0:T(8,128)(2,1)S(1)}, u32[]{:S(2)}) copy-start(bf16[640,896]{1,0:T(8,128)(2,1)S(1)} %maximum_maximum_fusion.normed_ref) | copy-start | bytes 3440644
  99.8 1.9 copy-start.6
  139.4 1.2 copy-start.11
  143.6 1.3 copy-start.9
  143.6 2.0 copy-start.5
  166.9 1.1 copy-start.2
  168.1 3.2 copy-start.8
  172.0 1.9 copy-start.3
  173.6 6.5 %copy-start.10 = (bf16[640,768]{1,0:T(8,128)(2,1)}, bf16[640,768]{1,0:T(8,128)(2,1)S(1)}, u32[]{:S(2)}) copy-start(bf16[640,768]{1,0:T(8,128)(2,1)S(1)} %get-tuple-element.95.attn_ref) | copy-start | bytes 2949124
  345.1 2.8 copy-start.15
  347.9 15.8 %collective-permute-start.2 = (bf16[192,1536]{1,0:T(8,128)(2,1)S(1)}, bf16[192,1536]{1,0:T(8,128)(2,1)S(1)}, u32[]{:S(2)}, u32[]{:S(2)}) collective-permute-start(bf16[192,1536]{1,0:T(8,128)(2,1)S(1)} %copy-done.15), channel_id=1, source_target_pairs={{0,16},{16,0},{1,17},{17,1},{2,18},{18,2},{3,19},{19,3},{4,20},{20... | collective-permute-start | bytes 1769480 | tf_op jit(solution)/shard_map/ppermute | solution.py:815
  353.8 1.6 copy-start.17
  358.0 6.8 %copy-start.12 = (f32[640,768]{1,0:T(8,128)S(1)}, f32[640,768]{1,0:T(8,128)}, u32[]{:S(2)}) copy-start(f32[640,768]{1,0:T(8,128)} %get-tuple-element.159) | copy-start | bytes 5898244
  364.9 2.0 copy-start.1
Sparse Core Ops, SparseCore 0:
  10.9 66.5 all-gather.2
  79.9 51.9 all-gather.4
  168.2 120.2 reduce-scatter.1

commit v4 on v3

--- a/solution.py
+++ b/solution.py
@@ -598,7 +598,7 @@
     )(dq, context, attn, small, table, window, dk, dv, wq, wk, wv, mid)
 
 
-UB = 512
+UB = 768
 
 
 def gelu_and_slope(x):

time: 375 us -> 375 us (level)
  waiting for transfers between devices: 36.6 us -> 41.7 us
  Pallas kernels: 242 us -> 238 us
    pallas_call x1, Pallas kernels: 107 us -> 116 us  [sum_everywhere(): pl.pallas_call(functools.partial(sum_kernel, orders, length, n_ffn), out_...]
    pallas_call x1, Pallas kernels: 57.6 us -> 51.1 us  [attention_bwd(): pl.pallas_call(bwd_kernel, grid_spec=pltpu.PrefetchScalarGridSpec(num_sca...]
    all_gather x1, waiting for transfers between devices: 30.2 us -> 34.8 us  [on_device(): down_all = lax.all_gather(later, 'ffn', axis=0, tiled=True)]
    pallas_call x1, Pallas kernels: 41.7 us -> 37.3 us  [attention_fwd(): pl.pallas_call(fwd_kernel, grid_spec=pltpu.PrefetchScalarGridSpec(num_sca...]
  transfers between devices with their start and end apart: 6 -> 6, of which waited for: 2 -> 2; matrix products, arithmetic and copies ran while one was open for 13% -> 13% of each run, Pallas kernels for 59% -> 58%
where the time goes in v4:
time: 375 us; the launch traced here: 374 us
  Pallas kernels  238 us (63%)
  waiting for transfers between devices  41.7 us (11%)
  local copies, waits for them, and re-layouts  31.4 us (8%)
  matrix products  22.3 us (6%)
  other arithmetic  21.3 us (6%)
  between operations  14.4 us (4%)
  starting transfers between devices  4.92 us (1%)
    pallas_call x1, Pallas kernels, sum_everywhere(): pl.pallas_call(functools.partial(sum_kernel, orders, length, n_ffn), out_...  116 us
    pallas_call x1, Pallas kernels, attention_bwd(): pl.pallas_call(bwd_kernel, grid_spec=pltpu.PrefetchScalarGridSpec(num_sca...  51.1 us
    pallas_call x1, Pallas kernels, attention_fwd(): pl.pallas_call(fwd_kernel, grid_spec=pltpu.PrefetchScalarGridSpec(num_sca...  37.3 us
    all_gather x1, waiting for transfers between devices, on_device(): down_all = lax.all_gather(later, 'ffn', axis=0, tiled=True)  34.8 us
    pallas_call x1, Pallas kernels, ffn_back(): pl.pallas_call(ffn_back_kernel, grid=(units // UB,), in_specs=[full(rows,...  20.3 us
    pallas_call x1, Pallas kernels, ffn_up(): pl.pallas_call(ffn_up_kernel, grid=(units // UB,), in_specs=[full(rows, w...  13.7 us
    unnamed x54, local copies, waits for them, and re-layouts  10.7 us
  transfers between devices with their start and end apart: 6, of which 2 were waited for; matrix products, arithmetic and copies ran while one was open for 13% of the time, Pallas kernels for 58%

profile of v4, /device:TPU:0, one launch (start us, length us, event | category | flops | bytes accessed | tf_op | source)
XLA Modules:
  0.0 374.1 jit_solution(2418413457043454180)
XLA Ops:
  7.3 0.8 copy.93
  8.1 0.7 broadcast_in_dim.140
  8.9 1.8 maximum_maximum_fusion.1
  10.7 0.7 all-gather.5.cloned.1.call-update
  11.5 3.5 collective-permute-start
  14.9 1.3 collective-permute-start.1
  16.2 0.7 copy.78
  17.5 0.8 fusion.14
  18.5 0.8 maximum_bitcast_fusion
  19.4 0.7 convert_element_type.112
  20.1 0.7 convert_element_type.108
  21.0 0.3 select_reduce_fusion.3
  21.8 0.7 convert_element_type.100
  22.5 0.7 convert_element_type.103
  23.2 0.4 copy.81
  23.8 1.1 pad.10.kmeta_ref
  24.9 0.6 pad.11.qmeta_ref
  25.6 0.7 pad_add_fusion.tiles
  26.3 0.6 pad_maximum_fusion.tab_ref
  26.9 1.9 multiply_convert_fusion.1.q_ref
  28.8 1.3 constant_dynamic-update-slice_fusion.2
  30.1 1.4 constant_dynamic-update-slice_fusion.window_hbm
  31.6 4.1 %convolution_convert_fusion.k_hbm = bf16[1920,768]{1,0:T(8,128)(2,1)} fusion(bf16[1920,768]{1,0:T(8,128)(2,1)S(1)} %constant_dynamic-update-slice_fusion.window_hbm, bf16[768,768]{1,0:T(8,128)(2,1)S(1)} %copy-done.23), kind=kOutput, calls=%fused_computation.1 | convolution fusion | flops 2266398720 | bytes 7077888 | tf_op jit(solution)/shard_map/dot_general | solution.py:763
  35.8 4.1 %add_convert_fusion.v_hbm = bf16[1920,768]{1,0:T(8,128)(2,1)} fusion(bf16[1920,768]{1,0:T(8,128)(2,1)S(1)} %constant_dynamic-update-slice_fusion.window_hbm, bf16[768,768]{1,0:T(8,128)(2,1)S(1)} %copy-done.24, f32[768]{0:T(1024)S(1)} %convert_element_type.103), kind=kOutput, calls=%fused_computation | convolution fusion | flops 2267873280 | bytes 7080960 | tf_op jit(solution)/shard_map/dot_general | solution.py:764
  39.9 37.3 %attention_forward.1 = (f32[640,768]{1,0:T(8,128)}, f32[640,768]{1,0:T(8,128)}, bf16[5,12,6,128,256]{4,3,2,1,0:T(8,128)(2,1)}) custom-call(s32[5,25]{1,0:T(8,128)} %pad_add_fusion.tiles, bf16[640,768]{1,0:T(8,128)(2,1)} %multiply_convert_fusion.1.q_ref, bf16[1920,768]{1,0:T(8,128)(2,1)} %convolution_convert_fusion.k_hbm, ...), custom_call_target="tpu_custom_call" | custom-call | flops 24999999488 | bytes 31457280 | tf_op jit(solution)/shard_map/attention_forward/pallas_call | solution.py:178
  77.2 1.6 convert_element_type.107.context_ref
  78.9 1.0 fusion.30
  79.9 0.4 multiply_reduce_fusion.3
  80.3 0.4 fusion.4
  80.7 0.5 copy-done.7
  81.5 13.7 %ffn_up.1 = (bf16[640,3072]{1,0:T(8,128)(2,1)S(1)}, bf16[640,3072]{1,0:T(8,128)(2,1)}) custom-call(bf16[640,896]{1,0:T(8,128)(2,1)S(1)} %maximum_maximum_fusion.normed_ref, bf16[3072,896]{1,0:T(8,128)(2,1)} %all-gather.3.cloned.1.call-done.up_ref), custom_call_target="tpu_custom_call" | custom-call | flops 3523215360 | bytes 15728640 | tf_op jit(solution)/shard_map/ffn_up/pallas_call | solution.py:634
  95.2 1.9 copy-done.6
  97.1 34.8 %all-gather.5.cloned.1.call-done.down_ref = bf16[3072,768]{1,0:T(8,128)(2,1)} async-done(((bf16[192,768]{1,0:T(8,128)(2,1)}), bf16[3072,768]{1,0:T(8,128)(2,1)}) %all-gather.5.cloned.1.call-update) | async-done | bytes 4718608 | tf_op jit(solution)/shard_map/all_gather | solution.py:738
  131.9 7.5 %fusion.31 = (f32[640]{0:T(1024)S(1)}, f32[640,768]{1,0:T(8,128)S(1)}) fusion(f32[768]{0:T(1024)S(1)} %convert_element_type.112, bf16[640,3072]{1,0:T(8,128)(2,1)} %copy-done.6, bf16[3072,768]{1,0:T(8,128)(2,1)} %all-gather.5.cloned.1.call-done.down_ref, f32[768]{0:T(1024)S(1)} %convert_element_type.110, f32[768]{0:T(1024)S(1)} %convert_element_type.109, ...), kind=kOutput, calls=%fused_computation.135 | convolution fusion | flops 3023339008 | bytes 12599808 | tf_op jit(solution)/shard_map/dot_general | solution.py:777
  139.4 0.4 multiply_reduce_fusion.2
  139.8 0.8 copy-done.11
  140.6 0.9 fusion.3
  141.4 2.1 fusion.24
  143.8 1.0 copy-done.9
  144.8 0.7 copy-done.5
  145.5 20.3 %ffn_back.1 = (bf16[3072,1536]{1,0:T(8,128)(2,1)}, f32[3072,128]{1,0:T(8,128)S(1)}, f32[640,768]{1,0:T(8,128)S(1)}) custom-call(bf16[640,768]{1,0:T(8,128)(2,1)S(1)} %get-tuple-element.93.grad_ref, bf16[640,896]{1,0:T(8,128)(2,1)S(1)} %copy-done.5, bf16[3072,896]{1,0:T(8,128)(2,1)} %all-gather.3.cloned.1.call-done.up_ref, ...), custom_call_target="tpu_custom_call" | custom-call | flops 13086228480 | bytes 31457280 | tf_op jit(solution)/shard_map/ffn_back/pallas_call | solution.py:668
  165.9 1.1 copy-done.2
  167.1 3.2 multiply_reduce_fusion
  170.3 0.7 fusion.23
  171.0 1.5 convert_reduce_fusion.2
  172.6 0.3 copy-done.3
  172.9 0.5 slice_reduce_fusion
  173.5 1.9 concatenate.49.small_ref
  175.4 3.7 multiply_convert_fusion.dc_ref
  179.0 51.1 %attention_backward.1 = (bf16[640,768]{1,0:T(8,128)(2,1)}, bf16[1920,768]{1,0:T(8,128)(2,1)}, bf16[1920,768]{1,0:T(8,128)(2,1)}, f32[16,160]{1,0:T(8,128)}) custom-call(s32[5,25]{1,0:T(8,128)} %pad_add_fusion.tiles, bf16[640,768]{1,0:T(8,128)(2,1)} %multiply_convert_fusion.1.q_ref, bf16[640,768]{1,0:T(8,128)(2,1)} %multiply_convert_fusion.dc_ref, ...), custom_call_target="tpu_custom_call" | custom-call | flops 40000000000 | bytes 41943040 | tf_op jit(solution)/shard_map/attention_backward/pallas_call | solution.py:313
  230.1 115.7 %sum_everywhere.1 = (bf16[3072,768]{1,0:T(8,128)(2,1)}, f32[28,768]{1,0:T(8,128)}, f32[640,768]{1,0:T(8,128)}) custom-call(bf16[640,768]{1,0:T(8,128)(2,1)} %get-tuple-element.60.dq_ref, bf16[640,768]{1,0:T(8,128)(2,1)} %copy-done.14, bf16[640,768]{1,0:T(8,128)(2,1)} %copy-done.10, f32[28,768]{1,0:T(8,128)} %concatenate.49.small_ref, ...), custom_call_target="tpu_custom_call" | custom-call | flops 15000000512 | bytes 31457280 | tf_op jit(solution)/shard_map/sum_everywhere/pallas_call | solution.py:581
  345.8 2.8 slice_bitcast_fusion.2
  349.4 1.6 copy.83
  351.0 1.6 copy.84
  352.5 1.6 copy.85
  354.1 1.6 copy.86
  355.7 0.6 slice.207
  356.3 0.6 dynamic_slice.15
  357.0 0.7 slice_reduce_fusion.1
  357.6 0.7 fusion.29
  358.3 6.1 %collective-permute-done.2 = bf16[192,1536]{1,0:T(8,128)(2,1)S(1)} collective-permute-done((bf16[192,1536]{1,0:T(8,128)(2,1)S(1)}, bf16[192,1536]{1,0:T(8,128)(2,1)S(1)}, u32[]{:S(2)}, u32[]{:S(2)}) %collective-permute-start.2) | collective-permute-done | bytes 589856 | tf_op jit(solution)/shard_map/ppermute | solution.py:815
  364.5 1.1 fusion.28
  365.6 1.3 copy.94
  366.9 0.7 copy-done.1
  (122 shorter events, 3.7 us)
Async XLA Ops:
  7.2 71.7 %copy-start = (bf16[768,768]{1,0:T(8,128)(2,1)S(1)}, bf16[768,768]{1,0:T(8,128)(2,1)}, u32[]{:S(2)}) copy-start(bf16[768,768]{1,0:T(8,128)(2,1)} %param.36) | copy-start | bytes 3538948
  7.2 16.5 %copy-start.19 = (bf16[768]{0:T(1024)(128)(2,1)S(1)}, bf16[768]{0:T(1024)(128)(2,1)}, u32[]{:S(2)}) copy-start(bf16[768]{0:T(1024)(128)(2,1)} %param.38) | copy-start | bytes 4612
  7.2 16.4 %copy-start.18 = (bf16[768]{0:T(1024)(128)(2,1)S(1)}, bf16[768]{0:T(1024)(128)(2,1)}, u32[]{:S(2)}) copy-start(bf16[768]{0:T(1024)(128)(2,1)} %param.39) | copy-start | bytes 4612
  7.2 16.5 %copy-start.20 = (bf16[768]{0:T(1024)(128)(2,1)S(1)}, bf16[768]{0:T(1024)(128)(2,1)}, u32[]{:S(2)}) copy-start(bf16[768]{0:T(1024)(128)(2,1)} %param.44) | copy-start | bytes 4612
  7.2 16.5 %copy-start.21 = (bf16[768]{0:T(1024)(128)(2,1)S(1)}, bf16[768]{0:T(1024)(128)(2,1)}, u32[]{:S(2)}) copy-start(bf16[768]{0:T(1024)(128)(2,1)} %param.45) | copy-start | bytes 4612
  7.2 74.2 %all-gather.3.cloned.1.call-start = ((), (), s32[]{:S(2)}) async-start(), calls=%async_computation.1 | async-start | bytes 5849088 | tf_op jit(solution)/shard_map/all_gather | solution.py:737
  10.7 121.2 %all-gather.5.cloned.1.call-start = ((), (), s32[]{:S(2)}) async-start(), calls=%async_computation.2 | async-start | bytes 5013504 | tf_op jit(solution)/shard_map/all_gather | solution.py:738
  11.4 15.5 %copy-start.13 = (bf16[640,768]{1,0:T(8,128)(2,1)S(1)}, bf16[640,768]{1,0:T(8,128)(2,1)}, u32[]{:S(2)}) copy-start(bf16[640,768]{1,0:T(8,128)(2,1)} %param.26) | copy-start | bytes 2949124
  11.4 334.4 %reduce-scatter.2.cloned.1.call-start = ((), (), s32[]{:S(2)}) async-start(), calls=%async_computation.3 | async-start | bytes 10027008 | tf_op jit(solution)/shard_map/reduce_scatter | solution.py:785
  11.5 17.3 %collective-permute-start = (bf16[640,768]{1,0:T(8,128)(2,1)}, bf16[640,768]{1,0:T(8,128)(2,1)}, u32[]{:S(2)}, u32[]{:S(2)}) collective-permute-start(bf16[640,768]{1,0:T(8,128)(2,1)} %param.26), channel_id=1, source_target_pairs={{0,1},{1,2},{2,3},{3,4},{4,5},{5,6},{6,7},{7,8},{8,9},{9,10},{10,1... | collective-permute-start | bytes 2949128 | tf_op jit(solution)/shard_map/ppermute | solution.py:731
  14.9 15.2 %collective-permute-start.1 = (bf16[640,768]{1,0:T(8,128)(2,1)}, bf16[640,768]{1,0:T(8,128)(2,1)}, u32[]{:S(2)}, u32[]{:S(2)}) collective-permute-start(bf16[640,768]{1,0:T(8,128)(2,1)} %param.26), channel_id=1, source_target_pairs={{1,0},{2,1},{3,2},{4,3},{5,4},{6,5},{7,6},{8,7},{9,8},{10,9},{11,1... | collective-permute-start | bytes 2949128 | tf_op jit(solution)/shard_map/ppermute | solution.py:732
  23.6 3.3 copy-start.22
  30.0 1.6 copy-start.23
  31.6 4.1 %copy-start.16 = (bf16[1920,768]{1,0:T(8,128)(2,1)}, bf16[1920,768]{1,0:T(8,128)(2,1)S(1)}, u32[]{:S(2)}) copy-start(bf16[1920,768]{1,0:T(8,128)(2,1)S(1)} %constant_dynamic-update-slice_fusion.window_hbm) | copy-start | bytes 8847364
  31.6 4.1 %copy-start.24 = (bf16[768,768]{1,0:T(8,128)(2,1)S(1)}, bf16[768,768]{1,0:T(8,128)(2,1)}, u32[]{:S(2)}) copy-start(bf16[768,768]{1,0:T(8,128)(2,1)} %wv_hbm.1) | copy-start | bytes 3538948
  78.9 1.1 copy-start.14
  79.9 1.3 copy-start.7
  81.5 13.7 %copy-start.4 = (bf16[640,896]{1,0:T(8,128)(2,1)}, bf16[640,896]{1,0:T(8,128)(2,1)S(1)}, u32[]{:S(2)}) copy-start(bf16[640,896]{1,0:T(8,128)(2,1)S(1)} %maximum_maximum_fusion.normed_ref) | copy-start | bytes 3440644
  95.2 1.9 copy-start.6
  139.4 1.2 copy-start.11
  143.6 1.3 copy-start.9
  143.6 2.0 copy-start.5
  165.9 1.1 copy-start.2
  167.1 3.2 copy-start.8
  171.0 1.9 copy-start.3
  172.6 6.5 %copy-start.10 = (bf16[640,768]{1,0:T(8,128)(2,1)}, bf16[640,768]{1,0:T(8,128)(2,1)S(1)}, u32[]{:S(2)}) copy-start(bf16[640,768]{1,0:T(8,128)(2,1)S(1)} %get-tuple-element.95.attn_ref) | copy-start | bytes 2949124
  345.8 2.8 copy-start.15
  348.7 15.8 %collective-permute-start.2 = (bf16[192,1536]{1,0:T(8,128)(2,1)S(1)}, bf16[192,1536]{1,0:T(8,128)(2,1)S(1)}, u32[]{:S(2)}, u32[]{:S(2)}) collective-permute-start(bf16[192,1536]{1,0:T(8,128)(2,1)S(1)} %copy-done.15), channel_id=1, source_target_pairs={{0,16},{16,0},{1,17},{17,1},{2,18},{18,2},{3,19},{19,3},{4,20},{20... | collective-permute-start | bytes 1769480 | tf_op jit(solution)/shard_map/ppermute | solution.py:815
  354.1 1.6 copy-start.17
  358.3 7.3 %copy-start.12 = (f32[640,768]{1,0:T(8,128)S(1)}, f32[640,768]{1,0:T(8,128)}, u32[]{:S(2)}) copy-start(f32[640,768]{1,0:T(8,128)} %get-tuple-element.159) | copy-start | bytes 5898244
  365.6 2.0 copy-start.1
Sparse Core Ops, SparseCore 0:
  10.9 66.5 all-gather.2
  79.9 51.9 all-gather.4
  167.2 117.3 reduce-scatter.1
